TPU v7x, 32 devices: a whole 2x2x4 slice. The times are simulated.
32 devices in a mesh: win: 8 (over y, x, core), head: 4 (over z).
Axes of the slice: x: 2, y: 2, z: 4, core: 2. Of those that a mesh axis runs over, the one named last changes fastest.
Arguments:
- tokens: bfloat16 [65536, 384], P(('win', 'head')), may hold values from -6 to 6
- out_grad: bfloat16 [65536, 384], P(('win', 'head')), may hold values from -6 to 6
- clip_frames: int32 [256], P('win'), may hold values from 4 to 16, as said below
- qkv_weight: float32 [384, 3, 384], P(None, None, 'head'), may hold values from -0.3125 to 0.3125
- qv_bias: float32 [2, 384], P(None, 'head'), may hold values from -3 to 3
- rel_table: float32 [225, 16], P(None, 'head'), may hold values from -6 to 6
- proj_weight: float32 [384, 384], P('head'), may hold values from -1.25 to 1.25
- fc1_weight: float32 [384, 1536], P(None, 'head'), may hold values from -0.3125 to 0.3125
- fc1_bias: float32 [1536], P('head'), may hold values from -1.75 to 1.75
- fc2_weight: float32 [1536, 384], P('head'), may hold values from -0.15625 to 0.15625
- row_params: float32 [6, 384], replicated, as said below
- qkv_first: float32 [384, 3, 384], P(None, None, 'head'), may hold values from -0.00048828125 to 0.00048828125
- qkv_second: float32 [384, 3, 384], P(None, None, 'head'), may hold values from 5.6253097e-10 to 3.3751857e-09
- qvb_first: float32 [2, 384], P(None, 'head'), may hold values from -0.0014648438 to 0.0014648438
- qvb_second: float32 [2, 384], P(None, 'head'), may hold values from 5.0627786e-09 to 3.0376672e-08
- table_first: float32 [225, 16], P(None, 'head'), may hold values from -0.00036621094 to 0.00036621094
- table_second: float32 [225, 16], P(None, 'head'), may hold values from 1.4063274e-10 to 5.6253097e-10
- proj_first: float32 [384, 384], P('head'), may hold values from -0.00048828125 to 0.00048828125
- proj_second: float32 [384, 384], P('head'), may hold values from 5.6253097e-10 to 3.3751857e-09
- fc1_first: float32 [384, 1536], P(None, 'head'), may hold values from -0.00048828125 to 0.00048828125
- fc1_second: float32 [384, 1536], P(None, 'head'), may hold values from 5.6253097e-10 to 3.3751857e-09
- fc1b_first: float32 [1536], P('head'), may hold values from -0.00018310547 to 0.00018310547
- fc1b_second: float32 [1536], P('head'), may hold values from 2.8126546e-11 to 1.12506185e-10
- fc2_first: float32 [1536, 384], P('head'), may hold values from -0.00048828125 to 0.00048828125
- fc2_second: float32 [1536, 384], P('head'), may hold values from 5.6253097e-10 to 3.3751857e-09
- rows_first: float32 [6, 384], replicated, may hold values from -0.0014648438 to 0.0014648438
- rows_second: float32 [6, 384], replicated, may hold values from 5.0627786e-09 to 3.0376672e-08
Outputs:
- output: float32 [65536, 384], P(('win', 'head'))
- input_grad: float32 [65536, 384], P(('win', 'head'))
- grad_norm: float32 [], replicated
- qkv_grad: float32 [384, 3, 384], P(None, None, 'head')
- qkv_moment: float32 [384, 3, 384], P(None, None, 'head')
- qkv_square: float32 [384, 3, 384], P(None, None, 'head')
- qkv_master: float32 [384, 3, 384], P(None, None, 'head')
- qvb_grad: float32 [2, 384], P(None, 'head')
- qvb_moment: float32 [2, 384], P(None, 'head')
- qvb_square: float32 [2, 384], P(None, 'head')
- qvb_master: float32 [2, 384], P(None, 'head')
- table_grad: float32 [225, 16], P(None, 'head')
- table_moment: float32 [225, 16], P(None, 'head')
- table_square: float32 [225, 16], P(None, 'head')
- table_master: float32 [225, 16], P(None, 'head')
- proj_grad: float32 [384, 384], P('head')
- proj_moment: float32 [384, 384], P('head')
- proj_square: float32 [384, 384], P('head')
- proj_master: float32 [384, 384], P('head')
- fc1_grad: float32 [384, 1536], P(None, 'head')
- fc1_moment: float32 [384, 1536], P(None, 'head')
- fc1_square: float32 [384, 1536], P(None, 'head')
- fc1_master: float32 [384, 1536], P(None, 'head')
- fc1b_grad: float32 [1536], P('head')
- fc1b_moment: float32 [1536], P('head')
- fc1b_square: float32 [1536], P('head')
- fc1b_master: float32 [1536], P('head')
- fc2_grad: float32 [1536, 384], P('head')
- fc2_moment: float32 [1536, 384], P('head')
- fc2_square: float32 [1536, 384], P('head')
- fc2_master: float32 [1536, 384], P('head')
- rows_grad: float32 [6, 384], replicated
- rows_moment: float32 [6, 384], replicated
- rows_square: float32 [6, 384], replicated
- rows_master: float32 [6, 384], replicated
Inputs may be any that keep to these rules, and one draw needn't show every extreme that they name: Patches of a clip are valid in its first clip_frames time rows; some clip of every draw has all 16. `row_params`: rows in order: first norm's gain, its shift, second norm's gain, its shift, attention output bias, feed-forward output bias.
All inputs are finite; a program needn't handle non-finite values.
Results may differ from a plain program's by a relative error of at most 0.015.
Values may be sent and summed in bfloat16 or wider, within the bound.
A program may use at most 256 MiB of HBM per device.

v0:
```python
from functools import partial

import jax
import jax.numpy as jnp
from jax import lax
from jax.sharding import PartitionSpec as P

D = 384
HDIM = 24
GRID = 16
WIN = 8
SHIFT = 4
STEP = 10


NORM_EPS = 1e-05
MASKED = -1000000000.0
CLIP_LIMIT = 1.0
LEARN_RATE = 0.1
ROW_RATE = 0.5
BETA_ONE = 0.9
BETA_TWO = 0.999
ADAM_EPS = 1e-08
WEIGHT_DECAY = 0.01
HIGHEST_MODE = lax.Precision.HIGHEST


def layer_norm(values, gain, shift):
    center = values - jnp.mean(values, axis=-1, keepdims=True)
    spread = jnp.mean(center * center, axis=-1, keepdims=True)
    return center * lax.rsqrt(spread + NORM_EPS) * gain + shift


def split_grid(grid_values):
    leading = grid_values.shape[:-2]
    rank_lead = len(leading)
    shaped = grid_values.reshape(leading + (GRID // WIN, WIN, GRID // WIN, WIN))
    axes_order = tuple(range(rank_lead)) + (rank_lead, rank_lead + 2, rank_lead + 1, rank_lead + 3)
    return shaped.transpose(axes_order).reshape(leading + ((GRID // WIN) ** 2, WIN * WIN))


def window_masks(frames):
    places = jnp.arange(GRID, dtype=jnp.int32)
    region = jnp.where(places < GRID - WIN, 0, jnp.where(places < GRID - SHIFT, 1, 2)).astype(
        jnp.int32
    )
    region_grid = split_grid(region[:, None] * 3 + region[None, :])
    anchor = (places + SHIFT) % GRID
    valid_rows = anchor[None, :] < frames[:, None]
    valid_grid = split_grid(jnp.broadcast_to(valid_rows[:, :, None], (frames.shape[0], GRID, GRID)))
    same_region = region_grid[:, :, None] == region_grid[:, None, :]
    allowed = same_region[None] & valid_grid[:, :, None, :]
    return allowed.reshape(-1, WIN * WIN, WIN * WIN)


def position_index():
    places = jnp.arange(WIN * WIN, dtype=jnp.int32)
    row_at = places // WIN
    col_at = places % WIN
    return (
        (row_at[:, None] - row_at[None, :] + WIN - 1) * (2 * WIN - 1)
        + col_at[:, None]
        - col_at[None, :]
        + WIN
        - 1
    )


def to_windows(values):
    columns = values.shape[-1]
    number = values.shape[0] // (GRID * GRID)
    shaped = jnp.roll(values.reshape(number, GRID, GRID, columns), (-SHIFT, -SHIFT), axis=(1, 2))
    shaped = shaped.reshape(number, GRID // WIN, WIN, GRID // WIN, WIN, columns).transpose(
        0, 1, 3, 2, 4, 5
    )
    return shaped.reshape(number * GRID * GRID, columns)


def from_windows(values):
    columns = values.shape[-1]
    number = values.shape[0] // (GRID * GRID)
    shaped = values.reshape(number, GRID // WIN, GRID // WIN, WIN, WIN, columns).transpose(
        0, 1, 3, 2, 4, 5
    )
    shaped = jnp.roll(shaped.reshape(number, GRID, GRID, columns), (SHIFT, SHIFT), axis=(1, 2))
    return shaped.reshape(number * GRID * GRID, columns)


def sum_squares(arrays):
    running = jnp.zeros((), jnp.float32)
    for member in arrays:
        running = running + jnp.sum(member * member)
    return running


def adam_step(weight, gradient, moment, second, factor, rate):
    clipped = gradient * factor
    moment_new = BETA_ONE * moment + (1.0 - BETA_ONE) * clipped
    second_new = BETA_TWO * second + (1.0 - BETA_TWO) * clipped * clipped
    moment_hat = moment_new / (1.0 - BETA_ONE**STEP)
    second_hat = second_new / (1.0 - BETA_TWO**STEP)
    master = weight - rate * (
        moment_hat / (jnp.sqrt(second_hat) + ADAM_EPS) + WEIGHT_DECAY * weight
    )
    return (gradient, moment_new, second_new, master)


def attend_forward(windowed, qkv_low, bias_pair, table, frames):
    local_heads = table.shape[1]
    local_width = local_heads * HDIM
    joined_rows = jnp.dot(windowed, qkv_low, preferred_element_type=jnp.float32)
    window_count = joined_rows.shape[0] // (WIN * WIN)
    shape_four = (window_count, WIN * WIN, local_heads, HDIM)
    query_heads = (
        (joined_rows[:, :local_width] + bias_pair[0]).astype(jnp.bfloat16).reshape(shape_four)
    )
    keys_heads = (
        joined_rows[:, local_width : 2 * local_width].astype(jnp.bfloat16).reshape(shape_four)
    )
    values_heads = (
        (joined_rows[:, 2 * local_width :] + bias_pair[1]).astype(jnp.bfloat16).reshape(shape_four)
    )
    allowed = window_masks(frames)[:, None]
    table_rows = jnp.arange(table.shape[0], dtype=jnp.int32)
    onehot = (position_index().reshape(-1)[:, None] == table_rows[None, :]).astype(jnp.float32)
    position_bias = jnp.dot(onehot, table, precision=HIGHEST_MODE)
    position_bias = position_bias.reshape(WIN * WIN, WIN * WIN, local_heads).transpose(2, 0, 1)
    raw_scores = jnp.einsum(
        "wqhd,wkhd->whqk", query_heads, keys_heads, preferred_element_type=jnp.float32
    )
    scores = jnp.where(allowed, raw_scores * HDIM ** (-0.5) + position_bias, MASKED)
    row_peak = jnp.max(scores, axis=-1, keepdims=True)
    row_exp = jnp.exp(scores - row_peak)
    row_total = jnp.sum(row_exp, axis=-1, keepdims=True)
    probs_low = (row_exp / row_total).astype(jnp.bfloat16)
    mixed_heads = jnp.einsum(
        "whqk,wkhd->wqhd", probs_low, values_heads, preferred_element_type=jnp.float32
    )
    kept = (
        query_heads,
        keys_heads,
        values_heads,
        allowed,
        onehot,
        position_bias,
        row_peak,
        row_total,
    )
    return (mixed_heads.astype(jnp.bfloat16).reshape(-1, local_width), kept)


def attend_backward(d_attended_rows, kept):
    query_heads, keys_heads, values_heads, allowed, onehot, position_bias, row_peak, row_total = (
        kept
    )
    local_heads = query_heads.shape[2]
    local_width = local_heads * HDIM
    score_scale = HDIM ** (-0.5)
    d_attended = d_attended_rows.reshape(query_heads.shape)
    raw_scores = jnp.einsum(
        "wqhd,wkhd->whqk", query_heads, keys_heads, preferred_element_type=jnp.float32
    )
    scores = jnp.where(allowed, raw_scores * score_scale + position_bias, MASKED)
    probs = jnp.exp(scores - row_peak) / row_total
    d_probs = jnp.einsum(
        "wqhd,wkhd->whqk", d_attended, values_heads, preferred_element_type=jnp.float32
    )
    d_values = (
        jnp.einsum(
            "whqk,wqhd->wkhd",
            probs.astype(jnp.bfloat16),
            d_attended,
            preferred_element_type=jnp.float32,
        )
        .astype(jnp.bfloat16)
        .reshape(-1, local_width)
    )
    row_inner = jnp.sum(probs * d_probs, axis=-1, keepdims=True)
    d_scores = jnp.where(
        allowed, (probs * (d_probs - row_inner)).astype(jnp.bfloat16), jnp.zeros((), jnp.bfloat16)
    )
    table_terms = (
        jnp.sum(d_scores, axis=0, dtype=jnp.float32).transpose(1, 2, 0).reshape(-1, local_heads)
    )
    table_gradient = jnp.dot(onehot.T, table_terms, precision=HIGHEST_MODE)
    d_query = (
        (
            jnp.einsum("whqk,wkhd->wqhd", d_scores, keys_heads, preferred_element_type=jnp.float32)
            * score_scale
        )
        .astype(jnp.bfloat16)
        .reshape(-1, local_width)
    )
    d_keys = (
        (
            jnp.einsum("whqk,wqhd->wkhd", d_scores, query_heads, preferred_element_type=jnp.float32)
            * score_scale
        )
        .astype(jnp.bfloat16)
        .reshape(-1, local_width)
    )
    d_joined = jnp.concatenate([d_query, d_keys, d_values], axis=1)
    qvb_gradient = jnp.stack(
        [jnp.sum(d_query, axis=0, dtype=jnp.float32), jnp.sum(d_values, axis=0, dtype=jnp.float32)]
    )
    return (d_joined, qvb_gradient, table_gradient)


def shards(
    tokens,
    out_grad,
    clip_frames,
    qkv_weight,
    qv_bias,
    rel_table,
    proj_weight,
    fc1_weight,
    fc1_bias,
    fc2_weight,
    row_params,
    qkv_first,
    qkv_second,
    qvb_first,
    qvb_second,
    table_first,
    table_second,
    proj_first,
    proj_second,
    fc1_first,
    fc1_second,
    fc1b_first,
    fc1b_second,
    fc2_first,
    fc2_second,
    rows_first,
    rows_second,
):
    row_count = tokens.shape[0]
    inputs = tokens.astype(jnp.float32)
    cotangent = out_grad.astype(jnp.float32)
    normed_one, pull_one = jax.vjp(layer_norm, inputs, row_params[0], row_params[1])
    local_width = rel_table.shape[1] * HDIM
    gathered_one = lax.all_gather(normed_one.astype(jnp.bfloat16), "head", axis=0, tiled=True)
    windowed_one = to_windows(gathered_one)
    qkv_low = qkv_weight.astype(jnp.bfloat16).reshape(D, 3 * local_width)
    mixed_rows, kept = attend_forward(windowed_one, qkv_low, qv_bias, rel_table, clip_frames)
    attended = from_windows(mixed_rows)
    proj_low = proj_weight.astype(jnp.bfloat16)
    block_rows = attended
    branch = (
        lax.psum_scatter(
            jnp.dot(block_rows, proj_low, preferred_element_type=jnp.float32),
            "head",
            scatter_dimension=0,
            tiled=True,
        )
        + row_params[4]
    )
    middle = inputs + branch
    normed_two, pull_two = jax.vjp(layer_norm, middle, row_params[2], row_params[3])
    gathered_two = lax.all_gather(normed_two.astype(jnp.bfloat16), "head", axis=0, tiled=True)
    fc1_low = fc1_weight.astype(jnp.bfloat16)
    upper_rows = jnp.dot(gathered_two, fc1_low, preferred_element_type=jnp.float32) + fc1_bias
    hidden, pull_gelu = jax.vjp(partial(jax.nn.gelu, approximate=False), upper_rows)
    hidden_low = hidden.astype(jnp.bfloat16)
    fc2_low = fc2_weight.astype(jnp.bfloat16)
    block_rows = lax.slice_in_dim(hidden_low, 0, lax.axis_size("head") * row_count, axis=0)
    output = (
        middle
        + lax.psum_scatter(
            jnp.dot(block_rows, fc2_low, preferred_element_type=jnp.float32).astype(jnp.bfloat16),
            "head",
            scatter_dimension=0,
            tiled=True,
        ).astype(jnp.float32)
        + row_params[5]
    )
    gathered_cot = lax.all_gather(out_grad, "head", axis=0, tiled=True)
    fc2_gradient = jnp.dot(hidden_low.T, gathered_cot, preferred_element_type=jnp.float32)
    d_hidden = jnp.dot(gathered_cot, fc2_low.T, preferred_element_type=jnp.float32)
    d_upper = pull_gelu(d_hidden)[0].astype(jnp.bfloat16)
    fc1_gradient = jnp.dot(gathered_two.T, d_upper, preferred_element_type=jnp.float32)
    fc1b_gradient = jnp.sum(d_upper, axis=0, dtype=jnp.float32)
    block_rows = d_upper
    d_normed_two = lax.psum_scatter(
        jnp.dot(block_rows, fc1_low.T, preferred_element_type=jnp.float32).astype(jnp.bfloat16),
        "head",
        scatter_dimension=0,
        tiled=True,
    ).astype(jnp.float32)
    d_middle_part, gain_two, shift_two = pull_two(d_normed_two)
    d_middle = cotangent + d_middle_part
    d_branch = d_middle.astype(jnp.bfloat16)
    gathered_branch = lax.all_gather(d_branch, "head", axis=0, tiled=True)
    proj_gradient = jnp.dot(attended.T, gathered_branch, preferred_element_type=jnp.float32)
    d_attended = jnp.dot(gathered_branch, proj_low.T, preferred_element_type=jnp.float32).astype(
        jnp.bfloat16
    )
    d_joined, qvb_gradient, table_gradient = attend_backward(to_windows(d_attended), kept)
    qkv_gradient = jnp.dot(windowed_one.T, d_joined, preferred_element_type=jnp.float32).reshape(
        D, 3, local_width
    )
    d_joined_rows = from_windows(d_joined)
    block_rows = d_joined_rows
    d_normed_one = lax.psum_scatter(
        jnp.dot(block_rows, qkv_low.T, preferred_element_type=jnp.float32).astype(jnp.bfloat16),
        "head",
        scatter_dimension=0,
        tiled=True,
    ).astype(jnp.float32)
    d_input_part, gain_one, shift_one = pull_one(d_normed_one)
    input_grad = d_middle + d_input_part
    row_terms = jnp.stack(
        [
            gain_one,
            shift_one,
            gain_two,
            shift_two,
            jnp.sum(d_branch, axis=0, dtype=jnp.float32),
            jnp.sum(cotangent, axis=0),
        ]
    )
    rows_gradient = lax.psum(row_terms, ("win", "head"))
    qkv_summed, qvb_summed, table_summed, proj_summed, fc1_summed, fc1b_summed, fc2_summed = (
        lax.psum(
            (
                qkv_gradient,
                qvb_gradient,
                table_gradient,
                proj_gradient,
                fc1_gradient,
                fc1b_gradient,
                fc2_gradient,
            ),
            "win",
        )
    )
    total_square = lax.psum(
        sum_squares(
            (qkv_summed, qvb_summed, table_summed, proj_summed, fc1_summed, fc1b_summed, fc2_summed)
        ),
        "head",
    )
    grad_norm = jnp.sqrt(total_square + sum_squares((rows_gradient,)))
    factor = jnp.minimum(1.0, CLIP_LIMIT / (grad_norm + 1e-06))
    weights = (
        qkv_weight,
        qv_bias,
        rel_table,
        proj_weight,
        fc1_weight,
        fc1_bias,
        fc2_weight,
        row_params,
    )
    gradients = (
        qkv_summed,
        qvb_summed,
        table_summed,
        proj_summed,
        fc1_summed,
        fc1b_summed,
        fc2_summed,
        rows_gradient,
    )
    firsts = (
        qkv_first,
        qvb_first,
        table_first,
        proj_first,
        fc1_first,
        fc1b_first,
        fc2_first,
        rows_first,
    )
    seconds = (
        qkv_second,
        qvb_second,
        table_second,
        proj_second,
        fc1_second,
        fc1b_second,
        fc2_second,
        rows_second,
    )
    rates = (
        LEARN_RATE,
        LEARN_RATE,
        ROW_RATE,
        LEARN_RATE,
        LEARN_RATE,
        LEARN_RATE,
        LEARN_RATE,
        ROW_RATE,
    )
    updated = []
    for weight, gradient, moment, second, rate in zip(weights, gradients, firsts, seconds, rates):
        updated.extend(adam_step(weight, gradient, moment, second, factor, rate))
    return (
        output,
        input_grad,
        grad_norm,
        updated[0],
        updated[1],
        updated[2],
        updated[3],
        updated[4],
        updated[5],
        updated[6],
        updated[7],
        updated[8],
        updated[9],
        updated[10],
        updated[11],
        updated[12],
        updated[13],
        updated[14],
        updated[15],
        updated[16],
        updated[17],
        updated[18],
        updated[19],
        updated[20],
        updated[21],
        updated[22],
        updated[23],
        updated[24],
        updated[25],
        updated[26],
        updated[27],
        updated[28],
        updated[29],
        updated[30],
        updated[31],
    )


def solution(mesh):
    return jax.shard_map(
        shards,
        mesh=mesh,
        in_specs=(
            P(("win", "head"), None),
            P(("win", "head"), None),
            P("win"),
            P(None, None, "head"),
            P(None, "head"),
            P(None, "head"),
            P("head", None),
            P(None, "head"),
            P("head"),
            P("head", None),
            P(),
            P(None, None, "head"),
            P(None, None, "head"),
            P(None, "head"),
            P(None, "head"),
            P(None, "head"),
            P(None, "head"),
            P("head", None),
            P("head", None),
            P(None, "head"),
            P(None, "head"),
            P("head"),
            P("head"),
            P("head", None),
            P("head", None),
            P(),
            P(),
        ),
        out_specs=(
            P(("win", "head"), None),
            P(("win", "head"), None),
            P(),
            P(None, None, "head"),
            P(None, None, "head"),
            P(None, None, "head"),
            P(None, None, "head"),
            P(None, "head"),
            P(None, "head"),
            P(None, "head"),
            P(None, "head"),
            P(None, "head"),
            P(None, "head"),
            P(None, "head"),
            P(None, "head"),
            P("head", None),
            P("head", None),
            P("head", None),
            P("head", None),
            P(None, "head"),
            P(None, "head"),
            P(None, "head"),
            P(None, "head"),
            P("head"),
            P("head"),
            P("head"),
            P("head"),
            P("head", None),
            P("head", None),
            P("head", None),
            P("head", None),
            P(),
            P(),
            P(),
            P(),
        ),
        check_vma=False,
    )
```

profile of v0, /device:TPU:0, one launch (start us, length us, event | category | flops | bytes accessed | tf_op | source)
XLA Modules:
  0.0 1526.6 jit_solution(17874301605531064085)
XLA Ops:
  14.1 2.8 fusion.37
  23.0 112.1 %all-gather.5.cloned.1.call-done = bf16[8192,384]{1,0:T(8,128)(2,1)} async-done(((bf16[2048,384]{1,0:T(8,128)(2,1)}), bf16[8192,384]{1,0:T(8,128)(2,1)}) %all-gather.5.cloned.1.call-update) | async-done | bytes 6291472 | tf_op jit(solution)/shard_map/all_gather | solution.py:243
  136.7 2.8 slice.125
  145.2 2.7 fusion.126
  149.8 4.4 reshape.389
  154.2 4.3 reshape.390
  158.5 4.3 reshape.388
  162.8 19.6 %fusion.121 = (f32[128,4,64]{2,1,0:T(4,128)S(1)}, f32[128,4,64,64]{2,3,1,0:T(8,128)}) fusion(f32[4,64,64]{1,2,0:T(8,128)S(1)} %bitcast.112, pred[128,64,64]{1,2,0:T(8,128)(4,1)} %bitcast_and_fusion, bf16[128,64,4,24]{1,0,3,2:T(8,128)(2,1)} %reshape.390, bf16[128,64,4,24]{1,0,3,2:T(8,128)(2,1)} %reshape.389), kind=kOutput, calls=%fused_computation.212 | convolution fusion | flops 111149120 | bytes 12255232 | tf_op jit(solution)/shard_map/sub | solution.py:133
  182.5 11.8 convert_bitcast_fusion.1
  194.2 11.2 copy.131
  205.4 20.8 %reshape_reshape.6 = bf16[32,2,2,8,8,96]{5,4,3,2,1,0:T(8,128)(2,1)S(1)} reshape(bf16[128,64,4,24]{3,2,1,0:T(4,128)(2,1)} %copy.131) | data formatting | bytes 3145728 | tf_op jit(solution)/shard_map/reshape;reshape | solution.py:82
  229.5 6.3 fusion.92
  235.9 210.2 %reduce-scatter.5.cloned.1.call-done = f32[2048,384]{1,0:T(8,128)} async-done(((f32[8192,384]{1,0:T(8,128)}), f32[2048,384]{1,0:T(8,128)}) %reduce-scatter.5.cloned.1.call-update) | async-done | bytes 3145744 | tf_op jit(solution)/shard_map/reduce_scatter | solution.py:251
  446.0 2.8 fusion.120
  451.9 115.9 %all-gather.7.cloned.1.call-done = bf16[8192,384]{1,0:T(8,128)(2,1)} async-done(((bf16[2048,384]{1,0:T(8,128)(2,1)}), bf16[8192,384]{1,0:T(8,128)(2,1)}) %all-gather.7.cloned.1.call-update) | async-done | bytes 6291472 | tf_op jit(solution)/shard_map/all_gather | solution.py:261
  567.8 34.0 %multiply_convert_fusion.1 = (bf16[8192,384]{1,0:T(8,128)(2,1)}, f32[8192,384]{1,0:T(8,128)}, f32[8192,384]{1,0:T(8,128)}) fusion(f32[384]{0:T(512)S(1)} %copy-done.57, bf16[8192,384]{1,0:T(8,128)(2,1)} %all-gather.7.cloned.1.call-done, f32[384,384]{1,0:T(8,128)} %param.34), kind=kOutput, calls=%fused_computation.12 | convolution fusion | flops 2623684608 | bytes 38340096 | tf_op jit(solution)/shard_map/dot_general | solution.py:263
  601.8 81.1 %all-gather.9.cloned.1.call-done = bf16[8192,384]{1,0:T(8,128)(2,1)} async-done(((bf16[2048,384]{1,0:T(8,128)(2,1)}), bf16[8192,384]{1,0:T(8,128)(2,1)}) %all-gather.9.cloned.1.call-update) | async-done | bytes 6291472 | tf_op jit(solution)/shard_map/all_gather | solution.py:278
  682.9 16.6 %convert_reduce_fusion.1 = (f32[384]{0:T(512)}, bf16[8192,384]{1,0:T(8,128)(2,1)S(1)}) fusion(f32[8192,384]{1,0:T(8,128)} %get-tuple-element.84, bf16[8192,384]{1,0:T(8,128)(2,1)} %all-gather.9.cloned.1.call-done, f32[384,384]{1,0:T(8,128)} %param.36, f32[8192,384]{1,0:T(8,128)} %get-tuple-element.96, f32[384]{0:T(512)S(1)} %copy-done.57), kind=kOutput, calls=%fused_computation.10 | convolution fusion | flops 2469543424 | bytes 38341632 | tf_op jit(solution)/shard_map/dot_general | solution.py:280
  702.1 7.0 convolution_convert_fusion.1
  709.6 9.5 convolution_convert_fusion.2
  719.2 99.1 %reduce-scatter.9.cloned.1.call-done = bf16[2048,384]{1,0:T(8,128)(2,1)} async-done(((bf16[8192,384]{1,0:T(8,128)(2,1)}), bf16[2048,384]{1,0:T(8,128)(2,1)}) %reduce-scatter.9.cloned.1.call-update) | async-done | bytes 1572880 | tf_op jit(solution)/shard_map/reduce_scatter | solution.py:285
  818.3 3.0 fusion.41
  821.3 110.4 %reduce-scatter.7.cloned.1.call-done = bf16[2048,384]{1,0:T(8,128)(2,1)} async-done(((bf16[8192,384]{1,0:T(8,128)(2,1)}), bf16[2048,384]{1,0:T(8,128)(2,1)}) %reduce-scatter.7.cloned.1.call-update) | async-done | bytes 1572880 | tf_op jit(solution)/shard_map/reduce_scatter | solution.py:270
  931.7 4.1 fusion.118
  939.9 8.9 fusion.130
  948.8 9.6 fusion.129
  958.4 97.5 %all-gather.11.cloned.1.call-done = bf16[8192,384]{1,0:T(8,128)(2,1)} async-done(((bf16[2048,384]{1,0:T(8,128)(2,1)}), bf16[8192,384]{1,0:T(8,128)(2,1)}) %all-gather.11.cloned.1.call-update) | async-done | bytes 6291472 | tf_op jit(solution)/shard_map/all_gather | solution.py:294
  1055.9 6.0 convolution_convert_fusion.3
  1061.9 3.3 copy.133
  1067.6 6.1 reshape_reshape.7
  1073.7 11.6 copy.135
  1085.4 13.0 convert_reduce_fusion.2
  1098.4 3.1 copy.149
  1101.5 11.2 copy.145
  1112.7 12.0 fusion.47
  1124.7 29.8 %convert_reduce_fusion = (f32[4,64,64]{1,2,0:T(8,128)S(1)}, bf16[128,4,64,64]{2,3,1,0:T(8,128)(2,1)}) fusion(pred[128,64,64]{1,2,0:T(8,128)(4,1)} %bitcast_and_fusion, f32[128,4,64,64]{2,3,1,0:T(8,128)} %fusion.47, f32[128,4,64,64]{2,3,1,0:T(8,128)} %get-tuple-element.95, f32[128,4,64]{2,1,0:T(4,128)} %copy-done.61), kind=kOutput, calls=%fused_computation.3 | output fusion | flops 18890816 | bytes 21692416 | tf_op jit(solution)/shard_map/sub | solution.py:180
  1154.5 10.7 fusion.44
  1165.2 11.1 convert_reduce_fusion.3
  1176.3 2.9 copy.148
  1179.2 11.3 copy.142
  1190.4 4.8 copy.147
  1195.2 11.2 copy.139
  1206.5 10.7 concatenate.52
  1217.2 10.5 concatenate.51
  1227.7 10.6 concatenate.50
  1238.3 5.9 maximum_bitcast_fusion
  1246.5 2.7 slice.139
  1249.2 3.4 reshape.400
  1252.6 5.3 reshape.398
  1257.9 3.4 reshape.399
  1261.4 2.7 pad_maximum_fusion.3
  1264.1 7.0 fusion.127
  1271.1 5.3 fusion.16
  1278.5 9.3 convolution_convert_fusion
  1290.4 14.3 all-reduce
  1306.5 30.7 %all-reduce.4.cloned.1.call-done = (f32[384,3,96]{0,2,1:T(8,128)}, f32[96,384]{1,0:T(8,128)}, f32[384,384]{1,0:T(8,128)}, f32[384,384]{1,0:T(8,128)}) async-done(((f32[384,3,96]{0,2,1:T(8,128)}, f32[96,384]{1,0:T(8,128)}, f32[384,384]{1,0:T(8,128)}, f32[384,384]{1,0:T(8,128)}), (f32[384,3,96]{0,2,1:T(8,128)}, f32[96,384]{1,0:T(8,128)}, f32[384,384]{1,0:T(8,128)}, ...) | async-done | bytes 1769488 | tf_op jit(solution)/shard_map/psum | solution.py:325
  1348.7 12.7 psum.70
  1361.5 88.5 %reduce-scatter.11.cloned.1.call-done = bf16[2048,384]{1,0:T(8,128)(2,1)} async-done(((bf16[8192,384]{1,0:T(8,128)(2,1)}), bf16[2048,384]{1,0:T(8,128)(2,1)}) %reduce-scatter.11.cloned.1.call-update) | async-done | bytes 1572880 | tf_op jit(solution)/shard_map/reduce_scatter | solution.py:305
  1450.0 2.8 convert_reduce_fusion.4
  1452.8 2.8 fusion.42
  1455.9 3.2 convert_reduce_fusion.7
  1459.2 41.2 %psum.71 = f32[6,384]{1,0:T(8,128)S(1)} all-reduce(f32[6,384]{1,0:T(8,128)S(1)} %stack.27), channel_id=1, replica_groups=mesh['win'=8,'head'=4] {'win','head'}, use_global_device_ids=true, to_apply=%region_40.41 | all-reduce | flops 2304 | bytes 18432 | tf_op jit(solution)/shard_map/psum | solution.py:323
  1508.1 2.7 multiply_subtract_fusion.2
  1510.9 3.1 multiply_subtract_fusion.1
  (234 shorter events, 64.3 us)
Async XLA Ops:
  7.2 10.1 copy-start.50
  7.2 12.5 copy-start.60
  7.2 13.0 copy-start.21
  7.2 15.7 %copy-start.54 = (f32[2,96]{1,0:T(2,128)S(1)}, f32[2,96]{1,0:T(2,128)}, u32[]{:S(2)}) copy-start(f32[2,96]{1,0:T(2,128)} %param.31) | copy-start | bytes 2308
  7.3 127.9 %all-gather.5.cloned.1.call-start = ((), (), s32[]{:S(2)}) async-start(), calls=%async_computation.4 | async-start | bytes 7864320 | tf_op jit(solution)/shard_map/all_gather | solution.py:243
  9.1 4.4 copy-start.28
  16.9 429.1 %reduce-scatter.5.cloned.1.call-start = ((), (), s32[]{:S(2)}) async-start(), calls=%async_computation.5 | async-start | bytes 15728640 | tf_op jit(solution)/shard_map/reduce_scatter | solution.py:251
  20.3 124.9 %copy-start.19 = (bf16[384,3,96]{0,2,1:T(8,128)(2,1)}, bf16[384,3,96]{0,2,1:T(8,128)(2,1)S(1)}, u32[]{:S(2)}) copy-start(bf16[384,3,96]{0,2,1:T(8,128)(2,1)S(1)} %convert_element_type.112) | copy-start | bytes 663556
  145.2 2.7 copy-start.2
  162.8 19.7 %copy-start.12 = (bf16[128,64,4,24]{1,0,3,2:T(8,128)(2,1)}, bf16[128,64,4,24]{1,0,3,2:T(8,128)(2,1)S(1)}, u32[]{:S(2)}) copy-start(bf16[128,64,4,24]{1,0,3,2:T(8,128)(2,1)S(1)} %reshape.388) | copy-start | bytes 4718596
  182.4 11.8 copy-start.61
  226.3 3.2 copy-start.22
  235.8 332.0 %all-gather.7.cloned.1.call-start = ((), (), s32[]{:S(2)}) async-start(), calls=%async_computation.6 | async-start | bytes 7864320 | tf_op jit(solution)/shard_map/all_gather | solution.py:261
  448.9 118.9 %copy-start.57 = (f32[384]{0:T(512)S(1)}, f32[384]{0:T(512)}, u32[]{:S(2)}) copy-start(f32[384]{0:T(512)} %param.35) | copy-start | bytes 4612
  451.3 231.6 %all-gather.9.cloned.1.call-start = ((), (), s32[]{:S(2)}) async-start(), calls=%async_computation.8 | async-start | bytes 7864320 | tf_op jit(solution)/shard_map/all_gather | solution.py:278
  451.8 366.4 %reduce-scatter.9.cloned.1.call-start = ((), (), s32[]{:S(2)}) async-start(), calls=%async_computation.9 | async-start | bytes 7864320 | tf_op jit(solution)/shard_map/reduce_scatter | solution.py:285
  709.1 222.6 %reduce-scatter.7.cloned.1.call-start = ((), (), s32[]{:S(2)}) async-start(), calls=%async_computation.7 | async-start | bytes 7864320 | tf_op jit(solution)/shard_map/reduce_scatter | solution.py:270
  719.1 212.6 %copy-start.48 = (f32[384]{0:T(512)S(1)}, f32[384]{0:T(512)}, u32[]{:S(2)}) copy-start(f32[384]{0:T(512)} %get-tuple-element.42) | copy-start | bytes 4612
  719.1 336.8 %all-gather.11.cloned.1.call-start = ((), (), s32[]{:S(2)}) async-start(), calls=%async_computation.10 | async-start | bytes 7864320 | tf_op jit(solution)/shard_map/all_gather | solution.py:294
  931.7 5.8 copy-start.8
  935.8 4.1 copy-start.35
  939.9 397.3 %all-reduce.4.cloned.1.call-start = ((), (), s32[]{:S(2)}) async-start(), calls=%async_computation.12 | async-start | bytes 3538944 | tf_op jit(solution)/shard_map/psum | solution.py:325
  948.8 107.1 %copy-start.23 = (f32[96,384]{1,0:T(8,128)S(1)}, f32[96,384]{1,0:T(8,128)}, u32[]{:S(2)}) copy-start(f32[96,384]{1,0:T(8,128)} %param.33) | copy-start | bytes 442372
  1073.7 11.6 copy-start.62
  1085.3 13.0 copy-start.13
  1165.2 11.1 copy-start.11
  1252.6 5.3 copy-start.10
  1261.4 9.7 slice-start.2
  1261.4 15.0 slice-start
  1264.1 7.0 slice-start.3
  1264.1 7.0 copy-start.14
  1264.1 12.3 slice-start.1
  1271.1 5.3 copy-start.4
  1278.5 171.5 %reduce-scatter.11.cloned.1.call-start = ((), (), s32[]{:S(2)}) async-start(), calls=%async_computation.11 | async-start | bytes 7864320 | tf_op jit(solution)/shard_map/reduce_scatter | solution.py:305
  1287.9 60.8 %copy-start.47 = (f32[384]{0:T(512)S(1)}, f32[384]{0:T(512)}, u32[]{:S(2)}) copy-start(f32[384]{0:T(512)} %get-tuple-element.79) | copy-start | bytes 4612
  1287.9 162.1 %copy-start = (bf16[2048,384]{1,0:T(8,128)(2,1)S(1)}, bf16[2048,384]{1,0:T(8,128)(2,1)}, u32[]{:S(2)}) copy-start(bf16[2048,384]{1,0:T(8,128)(2,1)} %param.27) | copy-start | bytes 4718596
  1287.9 162.0 %copy-start.29 = (f32[2048]{0:T(1024)S(1)}, f32[2048]{0:T(1024)}, u32[]{:S(2)}) copy-start(f32[2048]{0:T(1024)} %copy-done.28) | copy-start | bytes 24580
  1287.9 162.0 %copy-start.38 = (f32[384]{0:T(512)S(1)}, f32[384]{0:T(512)}, u32[]{:S(2)}) copy-start(f32[384]{0:T(512)} %copy-done.37) | copy-start | bytes 4612
  1287.9 164.9 %copy-start.34 = (f32[2048]{0:T(1024)S(1)}, f32[2048]{0:T(1024)}, u32[]{:S(2)}) copy-start(f32[2048]{0:T(1024)} %copy-done.33) | copy-start | bytes 24580
  1287.9 164.9 %copy-start.31 = (f32[2048]{0:T(1024)S(1)}, f32[2048]{0:T(1024)}, u32[]{:S(2)}) copy-start(f32[2048]{0:T(1024)} %copy-done.30) | copy-start | bytes 24580
  1288.0 167.9 %copy-start.9 = (bf16[2048,384]{1,0:T(8,128)(2,1)S(1)}, bf16[2048,384]{1,0:T(8,128)(2,1)}, u32[]{:S(2)}) copy-start(bf16[2048,384]{1,0:T(8,128)(2,1)} %param.28) | copy-start | bytes 4718596
  1288.0 167.9 %copy-start.36 = (f32[2048]{0:T(1024)S(1)}, f32[2048]{0:T(1024)}, u32[]{:S(2)}) copy-start(f32[2048]{0:T(1024)} %copy-done.35) | copy-start | bytes 24580
  1304.6 148.2 %copy-start.59 = (f32[2,96]{1,0:T(2,128)}, f32[2,96]{1,0:T(2,128)S(1)}, u32[]{:S(2)}) copy-start(f32[2,96]{1,0:T(2,128)S(1)} %get-tuple-element.116) | copy-start | bytes 2308
  1304.7 199.1 %copy-start.49 = (f32[384]{0:T(512)}, f32[384]{0:T(512)S(1)}, u32[]{:S(2)}) copy-start(f32[384]{0:T(512)S(1)} %get-tuple-element.132) | copy-start | bytes 4612
  1304.7 200.4 %copy-start.42 = (f32[225,4]{0,1:T(4,128)}, f32[225,4]{0,1:T(4,128)S(1)}, u32[]{:S(2)}) copy-start(f32[225,4]{0,1:T(4,128)S(1)} %get-tuple-element.120) | copy-start | bytes 10804
  1449.9 5.9 copy-start.6
  1450.0 5.9 copy-start.7
  1455.7 46.7 %copy-start.55 = (f32[2,96]{1,0:T(2,128)S(1)}, f32[2,96]{1,0:T(2,128)}, u32[]{:S(2)}) copy-start(f32[2,96]{1,0:T(2,128)} %param.31) | copy-start | bytes 2308
  1455.7 48.0 %copy-start.58 = (f32[384]{0:T(512)S(1)}, f32[384]{0:T(512)}, u32[]{:S(2)}) copy-start(f32[384]{0:T(512)} %param.35) | copy-start | bytes 4612
  1455.7 49.3 %copy-start.51 = (f32[225,4]{0,1:T(4,128)S(1)}, f32[225,4]{0,1:T(4,128)}, u32[]{:S(2)}) copy-start(f32[225,4]{0,1:T(4,128)} %param.32) | copy-start | bytes 10804
  1455.7 49.3 %copy-start.52 = (f32[225,4]{0,1:T(4,128)S(1)}, f32[225,4]{0,1:T(4,128)}, u32[]{:S(2)}) copy-start(f32[225,4]{0,1:T(4,128)} %param.43) | copy-start | bytes 10804
  1455.7 49.3 %copy-start.53 = (f32[225,4]{0,1:T(4,128)S(1)}, f32[225,4]{0,1:T(4,128)}, u32[]{:S(2)}) copy-start(f32[225,4]{0,1:T(4,128)} %param.42) | copy-start | bytes 10804
  1455.8 49.9 %copy-start.39 = (f32[6,384]{1,0:T(8,128)S(1)}, f32[6,384]{1,0:T(8,128)}, u32[]{:S(2)}) copy-start(f32[6,384]{1,0:T(8,128)} %param.37) | copy-start | bytes 27652
  1455.8 49.9 %copy-start.43 = (f32[6,384]{1,0:T(8,128)S(1)}, f32[6,384]{1,0:T(8,128)}, u32[]{:S(2)}) copy-start(f32[6,384]{1,0:T(8,128)} %param.53) | copy-start | bytes 27652
  1455.8 49.9 %copy-start.44 = (f32[6,384]{1,0:T(8,128)S(1)}, f32[6,384]{1,0:T(8,128)}, u32[]{:S(2)}) copy-start(f32[6,384]{1,0:T(8,128)} %param.52) | copy-start | bytes 27652
  1455.8 50.5 %copy-start.24 = (f32[96,384]{1,0:T(8,128)S(1)}, f32[96,384]{1,0:T(8,128)}, u32[]{:S(2)}) copy-start(f32[96,384]{1,0:T(8,128)} %param.33) | copy-start | bytes 442372
  1455.8 50.5 %copy-start.25 = (f32[96,384]{1,0:T(8,128)S(1)}, f32[96,384]{1,0:T(8,128)}, u32[]{:S(2)}) copy-start(f32[96,384]{1,0:T(8,128)} %get-tuple-element.124) | copy-start | bytes 442372
  1459.1 54.9 %copy-start.15 = (f32[384,384]{1,0:T(8,128)S(1)}, f32[384,384]{1,0:T(8,128)}, u32[]{:S(2)}) copy-start(f32[384,384]{1,0:T(8,128)} %get-tuple-element.136) | copy-start | bytes 1769476
  1459.1 54.9 %copy-start.18 = (f32[384,384]{1,0:T(8,128)S(1)}, f32[384,384]{1,0:T(8,128)}, u32[]{:S(2)}) copy-start(f32[384,384]{1,0:T(8,128)} %param.36) | copy-start | bytes 1769476
  1459.1 54.9 %copy-start.26 = (f32[384,384]{1,0:T(8,128)S(1)}, f32[384,384]{1,0:T(8,128)}, u32[]{:S(2)}) copy-start(f32[384,384]{1,0:T(8,128)} %param.51) | copy-start | bytes 1769476
  1459.1 54.9 %copy-start.27 = (f32[384,384]{1,0:T(8,128)S(1)}, f32[384,384]{1,0:T(8,128)}, u32[]{:S(2)}) copy-start(f32[384,384]{1,0:T(8,128)} %param.50) | copy-start | bytes 1769476
  1500.4 15.1 copy-start.32
  1502.3 13.2 copy-start.17
  1508.1 8.8 copy-start.16
  (12 other events, 18.0 us)
Sparse Core Ops, SparseCore 0:
  17.0 118.0 all-gather.4
  235.9 210.0 reduce-scatter.4
  451.4 116.4 all-gather.6
  569.3 113.5 all-gather.8
  709.2 108.9 reduce-scatter.8
  820.4 111.2 reduce-scatter.6
  940.0 115.8 all-gather.10
  1278.6 58.5 all-reduce.3
  1339.6 110.2 reduce-scatter.10
where the time goes:
time: 1540 us; the launch traced here: 1530 us
  waiting for transfers between devices  946 us (61%)
  matrix products  201 us (13%)
  local copies, waits for them, and re-layouts  180 us (12%)
  other arithmetic  108 us (7%)
  blocking collectives  68.2 us (4%)
  between operations  22.4 us (1%)
    reduce_scatter x1, waiting for transfers between devices, shards(): lax.psum_scatter(jnp.dot(block_rows, proj_low, preferred_element_type=jnp...  210 us
    all_gather x1, waiting for transfers between devices, shards(): lax.all_gather(normed_two.astype(jnp.bfloat16), 'head', axis=0, tiled=True)  116 us
    all_gather x1, waiting for transfers between devices, shards(): lax.all_gather(normed_one.astype(jnp.bfloat16), 'head', axis=0, tiled=True)  112 us
    reduce_scatter x1, waiting for transfers between devices, shards(): lax.psum_scatter(jnp.dot(block_rows, fc2_low, preferred_element_type=jnp....  110 us
    reduce_scatter x1, waiting for transfers between devices, shards(): lax.psum_scatter(jnp.dot(block_rows, fc1_low.T, preferred_element_type=jn...  99.1 us
    all_gather x1, waiting for transfers between devices, shards(): gathered_branch = lax.all_gather(d_branch, 'head', axis=0, tiled=True)  97.5 us
    reduce_scatter x1, waiting for transfers between devices, shards(): lax.psum_scatter(jnp.dot(block_rows, qkv_low.T, preferred_element_type=jn...  88.5 us
    all_gather x1, waiting for transfers between devices, shards(): gathered_cot = lax.all_gather(out_grad, 'head', axis=0, tiled=True)  81.1 us
  transfers between devices with their start and end apart: 9, of which 9 were waited for; matrix products, arithmetic and copies ran while one was open for 6% of the time, Pallas kernels for 0%

commit v1 on v0

v1 whole, which is shorter than its diff:
```python
from functools import partial

import jax
import jax.numpy as jnp
from jax import lax
from jax.experimental import pallas as pl
from jax.experimental.pallas import tpu as pltpu
from jax.sharding import PartitionSpec as P

D = 384
HDIM = 24
HEADS = 16
GROUPS = 4
PER = 4
LANES = 128
FF = 1536
GRID = 16
WIN = 8
CLIP = GRID * GRID
SPOT = WIN * WIN
SHIFT = 4
STEP = 10
CHUNK = 384

NORM_EPS = 1e-05
MASKED = -1000000000.0
CLIP_LIMIT = 1.0
LEARN_RATE = 0.1
ROW_RATE = 0.5
BETA_ONE = 0.9
BETA_TWO = 0.999
ADAM_EPS = 1e-08
WEIGHT_DECAY = 0.01
SCALE = HDIM ** (-0.5)
F32 = jnp.float32
BF16 = jnp.bfloat16
VMEM_LIMIT = 58 * 1024 * 1024


def nn(a, b):
    return lax.dot_general(a, b, (((1,), (0,)), ((), ())), preferred_element_type=F32)


def nt(a, b):
    return lax.dot_general(a, b, (((1,), (1,)), ((), ())), preferred_element_type=F32)


def tn(a, b):
    return lax.dot_general(a, b, (((0,), (0,)), ((), ())), preferred_element_type=F32)


def iota(shape, axis):
    return lax.broadcasted_iota(jnp.int32, shape, axis)


def fold(x):
    return jnp.sum(x.reshape(x.shape[0] // 8, 8, x.shape[1]), axis=0)


def normalize(x):
    center = x - jnp.mean(x, axis=-1, keepdims=True)
    spread = jnp.mean(center * center, axis=-1, keepdims=True)
    inverse = lax.rsqrt(spread + NORM_EPS)
    return center * inverse, inverse


def norm_back(e, n, inverse, gain):
    q = e * gain
    return inverse * (
        q - jnp.mean(q, axis=-1, keepdims=True) - n * jnp.mean(q * n, axis=-1, keepdims=True)
    )


def to_windows(x):
    low = iota((8, x.shape[1]), 0) < 4
    first, second = [], []
    for t in range(GRID):
        a = x[16 * t : 16 * t + 8]
        b = x[16 * t + 8 : 16 * t + 16]
        first.append(pltpu.roll(jnp.where(low, b, a), 4, axis=0))
        second.append(pltpu.roll(jnp.where(low, a, b), 4, axis=0))
    pieces = []
    for wt in range(2):
        for side in (first, second):
            for a in range(WIN):
                pieces.append(side[(wt * WIN + a + SHIFT) % GRID])
    return jnp.concatenate(pieces, axis=0)


def from_windows(y):
    low = iota((8, y.shape[1]), 0) < 4
    pieces = []
    for t in range(GRID):
        rolled = (t - SHIFT) % GRID
        base = (rolled // WIN) * 128 + (rolled % WIN) * 8
        u = pltpu.roll(y[base : base + 8], 4, axis=0)
        v = pltpu.roll(y[base + 64 : base + 72], 4, axis=0)
        pieces.append(jnp.where(low, v, u))
        pieces.append(jnp.where(low, u, v))
    return jnp.concatenate(pieces, axis=0)


def head_masks(dtype):
    lane = iota((16, LANES), 1) // HDIM
    return [jnp.where(lane == h, 1.0, 0.0).astype(F32).astype(dtype) for h in range(PER)]


def stack_heads(x, masks):
    tiles = x.reshape(SPOT // 16, 16, LANES)
    return jnp.concatenate([(tiles * m[None]).reshape(SPOT, LANES) for m in masks], axis=0)


def pick_heads(r):
    lane = iota((SPOT, LANES), 1)
    out = r[3 * SPOT :]
    for h in (2, 1, 0):
        out = jnp.where(lane < (h + 1) * HDIM, r[h * SPOT : (h + 1) * SPOT], out)
    return out


def key_times(wt, wf):
    j = iota((SPOT, PER * SPOT), 0)
    i = iota((SPOT, PER * SPOT), 1) % SPOT
    time = (wt * WIN + j // WIN + SHIFT) % GRID
    same = j >= 0
    if wt:
        same = same & ((j // WIN < 4) == (i // WIN < 4))
    if wf:
        same = same & ((j % WIN < 4) == (i % WIN < 4))
    return jnp.where(same, time, 99)


def split_three(x):
    one = x.astype(BF16)
    rest = x - one.astype(F32)
    two = rest.astype(BF16)
    three = (rest - two.astype(F32)).astype(BF16)
    return one, two, three


def build_bias(table_ref, bias_ref):
    row = iota((256, 256), 0)
    lane = iota((256, 256), 1)
    spot = lane % SPOT
    base = spot // WIN * (2 * WIN - 1) + spot % WIN
    for g in range(GROUPS):
        total = None
        for h in range(PER):
            head = g * PER + h
            own = jnp.where((row == base) & (lane // SPOT == h), 1.0, 0.0).astype(F32).astype(BF16)
            line = jnp.broadcast_to(table_ref[head : head + 1, :], (8, 256))
            spread = jnp.concatenate(
                [
                    pltpu.roll(line, (15 * a + 144) % 256, axis=1, stride=1, stride_axis=0)
                    for a in range(WIN)
                ],
                axis=0,
            )
            for part in split_three(spread):
                term = nn(part, own)
                total = term if total is None else total + term
        bias_ref[g] = total


def gelu_parts(u):
    mag = jnp.abs(u) * (0.5**0.5)
    t = 1.0 / (1.0 + 0.3275911 * mag)
    bell = jnp.exp(-0.5 * (u * u))
    poly = t * (
        0.127414796
        + t * (-0.142248368 + t * (0.7107068705 + t * (-0.7265760135 + t * 0.5307027145)))
    )
    tail = poly * bell
    return jnp.where(u >= 0.0, 1.0 - tail, tail), bell * 0.3989422804014327


def front_kernel(
    frames_ref,
    tok_ref,
    og_ref,
    wqkv_ref,
    bqv_ref,
    table_ref,
    wproj_ref,
    w1_ref,
    b1_ref,
    w2_ref,
    rowp_ref,
    out_ref,
    qkv_ref,
    probs_ref,
    datt_ref,
    dmid_ref,
    g1_ref,
    g2_ref,
    gp_ref,
    rows_ref,
    gb_ref,
    bias_ref,
    time_ref,
    att_ref,
):
    step = pl.program_id(0)

    @pl.when(step == 0)
    def _():
        build_bias(table_ref, bias_ref)
        for wt in range(2):
            for wf in range(2):
                time_ref[wt * 2 + wf] = key_times(wt, wf)
        for ref in (g1_ref, g2_ref, gp_ref, rows_ref, gb_ref):
            ref[...] = jnp.zeros_like(ref)

    frames = frames_ref[step]
    x = to_windows(tok_ref[...].astype(F32))
    og = to_windows(og_ref[...].astype(F32))
    n1, _ = normalize(x)
    n1 = (n1 * rowp_ref[0:1] + rowp_ref[1:2]).astype(BF16)
    for part in range(3):
        cols = slice(part * 512, part * 512 + 512)
        y = nn(n1, wqkv_ref[:, cols])
        if part == 0:
            y = y + bqv_ref[0:1]
        if part == 2:
            y = y + bqv_ref[1:2]
        qkv_ref[:, cols] = y.astype(BF16)
    masks = head_masks(BF16)
    for w in range(4):
        rows = slice(w * SPOT, w * SPOT + SPOT)
        for g in range(GROUPS):
            q = qkv_ref[rows, g * LANES : g * LANES + LANES]
            k = qkv_ref[rows, 512 + g * LANES : 512 + g * LANES + LANES]
            v = qkv_ref[rows, 1024 + g * LANES : 1024 + g * LANES + LANES]
            s = nt(k, stack_heads(q, masks)) * SCALE + bias_ref[g]
            s = jnp.where(time_ref[w] < frames, s, MASKED)
            e = jnp.exp(s - jnp.max(s, axis=0, keepdims=True))
            p = (e * (1.0 / jnp.sum(e, axis=0, keepdims=True))).astype(BF16)
            probs_ref[0, w, g] = p
            o = pick_heads(tn(p, v))
            att_ref[rows, g * LANES : g * LANES + LANES] = o.astype(BF16)
    att = att_ref[...]
    middle = x + nn(att, wproj_ref[...]) + rowp_ref[4:5]
    nrm, inv = normalize(middle)
    n2f = nrm * rowp_ref[2:3] + rowp_ref[3:4]
    n2 = n2f.astype(BF16)
    n2t = n2.T
    ogb = og.astype(BF16)
    ogt = ogb.T
    ffn = None
    dn2 = None
    for c in range(FF // CHUNK):
        cols = slice(c * CHUNK, c * CHUNK + CHUNK)
        u = nn(n2, w1_ref[:, cols]) + b1_ref[0:1, cols]
        phi, dens = gelu_parts(u)
        hid = (u * phi).astype(BF16)
        du = ((phi + u * dens) * nt(ogb, w2_ref[cols, :])).astype(BF16)
        gb_ref[:, cols] += fold(du.astype(F32))
        g1_ref[:, cols] += nn(n2t, du)
        g2_ref[:, cols] += nn(ogt, hid)
        a = nn(hid, w2_ref[cols, :])
        b = nt(du, w1_ref[:, cols])
        ffn = a if ffn is None else ffn + a
        dn2 = b if dn2 is None else dn2 + b
    out_ref[...] = from_windows(middle + ffn + rowp_ref[5:6])
    dmid = og + norm_back(dn2, nrm, inv, rowp_ref[2:3])
    dmid_ref[...] = dmid
    dbr = dmid.astype(BF16)
    rows_ref[0] += fold(dn2 * nrm)
    rows_ref[1] += fold(dn2)
    rows_ref[2] += fold(dbr.astype(F32))
    rows_ref[3] += fold(og)
    gp_ref[...] += tn(att, dbr)
    datt_ref[...] = nt(dbr, wproj_ref[...]).astype(BF16)


def back_kernel(
    frames_ref,
    tok_ref,
    qkv_ref,
    probs_ref,
    datt_ref,
    dmid_ref,
    wqkv_ref,
    rowp_ref,
    din_ref,
    gq_ref,
    rows_ref,
    gqv_ref,
    gt_ref,
    time_ref,
    tacc_ref,
    dj_ref,
):
    step = pl.program_id(0)

    @pl.when(step == 0)
    def _():
        for wt in range(2):
            for wf in range(2):
                time_ref[wt * 2 + wf] = key_times(wt, wf)
        for ref in (gq_ref, rows_ref, gqv_ref, tacc_ref):
            ref[...] = jnp.zeros_like(ref)

    frames = frames_ref[step]
    masks = head_masks(BF16)
    for g in range(GROUPS):
        tacc = None
        for w in range(4):
            rows = slice(w * SPOT, w * SPOT + SPOT)
            cq = slice(g * LANES, g * LANES + LANES)
            ck = slice(512 + g * LANES, 512 + g * LANES + LANES)
            cv = slice(1024 + g * LANES, 1024 + g * LANES + LANES)
            q = qkv_ref[rows, cq]
            k = qkv_ref[rows, ck]
            v = qkv_ref[rows, cv]
            do = stack_heads(datt_ref[rows, cq], masks)
            p = probs_ref[0, w, g]
            pf = p.astype(F32)
            dp = nt(v, do)
            inner = jnp.sum(pf * dp, axis=0, keepdims=True)
            ds = jnp.where(time_ref[w] < frames, pf * (dp - inner), 0.0)
            tacc = ds if tacc is None else tacc + ds
            ds = ds.astype(BF16)
            dj_ref[rows, cq] = (pick_heads(tn(ds, k)) * SCALE).astype(BF16)
            dj_ref[rows, ck] = (nn(ds, stack_heads(q, masks)) * SCALE).astype(BF16)
            dj_ref[rows, cv] = nn(p, do).astype(BF16)
        tacc_ref[g] += tacc
    n, inv = normalize(to_windows(tok_ref[...].astype(F32)))
    n1t = (n * rowp_ref[0:1] + rowp_ref[1:2]).astype(BF16).T
    dj = dj_ref[...]
    gqv_ref[:, :512] += fold(dj[:, :512].astype(F32))
    gqv_ref[:, 512:] += fold(dj[:, 1024:].astype(F32))
    dn1 = nt(dj, wqkv_ref[...])
    gq_ref[...] += nn(n1t, dj)
    rows_ref[0] += fold(dn1 * n)
    rows_ref[1] += fold(dn1)
    din = dmid_ref[...] + norm_back(dn1, n, inv, rowp_ref[0:1])
    din_ref[...] = from_windows(din)

    @pl.when(step == pl.num_programs(0) - 1)
    def _():
        row = iota((256, 256), 0)
        lane = iota((256, 256), 1)
        spot = row % SPOT
        base = 112 - (spot // WIN * (2 * WIN - 1) + spot % WIN)
        for h in range(PER):
            own = jnp.where((lane == base) & (row // SPOT == h), 1.0, 0.0).astype(F32).astype(BF16)
            for g in range(GROUPS):
                spread = None
                for part in split_three(tacc_ref[g]):
                    term = nn(part, own)
                    spread = term if spread is None else spread + term
                total = None
                for a in range(WIN):
                    piece = pltpu.roll(
                        spread[a * 8 : a * 8 + 8], 15 * a, axis=1, stride=1, stride_axis=0
                    )
                    total = piece if total is None else total + piece
                head = g * PER + h
                gt_ref[head : head + 1, :] = jnp.sum(total, axis=0, keepdims=True)


def whole(shape):
    return pl.BlockSpec(shape, lambda i: (0,) * len(shape))


def front(frames, tok, og, wqkv, bqv, table, wproj, w1, b1, w2, rowp):
    rows = tok.shape[0]
    clips = rows // CLIP
    line = lambda width: pl.BlockSpec((CLIP, width), lambda i: (i, 0))
    probs = (1, 4, GROUPS, SPOT, PER * SPOT)
    shape = jax.ShapeDtypeStruct
    return pl.pallas_call(
        front_kernel,
        grid=(clips,),
        in_specs=[pl.BlockSpec(memory_space=pltpu.SMEM), line(D), line(D)]
        + [whole(a.shape) for a in (wqkv, bqv, table, wproj, w1, b1, w2, rowp)],
        out_specs=[
            line(D),
            line(1536),
            pl.BlockSpec(probs, lambda i: (i, 0, 0, 0, 0)),
            line(512),
            line(D),
            whole((D, FF)),
            whole((D, FF)),
            whole((512, D)),
            whole((4, 8, D)),
            whole((8, FF)),
        ],
        out_shape=[
            shape((rows, D), F32),
            shape((rows, 1536), BF16),
            shape((clips,) + probs[1:], BF16),
            shape((rows, 512), BF16),
            shape((rows, D), F32),
            shape((D, FF), F32),
            shape((D, FF), F32),
            shape((512, D), F32),
            shape((4, 8, D), F32),
            shape((8, FF), F32),
        ],
        scratch_shapes=[
            pltpu.VMEM((GROUPS, SPOT, PER * SPOT), F32),
            pltpu.VMEM((4, SPOT, PER * SPOT), jnp.int32),
            pltpu.VMEM((CLIP, 512), BF16),
        ],
        compiler_params=pltpu.CompilerParams(vmem_limit_bytes=VMEM_LIMIT),
    )(frames, tok, og, wqkv, bqv, table, wproj, w1, b1, w2, rowp)


def back(frames, tok, qkv, probs, datt, dmid, wqkv, rowp):
    rows = tok.shape[0]
    clips = rows // CLIP
    line = lambda width: pl.BlockSpec((CLIP, width), lambda i: (i, 0))
    shape = jax.ShapeDtypeStruct
    return pl.pallas_call(
        back_kernel,
        grid=(clips,),
        in_specs=[
            pl.BlockSpec(memory_space=pltpu.SMEM),
            line(D),
            line(1536),
            pl.BlockSpec((1,) + probs.shape[1:], lambda i: (i, 0, 0, 0, 0)),
            line(512),
            line(D),
            whole(wqkv.shape),
            whole(rowp.shape),
        ],
        out_specs=[
            line(D),
            whole((D, 1536)),
            whole((2, 8, D)),
            whole((8, 1024)),
            whole((HEADS, 256)),
        ],
        out_shape=[
            shape((rows, D), F32),
            shape((D, 1536), F32),
            shape((2, 8, D), F32),
            shape((8, 1024), F32),
            shape((HEADS, 256), F32),
        ],
        scratch_shapes=[
            pltpu.VMEM((4, SPOT, PER * SPOT), jnp.int32),
            pltpu.VMEM((GROUPS, SPOT, PER * SPOT), F32),
            pltpu.VMEM((CLIP, 1536), BF16),
        ],
        compiler_params=pltpu.CompilerParams(vmem_limit_bytes=VMEM_LIMIT),
    )(frames, tok, qkv, probs, datt, dmid, wqkv, rowp)


def adam_step(weight, gradient, moment, second, factor, rate):
    clipped = gradient * factor
    moment_new = BETA_ONE * moment + (1.0 - BETA_ONE) * clipped
    second_new = BETA_TWO * second + (1.0 - BETA_TWO) * clipped * clipped
    moment_hat = moment_new / (1.0 - BETA_ONE**STEP)
    second_hat = second_new / (1.0 - BETA_TWO**STEP)
    master = weight - rate * (
        moment_hat / (jnp.sqrt(second_hat) + ADAM_EPS) + WEIGHT_DECAY * weight
    )
    return (gradient, moment_new, second_new, master)


def shards(
    tokens,
    out_grad,
    clip_frames,
    qkv_weight,
    qv_bias,
    rel_table,
    proj_weight,
    fc1_weight,
    fc1_bias,
    fc2_weight,
    row_params,
    qkv_first,
    qkv_second,
    qvb_first,
    qvb_second,
    table_first,
    table_second,
    proj_first,
    proj_second,
    fc1_first,
    fc1_second,
    fc1b_first,
    fc1b_second,
    fc2_first,
    fc2_second,
    rows_first,
    rows_second,
):
    gather = partial(lax.all_gather, axis_name="head", tiled=True)
    clips = tokens.shape[0] // CLIP
    parts = lax.axis_size("head")
    local = rel_table.shape[1] * HDIM
    groups = rel_table.shape[1] // PER
    frames = lax.dynamic_slice(clip_frames, (lax.axis_index("head") * clips,), (clips,))
    pad = LANES - PER * HDIM
    wqkv = qkv_weight.astype(BF16).reshape(D, 3, groups, PER * HDIM)
    wqkv = gather(jnp.pad(wqkv, ((0, 0), (0, 0), (0, 0), (0, pad))), axis=2).reshape(D, 1536)
    bqv = jnp.pad(qv_bias.reshape(2, groups, PER * HDIM), ((0, 0), (0, 0), (0, pad)))
    bqv = gather(bqv, axis=1).reshape(2, 512)
    table = gather(jnp.pad(rel_table.T, ((0, 0), (0, 256 - rel_table.shape[0]))), axis=0)
    wproj = proj_weight.astype(BF16).reshape(groups, PER * HDIM, D)
    wproj = gather(jnp.pad(wproj, ((0, 0), (0, pad), (0, 0))), axis=0).reshape(512, D)
    w1 = gather(fc1_weight.astype(BF16), axis=1)
    b1 = gather(fc1_bias, axis=0).reshape(1, FF)
    w2 = gather(fc2_weight.astype(BF16), axis=0)
    output, qkv, probs, datt, dmid, g1, g2, gp, rows_f, gb = front(
        frames, tokens, out_grad, wqkv, bqv, table, wproj, w1, b1, w2, row_params
    )
    input_grad, gq, rows_b, gqv, gt = back(
        frames, tokens, qkv, probs, datt, dmid, wqkv, row_params
    )
    scatter = lambda v, dim: lax.psum(
        lax.psum_scatter(v, "head", scatter_dimension=dim, tiled=True), "win"
    )
    qkv_summed = scatter(gq.reshape(D, 3, GROUPS, LANES), 2)[..., : PER * HDIM].reshape(D, 3, local)
    gqv = jnp.sum(gqv, axis=0).reshape(2, GROUPS, LANES)
    qvb_summed = scatter(gqv, 1)[..., : PER * HDIM].reshape(2, local)
    table_summed = scatter(gt, 0)[:, : rel_table.shape[0]][:, ::-1].T
    proj_summed = scatter(gp.reshape(GROUPS, LANES, D), 0)[:, : PER * HDIM].reshape(local, D)
    fc1_summed = scatter(g1, 1)
    fc1b_summed = scatter(jnp.sum(gb, axis=0), 0)
    fc2_summed = scatter(g2, 1).T
    rows_gradient = lax.psum(jnp.sum(jnp.concatenate([rows_b, rows_f]), axis=1), ("win", "head"))
    gradients = (
        qkv_summed,
        qvb_summed,
        table_summed,
        proj_summed,
        fc1_summed,
        fc1b_summed,
        fc2_summed,
        rows_gradient,
    )
    square = lambda v: jnp.sum(v * v)
    total = lax.psum(sum(square(g) for g in gradients[:7]), "head")
    grad_norm = jnp.sqrt(total + square(rows_gradient))
    factor = jnp.minimum(1.0, CLIP_LIMIT / (grad_norm + 1e-06))
    weights = (
        qkv_weight,
        qv_bias,
        rel_table,
        proj_weight,
        fc1_weight,
        fc1_bias,
        fc2_weight,
        row_params,
    )
    firsts = (
        qkv_first,
        qvb_first,
        table_first,
        proj_first,
        fc1_first,
        fc1b_first,
        fc2_first,
        rows_first,
    )
    seconds = (
        qkv_second,
        qvb_second,
        table_second,
        proj_second,
        fc1_second,
        fc1b_second,
        fc2_second,
        rows_second,
    )
    rates = (
        LEARN_RATE,
        LEARN_RATE,
        ROW_RATE,
        LEARN_RATE,
        LEARN_RATE,
        LEARN_RATE,
        LEARN_RATE,
        ROW_RATE,
    )
    updated = []
    for weight, gradient, moment, second, rate in zip(weights, gradients, firsts, seconds, rates):
        updated.extend(adam_step(weight, gradient, moment, second, factor, rate))
    return (output, input_grad, grad_norm, *updated)


def solution(mesh):
    rows = P(("win", "head"), None)
    last3, last2, first2, first1 = P(None, None, "head"), P(None, "head"), P("head", None), P("head")
    each = (last3, last2, last2, first2, last2, first1, first2, P())
    return jax.shard_map(
        shards,
        mesh=mesh,
        in_specs=(rows, rows, P("win")) + each + tuple(s for s in each for _ in range(2)),
        out_specs=(rows, rows, P()) + tuple(s for s in each for _ in range(4)),
        check_vma=False,
    )
```

time: 1540 us -> 482 us (0.31)
  waiting for transfers between devices: 946 us -> 163 us
  matrix products: 201 us -> 0 us
  local copies, waits for them, and re-layouts: 180 us -> 33.8 us
  Pallas kernels: 0 us -> 96.2 us
  other arithmetic: 108 us -> 24.1 us
  blocking collectives: 68.2 us -> 141 us
    reduce_scatter x4, waiting for transfers between devices: 508 us -> 119 us  [shards(): lax.psum_scatter(v, 'head', scatter_dimension=dim, tiled=True)]
    all_gather x4 -> x3, waiting for transfers between devices: 407 us -> 37 us  [the longest x1 31.8 us: shards(): w1 = gather(fc1_weight.astype(BF16), axis=1)]
    dot_general x19 -> x0, matrix products: 181 us -> none  [the longest x1 34 us: shards(): jnp.dot(gathered_two, fc1_low, preferred_element_type=jnp.float32)]
    pallas_call x0 -> x2, Pallas kernels: none -> 96.2 us  [the longest x1 58.1 us: front(): pl.pallas_call(front_kernel, grid=(clips,), in_specs=[pl.BlockSpec(memory...]
    convert_element_type x8 -> x0, local copies, waits for them, and re-layouts: 59 us -> none  [the longest x2 16 us: attend_backward(): d_query = (jnp.einsum('whqk,wkhd->wqhd', d_scores, keys_heads, preferred_...]
    all_gather x0 -> x4, blocking collectives: none -> 56.1 us  [the longest x1 17.4 us: shards(): gather(jnp.pad(wproj, ((0, 0), (0, pad), (0, 0))), axis=0).reshape(512, D)]
    another operation x8 -> x0, local copies, waits for them, and re-layouts: 38.7 us -> none  [the longest x1 20.8 us: from_windows(): values.reshape(number, GRID // WIN, GRID // WIN, WIN, WIN, columns)]
    concatenate x3 -> x0, local copies, waits for them, and re-layouts: 31.8 us -> none  [attend_backward(): d_joined = jnp.concatenate([d_query, d_keys, d_values], axis=1)]
  transfers between devices with their start and end apart: 9 -> 8, of which waited for: 9 -> 6; matrix products, arithmetic and copies ran while one was open for 6% -> 5% of each run, Pallas kernels for 0% -> 8%
where the time goes in v1:
time: 482 us; the launch traced here: 481 us
  waiting for transfers between devices  163 us (34%)
  blocking collectives  141 us (29%)
  Pallas kernels  96.2 us (20%)
  local copies, waits for them, and re-layouts  33.8 us (7%)
  other arithmetic  24.1 us (5%)
  between operations  22.9 us (5%)
    reduce_scatter x4, waiting for transfers between devices, shards(): lax.psum_scatter(v, 'head', scatter_dimension=dim, tiled=True)  119 us
    pallas_call x1, Pallas kernels, front(): pl.pallas_call(front_kernel, grid=(clips,), in_specs=[pl.BlockSpec(memory...  58.1 us
    psum x1, blocking collectives, shards(): lax.psum(jnp.sum(jnp.concatenate([rows_b, rows_f]), axis=1), ('win', 'hea...  39.2 us
    pallas_call x1, Pallas kernels, back(): pl.pallas_call(back_kernel, grid=(clips,), in_specs=[pl.BlockSpec(memory_...  38.1 us
    all_gather x1, waiting for transfers between devices, shards(): w1 = gather(fc1_weight.astype(BF16), axis=1)  31.8 us
    unnamed x89, local copies, waits for them, and re-layouts  21 us
    unnamed x1, blocking collectives  18.9 us
    all_gather x1, blocking collectives, shards(): gather(jnp.pad(wproj, ((0, 0), (0, pad), (0, 0))), axis=0).reshape(512, D)  17.4 us
  transfers between devices with their start and end apart: 8, of which 6 were waited for; matrix products, arithmetic and copies ran while one was open for 5% of the time, Pallas kernels for 8%

profile of v1, /device:TPU:0, one launch (start us, length us, event | category | flops | bytes accessed | tf_op | source)
XLA Modules:
  0.0 481.2 jit_solution(17902563571430713910)
XLA Ops:
  7.3 1.3 copy.100
  8.6 0.8 pad.16
  9.5 1.8 convert_element_type.23
  11.4 0.7 convert_element_type.22
  12.3 14.8 %all-gather = f32[4,4,256]{2,1,0:T(4,128)S(1)} all-gather(f32[1,4,256]{2,1,0:T(4,128)S(1)} %pad_bitcast_fusion), channel_id=1, replica_groups=mesh['win'=8,'head'=4] {'head'}, dimensions={0}, use_global_device_ids=true | all-gather | bytes 20480 | tf_op jit(solution)/shard_map/all_gather | solution.py:504
  27.1 0.6 reshape.123.table_ref
  27.7 0.6 dynamic_slice.3.frames_ref
  28.3 11.7 %all_gather.22 = f32[2,4,128]{2,0,1:T(2,128)} all-gather(f32[2,1,128]{2,0,1:T(2,128)S(1)} %pad.17), channel_id=1, replica_groups=mesh['win'=8,'head'=4] {'head'}, dimensions={1}, use_global_device_ids=true | all-gather | bytes 5120 | tf_op jit(solution)/shard_map/all_gather | solution.py:503
  40.0 12.2 %all-gather.1 = f32[4,1,384]{2,1,0:T(1,128)} all-gather(f32[1,1,384]{2,1,0:T(1,128)S(1)} %reshape.124), channel_id=1, replica_groups=mesh['win'=8,'head'=4] {'head'}, dimensions={0}, use_global_device_ids=true | all-gather | bytes 7680 | tf_op jit(solution)/shard_map/all_gather | solution.py:508
  52.2 17.4 %all_gather.24 = bf16[4,128,384]{2,1,0:T(8,128)(2,1)} all-gather(bf16[1,128,384]{2,1,0:T(8,128)(2,1)S(1)} %pad.19), channel_id=1, replica_groups=mesh['win'=8,'head'=4] {'head'}, dimensions={0}, use_global_device_ids=true | all-gather | bytes 491520 | tf_op jit(solution)/shard_map/all_gather | solution.py:506
  69.5 2.2 copy.101
  71.7 1.3 reshape.110.wqkv_ref
  73.0 5.2 %all-gather.10.cloned.1.call-done.w2_ref = bf16[1536,384]{1,0:T(8,128)(2,1)} async-done(((bf16[384,384]{1,0:T(8,128)(2,1)}), bf16[1536,384]{1,0:T(8,128)(2,1)}) %all-gather.10.cloned.1.call-update) | async-done | bytes 1179664 | tf_op jit(solution)/shard_map/all_gather | solution.py:509
  78.2 31.8 %all-gather.8.cloned.1.call-done.w1_ref = bf16[384,1536]{1,0:T(8,128)(2,1)} async-done(((bf16[384,384]{1,0:T(8,128)(2,1)}), bf16[384,1536]{1,0:T(8,128)(2,1)}) %all-gather.8.cloned.1.call-update) | async-done | bytes 1179664 | tf_op jit(solution)/shard_map/all_gather | solution.py:507
  110.0 58.1 %shard_map.530 = (f32[2048,384]{1,0:T(8,128)}, bf16[2048,1536]{1,0:T(8,128)(2,1)}, bf16[8,4,4,64,256]{4,3,2,1,0:T(8,128)(2,1)}, bf16[2048,512]{1,0:T(8,128)(2,1)...) custom-call(s32[8]{0:T(128)} %dynamic_slice.3.frames_ref, ...), custom_call_target="tpu_custom_call" | custom-call | tf_op jit(solution)/shard_map/pallas_call | solution.py:373
  168.2 0.2 reduce-scatter.5.cloned.1.call-start
  168.4 38.1 %shard_map.531 = (f32[2048,384]{1,0:T(8,128)}, f32[384,1536]{1,0:T(8,128)}, f32[2,8,384]{2,1,0:T(8,128)}, f32[8,1024]{1,0:T(8,128)}, f32[16,256]{1,0:T(8,128)}) custom-call(s32[8]{0:T(128)} %dynamic_slice.3.frames_ref, bf16[2048,384]{1,0:T(8,128)(2,1)} %tok_ref.3, bf16[2048,1536]{1,0:T(8,128)(2,1)} %get-tuple-element.51.qkv_ref, ...), custom_call_target="tpu_custom_call" | custom-call | tf_op jit(solution)/shard_map/pallas_call | solution.py:416
  206.5 2.6 reshape.116
  209.2 2.6 copy.102
  211.8 1.6 copy-done.6
  213.4 2.0 copy.104
  215.5 0.7 reduce-scatter.11.cloned.1.call-update
  216.3 0.2 copy.108
  216.5 0.2 copy.112
  216.8 0.6 dynamic-slice
  218.7 0.2 copy.105
  218.9 0.2 copy.106
  219.2 1.1 copy.109
  220.2 2.1 copy.110
  222.4 18.9 %all-reduce.9 = (f32[2,4,128]{2,0,1:T(2,128)S(1)}, f32[16,256]{1,0:T(8,128)S(1)}, f32[1536]{0:T(1024)S(1)}) all-reduce(f32[2,4,128]{2,0,1:T(2,128)S(1)} %copy.103, f32[16,256]{1,0:T(8,128)S(1)} %copy-done.26, f32[1536]{0:T(1024)S(1)} %reduce_sum.105), channel_id=3, replica_groups=mesh['win'=8,'head'=4] {'head'}, use_global_device_ids=true, to_apply=%region_4.5.clone | all-reduce | flops 6656 | bytes 53248
  241.3 0.1 dynamic-slice.5
  241.4 19.0 %reduce-scatter.5.cloned.1.call-done = f32[384,3,1,128]{0,3,1,2:T(8,128)} async-done(((f32[384,3,4,128]{0,3,1,2:T(8,128)}), f32[384,3,1,128]{0,3,1,2:T(8,128)}) %reduce-scatter.5.cloned.1.call-update) | async-done | bytes 589840 | tf_op jit(solution)/shard_map/reduce_scatter | solution.py:517
  260.4 49.8 %reduce-scatter.9.cloned.1.call-done = f32[384,384]{0,1:T(8,128)} async-done(((f32[384,1536]{0,1:T(8,128)}), f32[384,384]{0,1:T(8,128)}) %reduce-scatter.9.cloned.1.call-update) | async-done | bytes 589840 | tf_op jit(solution)/shard_map/reduce_scatter | solution.py:517
  310.1 49.9 %reduce-scatter.11.cloned.1.call-done = f32[384,384]{1,0:T(8,128)} async-done(((f32[384,1536]{1,0:T(8,128)}), f32[384,384]{1,0:T(8,128)}) %reduce-scatter.11.cloned.1.call-update) | async-done | bytes 589840 | tf_op jit(solution)/shard_map/reduce_scatter | solution.py:517
  360.0 0.7 constant_dynamic-slice_fusion.1
  360.7 13.9 %all-reduce.7 = (f32[2,1,128]{2,0,1:T(2,128)S(1)}, f32[4,256]{1,0:T(4,128)S(1)}, f32[384]{0:T(512)S(1)}) all-reduce(f32[2,1,128]{2,0,1:T(2,128)S(1)} %constant_dynamic-slice_fusion.1, f32[4,256]{1,0:T(4,128)S(1)} %constant_dynamic-slice_fusion, f32[384]{0:T(512)S(1)} %dynamic-slice.5), channel_id=1, replica_groups=mesh['win'=8,'head'=4] {'win'}, use_global_device_ids=true, to_apply=%region_5.6 | all-reduce | flops 1664 | bytes 13312 | tf_op jit(solution)/shard_map/psum | solution.py:516
  374.7 0.2 reverse
  374.9 39.2 %psum.71 = f32[6,384]{1,0:T(8,128)S(1)} all-reduce(f32[6,384]{1,0:T(8,128)S(1)} %maximum_reduce_fusion), channel_id=1, replica_groups=mesh['win'=8,'head'=4] {'win','head'}, use_global_device_ids=true, to_apply=%region_25.26 | all-reduce | flops 2304 | bytes 18432 | tf_op jit(solution)/shard_map/psum | solution.py:527
  414.1 0.6 multiply_reduce_fusion.6
  414.7 0.7 multiply_reduce_fusion.5
  415.4 0.6 multiply_reduce_fusion.4
  416.0 1.2 multiply_reduce_fusion.7
  417.2 0.7 slice_bitcast_fusion.6
  417.8 6.8 %all-reduce.12.cloned.1.call-done = (f32[384,3,1,128]{0,3,1,2:T(8,128)}, f32[1,128,384]{2,1,0:T(8,128)}, f32[384,384]{0,1:T(8,128)}, f32[384,384]{0,1:T(8,128)}) async-done(((f32[384,3,1,128]{0,3,1,2:T(8,128)}, f32[1,128,384]{2,1,0:T(8,128)}, f32[384,384]{0,1:T(8,128)}, f32[384,384]{0,1:T(8,128)}), (f32[384,3,1,128]{0,3,1,2:T(8,128)}, f32[1,128,384]{2,1,0:T(8,128)}, f32[384,384]{0,1:T(8,128)}, ...) | async-done | bytes 1966096 | tf_op jit(solution)/shard_map/psum | solution.py:516
  424.6 1.9 multiply_reduce_fusion.1
  426.5 2.1 copy.113
  428.6 2.4 multiply_reduce_fusion.2
  431.1 2.2 multiply_reduce_fusion.3
  433.2 0.7 multiply_reduce_fusion
  438.5 1.1 copy.117
  439.6 12.5 %psum.70 = f32[]{:T(128)} all-reduce(f32[]{:T(128)S(6)} %add.187), channel_id=1, replica_groups=mesh['win'=8,'head'=4] {'head'}, use_global_device_ids=true, to_apply=%region_23.24 | all-reduce | flops 1 | bytes 8 | tf_op jit(solution)/shard_map/psum | solution.py:539
  453.4 3.6 multiply_subtract_fusion
  457.0 2.2 copy.114
  459.3 2.2 copy.115
  461.5 1.1 copy.116
  462.5 1.1 copy.118
  463.6 1.0 copy.119
  464.7 1.0 copy.120
  465.7 1.4 multiply_subtract_fusion.4
  467.1 1.3 multiply_subtract_fusion.6
  468.4 1.4 multiply_subtract_fusion.5
  469.8 0.8 multiply_subtract_fusion.3
  470.7 1.3 multiply_subtract_fusion.7
  472.0 1.3 multiply_subtract_fusion.2
  (91 shorter events, 0.7 us)
Async XLA Ops:
  7.2 4.1 copy-start.7
  7.2 5.0 %copy-start.11 = (f32[96,384]{1,0:T(8,128)S(1)}, f32[96,384]{1,0:T(8,128)}, u32[]{:S(2)}) copy-start(f32[96,384]{1,0:T(8,128)} %param.33) | copy-start | bytes 442372
  7.2 5.0 %copy-start.27 = (f32[225,4]{0,1:T(4,128)S(1)}, f32[225,4]{0,1:T(4,128)}, u32[]{:S(2)}) copy-start(f32[225,4]{0,1:T(4,128)} %param.32) | copy-start | bytes 10804
  7.2 20.4 %copy-start.28 = (f32[384]{0:T(512)S(1)}, f32[384]{0:T(512)}, u32[]{:S(2)}) copy-start(f32[384]{0:T(512)} %param.35) | copy-start | bytes 4612
  7.3 20.4 %copy-start.31 = (s32[32]{0:T(128)S(1)}, s32[32]{0:T(128)}, u32[]{:S(2)}) copy-start(s32[32]{0:T(128)} %param.29) | copy-start | bytes 388
  7.3 21.0 %copy-start.30 = (f32[2,96]{1,0:T(2,128)S(1)}, f32[2,96]{1,0:T(2,128)}, u32[]{:S(2)}) copy-start(f32[2,96]{1,0:T(2,128)} %param.31) | copy-start | bytes 2308
  7.3 62.2 %all-gather.6.cloned.1.call-start = ((), (), s32[]{:S(2)}) async-start(), calls=%async_computation.4 | async-start | bytes 1474560 | tf_op jit(solution)/shard_map/all_gather | solution.py:501
  9.4 68.8 %all-gather.10.cloned.1.call-start = ((), (), s32[]{:S(2)}) async-start(), calls=%async_computation.6 | async-start | bytes 1474560 | tf_op jit(solution)/shard_map/all_gather | solution.py:509
  11.3 98.7 %all-gather.8.cloned.1.call-start = ((), (), s32[]{:S(2)}) async-start(), calls=%async_computation.5 | async-start | bytes 1474560 | tf_op jit(solution)/shard_map/all_gather | solution.py:507
  12.1 229.2 %reduce-scatter.7.cloned.1.call-start = ((), (), s32[]{:S(2)}) async-start(), calls=%async_computation.8 | async-start | bytes 983040 | tf_op jit(solution)/shard_map/reduce_scatter | solution.py:517
  168.2 92.2 %reduce-scatter.5.cloned.1.call-start = ((), (), s32[]{:S(2)}) async-start(), calls=%async_computation.7 | async-start | bytes 2949120 | tf_op jit(solution)/shard_map/reduce_scatter | solution.py:517
  211.8 1.7 copy-start.6
  211.8 98.3 %reduce-scatter.9.cloned.1.call-start = ((), (), s32[]{:S(2)}) async-start(), calls=%async_computation.9 | async-start | bytes 2949120 | tf_op jit(solution)/shard_map/reduce_scatter | solution.py:517
  215.4 1.1 copy-start.8
  215.4 144.6 %reduce-scatter.11.cloned.1.call-start = ((), (), s32[]{:S(2)}) async-start(), calls=%async_computation.10 | async-start | bytes 2949120 | tf_op jit(solution)/shard_map/reduce_scatter | solution.py:517
  215.5 1.3 copy-start.32
  215.5 3.1 copy-start.14
  216.2 2.7 copy-start.15
  216.2 208.4 %all-reduce.12.cloned.1.call-start = ((), (), s32[]{:S(2)}) async-start(), calls=%async_computation.11 | async-start | bytes 3932160 | tf_op jit(solution)/shard_map/psum | solution.py:516
  216.5 2.6 copy-start.16
  218.7 3.8 copy-start.26
  219.1 3.2 copy-start.24
  219.2 3.2 copy-start.22
  219.2 155.7 %copy-start.23 = (f32[4,8,384]{2,1,0:T(8,128)S(1)}, f32[4,8,384]{2,1,0:T(8,128)}, u32[]{:S(2)}) copy-start(f32[4,8,384]{2,1,0:T(8,128)} %get-tuple-element.64) | copy-start | bytes 147460
  219.2 155.7 %copy-start.25 = (f32[2,8,384]{2,1,0:T(8,128)S(1)}, f32[2,8,384]{2,1,0:T(8,128)}, u32[]{:S(2)}) copy-start(f32[2,8,384]{2,1,0:T(8,128)} %get-tuple-element.63) | copy-start | bytes 73732
  374.6 50.0 %copy-start.29 = (f32[384]{0:T(512)}, f32[384]{0:T(512)S(1)}, u32[]{:S(2)}) copy-start(f32[384]{0:T(512)S(1)} %get-tuple-element.172) | copy-start | bytes 4612
  414.1 51.6 %copy-start.21 = (f32[6,384]{1,0:T(8,128)}, f32[6,384]{1,0:T(8,128)S(1)}, u32[]{:S(2)}) copy-start(f32[6,384]{1,0:T(8,128)S(1)} %psum.71) | copy-start | bytes 27652
  424.6 8.6 %copy-start.1 = (f32[384,384]{0,1:T(8,128)S(1)}, f32[384,384]{0,1:T(8,128)}, u32[]{:S(2)}) copy-start(f32[384,384]{0,1:T(8,128)} %get-tuple-element.176) | copy-start | bytes 1769476
  424.6 28.8 %copy-start = (f32[384,384]{0,1:T(8,128)S(1)}, f32[384,384]{0,1:T(8,128)}, u32[]{:S(2)}) copy-start(f32[384,384]{0,1:T(8,128)} %get-tuple-element.175) | copy-start | bytes 1769476
  457.0 4.4 copy-start.5
  457.0 5.5 %copy-start.4 = (f32[384,384]{0,1:T(8,128)S(1)}, f32[384,384]{0,1:T(8,128)}, u32[]{:S(2)}) copy-start(f32[384,384]{0,1:T(8,128)} %get-tuple-element.185) | copy-start | bytes 1769476
  457.0 6.6 %copy-start.3 = (f32[384,384]{0,1:T(8,128)S(1)}, f32[384,384]{0,1:T(8,128)}, u32[]{:S(2)}) copy-start(f32[384,384]{0,1:T(8,128)} %get-tuple-element.184) | copy-start | bytes 1769476
  459.3 5.4 %copy-start.2 = (f32[384,384]{0,1:T(8,128)S(1)}, f32[384,384]{0,1:T(8,128)}, u32[]{:S(2)}) copy-start(f32[384,384]{0,1:T(8,128)} %get-tuple-element.183) | copy-start | bytes 1769476
  461.5 8.4 %copy-start.12 = (f32[96,384]{1,0:T(8,128)S(1)}, f32[96,384]{1,0:T(8,128)}, u32[]{:S(2)}) copy-start(f32[96,384]{1,0:T(8,128)} %param.33) | copy-start | bytes 442372
  461.5 8.4 %copy-start.13 = (f32[96,384]{1,0:T(8,128)S(1)}, f32[96,384]{1,0:T(8,128)}, u32[]{:S(2)}) copy-start(f32[96,384]{1,0:T(8,128)} %get-tuple-element.205) | copy-start | bytes 442372
  461.5 8.4 %copy-start.19 = (f32[96,384]{1,0:T(8,128)S(1)}, f32[96,384]{1,0:T(8,128)}, u32[]{:S(2)}) copy-start(f32[96,384]{1,0:T(8,128)} %param.45) | copy-start | bytes 442372
  462.5 9.5 %copy-start.9 = (f32[384,3,96]{0,2,1:T(8,128)S(1)}, f32[384,3,96]{0,2,1:T(8,128)}, u32[]{:S(2)}) copy-start(f32[384,3,96]{0,2,1:T(8,128)} %get-tuple-element.209) | copy-start | bytes 1327108
  462.5 9.5 %copy-start.10 = (f32[384,3,96]{0,2,1:T(8,128)S(1)}, f32[384,3,96]{0,2,1:T(8,128)}, u32[]{:S(2)}) copy-start(f32[384,3,96]{0,2,1:T(8,128)} %param.30) | copy-start | bytes 1327108
  462.5 9.5 %copy-start.17 = (f32[384,3,96]{0,2,1:T(8,128)S(1)}, f32[384,3,96]{0,2,1:T(8,128)}, u32[]{:S(2)}) copy-start(f32[384,3,96]{0,2,1:T(8,128)} %param.39) | copy-start | bytes 1327108
  463.6 6.2 %copy-start.20 = (f32[96,384]{1,0:T(8,128)S(1)}, f32[96,384]{1,0:T(8,128)}, u32[]{:S(2)}) copy-start(f32[96,384]{1,0:T(8,128)} %param.44) | copy-start | bytes 442372
  463.6 8.4 %copy-start.18 = (f32[384,3,96]{0,2,1:T(8,128)S(1)}, f32[384,3,96]{0,2,1:T(8,128)}, u32[]{:S(2)}) copy-start(f32[384,3,96]{0,2,1:T(8,128)} %param.38) | copy-start | bytes 1327108
Sparse Core Ops, SparseCore 0:
  10.3 33.3 all-gather.5
  45.8 32.4 all-gather.9
  80.4 29.5 all-gather.7
  168.3 22.7 reduce-scatter.6
  211.9 48.3 reduce-scatter.4
  262.5 47.5 reduce-scatter.8
  312.4 47.5 reduce-scatter.10
  363.6 60.9 all-reduce.11

commit v2 on v1

--- a/solution.py
+++ b/solution.py
@@ -146,9 +146,8 @@
     for g in range(GROUPS):
         total = None
         for h in range(PER):
-            head = g * PER + h
             own = jnp.where((row == base) & (lane // SPOT == h), 1.0, 0.0).astype(F32).astype(BF16)
-            line = jnp.broadcast_to(table_ref[head : head + 1, :], (8, 256))
+            line = jnp.broadcast_to(table_ref[g, 1 + h : 2 + h, :256], (8, 256))
             spread = jnp.concatenate(
                 [
                     pltpu.roll(line, (15 * a + 144) % 256, axis=1, stride=1, stride_axis=0)
@@ -174,17 +173,108 @@
     return jnp.where(u >= 0.0, 1.0 - tail, tail), bell * 0.3989422804014327
 
 
+def place(win, head):
+    return {"win": win, "head": head}
+
+
+def remote(src, dst, send, recv, win, head):
+    return pltpu.make_async_remote_copy(
+        src_ref=src,
+        dst_ref=dst,
+        send_sem=send,
+        recv_sem=recv,
+        device_id=place(win, head),
+        device_id_type=pl.DeviceIdType.MESH,
+    )
+
+
+def position():
+    win, head = lax.axis_index("win"), lax.axis_index("head")
+    core, cell = win % 2, (win // 2) % 4
+    return win, head, core, cell, win - core - 2 * cell
+
+
+def greet():
+    win, head, core, cell, base = position()
+    barrier = pltpu.get_barrier_semaphore()
+    peers = [(win, (head + d) % 4) for d in (1, 2, 3)]
+    peers += [(base + 2 * ((cell + d) % 4) + core, head) for d in (1, 2, 3)]
+    peers += [(win + 1 - 2 * core, head)]
+    for w, h in peers:
+        pl.semaphore_signal(barrier, inc=1, device_id=place(w, h), device_id_type=pl.DeviceIdType.MESH)
+    pl.semaphore_wait(barrier, len(peers))
+
+
+def shard_view(ref, wide, head, start, count):
+    if wide:
+        return ref.at[pl.ds(start, count), pl.ds(pl.multiple_of(head * D, LANES), D)]
+    rows = ref.shape[0] // 4
+    return ref.at[pl.ds(pl.multiple_of(head * rows + start, 16), count), :]
+
+
+def gather_stages(own, full, wide, sems):
+    win, head, core, cell, base = position()
+    rows = own.shape[0]
+    half, part = rows // 2, rows // 8
+    mine = pl.multiple_of(core * half + cell * part, 16)
+    near = pl.multiple_of(core * half, 16)
+
+    def over_head(d):
+        view = shard_view(full, wide, head, mine, part)
+        return remote(
+            own.at[pl.ds(mine, part), :], view, sems.at[0, d], sems.at[1, d], win, (head + d + 1) % 4
+        )
+
+    def over_cell(d, c):
+        view = shard_view(full, wide, (head + 3 - d) % 4, mine, part)
+        peer = base + 2 * ((cell + c + 1) % 4) + core
+        return remote(view, view, sems.at[2 + c, d], sems.at[5 + c, d], peer, head)
+
+    def over_core(d):
+        view = shard_view(full, wide, (head + 3 - d) % 4, near, half)
+        return remote(view, view, sems.at[8, d], sems.at[9, d], win + 1 - 2 * core, head)
+
+    local = pltpu.make_async_copy(own, shard_view(full, wide, head, 0, rows), sems.at[10, 0])
+
+    def first():
+        local.start()
+        for d in range(3):
+            over_head(d).start()
+
+    def second():
+        for d in range(3):
+            over_head(d).wait_recv()
+            for c in range(3):
+                over_cell(d, c).start()
+
+    def third():
+        for d in range(3):
+            for c in range(3):
+                over_cell(d, c).wait_recv()
+            over_core(d).start()
+
+    def last():
+        for d in range(3):
+            over_core(d).wait_recv()
+        local.wait()
+        for d in range(3):
+            over_head(d).wait_send()
+            for c in range(3):
+                over_cell(d, c).wait_send()
+            over_core(d).wait_send()
+
+    return first, second, third, last
+
+
 def front_kernel(
     frames_ref,
     tok_ref,
     og_ref,
-    wqkv_ref,
-    bqv_ref,
-    table_ref,
-    wproj_ref,
-    w1_ref,
-    b1_ref,
-    w2_ref,
+    qown_ref,
+    pown_ref,
+    aown_ref,
+    bown_ref,
+    sown_ref,
     rowp_ref,
     out_ref,
     qkv_ref,
@@ -196,15 +286,59 @@
     gp_ref,
     rows_ref,
     gb_ref,
+    wout_ref,
     bias_ref,
     time_ref,
     att_ref,
+    wqkv_ref,
+    wproj_ref,
+    w1_ref,
+    w2_ref,
+    small_ref,
+    bqkv_ref,
+    b1_ref,
+    wsems,
+    ssems,
 ):
     step = pl.program_id(0)
 
     @pl.when(step == 0)
     def _():
-        build_bias(table_ref, bias_ref)
+        greet()
+        win, head = lax.axis_index("win"), lax.axis_index("head")
+        stages = [
+            gather_stages(own, full, wide, wsems.at[i])
+            for i, (own, full, wide) in enumerate(
+                (
+                    (qown_ref, wqkv_ref, True),
+                    (pown_ref, wproj_ref, False),
+                    (aown_ref, w1_ref, True),
+                    (bown_ref, w2_ref, False),
+                )
+            )
+        ]
+        small = [
+            remote(
+                sown_ref, small_ref.at[head], ssems.at[0, d], ssems.at[1, d], win, (head + d + 1) % 4
+            )
+            for d in range(3)
+        ]
+        own_small = pltpu.make_async_copy(sown_ref, small_ref.at[head], ssems.at[2, 0])
+        own_small.start()
+        for copy in small:
+            copy.start()
+        for k in range(4):
+            for stage in stages:
+                stage[k]()
+        own_small.wait()
+        for copy in small:
+            copy.wait()
+        for g in range(4):
+            bqkv_ref[0:1, g * D : g * D + LANES] = small_ref[g, 0:1, :LANES]
+            bqkv_ref[0:1, g * D + LANES : g * D + 2 * LANES] = jnp.zeros((1, LANES), F32)
+            bqkv_ref[0:1, g * D + 2 * LANES : g * D + D] = small_ref[g, 0:1, LANES : 2 * LANES]
+            b1_ref[0:1, g * D : g * D + D] = small_ref[g, 5:6, :]
+        build_bias(small_ref, bias_ref)
         for wt in range(2):
             for wf in range(2):
                 time_ref[wt * 2 + wf] = key_times(wt, wf)
@@ -218,19 +352,15 @@
     n1 = (n1 * rowp_ref[0:1] + rowp_ref[1:2]).astype(BF16)
     for part in range(3):
         cols = slice(part * 512, part * 512 + 512)
-        y = nn(n1, wqkv_ref[:, cols])
-        if part == 0:
-            y = y + bqv_ref[0:1]
-        if part == 2:
-            y = y + bqv_ref[1:2]
+        y = nn(n1, wqkv_ref[:, cols]) + bqkv_ref[0:1, cols]
         qkv_ref[:, cols] = y.astype(BF16)
     masks = head_masks(BF16)
     for w in range(4):
         rows = slice(w * SPOT, w * SPOT + SPOT)
         for g in range(GROUPS):
-            q = qkv_ref[rows, g * LANES : g * LANES + LANES]
-            k = qkv_ref[rows, 512 + g * LANES : 512 + g * LANES + LANES]
-            v = qkv_ref[rows, 1024 + g * LANES : 1024 + g * LANES + LANES]
+            q = qkv_ref[rows, g * D : g * D + LANES]
+            k = qkv_ref[rows, g * D + LANES : g * D + 2 * LANES]
+            v = qkv_ref[rows, g * D + 2 * LANES : g * D + D]
             s = nt(k, stack_heads(q, masks)) * SCALE + bias_ref[g]
             s = jnp.where(time_ref[w] < frames, s, MASKED)
             e = jnp.exp(s - jnp.max(s, axis=0, keepdims=True))
@@ -272,6 +402,10 @@
     gp_ref[...] += tn(att, dbr)
     datt_ref[...] = nt(dbr, wproj_ref[...]).astype(BF16)
 
+    @pl.when(step == pl.num_programs(0) - 1)
+    def _():
+        wout_ref[...] = wqkv_ref[...]
+
 
 def back_kernel(
     frames_ref,
@@ -307,13 +441,13 @@
         tacc = None
         for w in range(4):
             rows = slice(w * SPOT, w * SPOT + SPOT)
-            cq = slice(g * LANES, g * LANES + LANES)
-            ck = slice(512 + g * LANES, 512 + g * LANES + LANES)
-            cv = slice(1024 + g * LANES, 1024 + g * LANES + LANES)
+            cq = slice(g * D, g * D + LANES)
+            ck = slice(g * D + LANES, g * D + 2 * LANES)
+            cv = slice(g * D + 2 * LANES, g * D + D)
             q = qkv_ref[rows, cq]
             k = qkv_ref[rows, ck]
             v = qkv_ref[rows, cv]
-            do = stack_heads(datt_ref[rows, cq], masks)
+            do = stack_heads(datt_ref[rows, g * LANES : g * LANES + LANES], masks)
             p = probs_ref[0, w, g]
             pf = p.astype(F32)
             dp = nt(v, do)
@@ -328,8 +462,7 @@
     n, inv = normalize(to_windows(tok_ref[...].astype(F32)))
     n1t = (n * rowp_ref[0:1] + rowp_ref[1:2]).astype(BF16).T
     dj = dj_ref[...]
-    gqv_ref[:, :512] += fold(dj[:, :512].astype(F32))
-    gqv_ref[:, 512:] += fold(dj[:, 1024:].astype(F32))
+    gqv_ref[...] += fold(dj.astype(F32))
     dn1 = nt(dj, wqkv_ref[...])
     gq_ref[...] += nn(n1t, dj)
     rows_ref[0] += fold(dn1 * n)
@@ -364,17 +497,18 @@
     return pl.BlockSpec(shape, lambda i: (0,) * len(shape))
 
 
-def front(frames, tok, og, wqkv, bqv, table, wproj, w1, b1, w2, rowp):
+def front(frames, tok, og, qown, pown, aown, bown, sown, rowp):
     rows = tok.shape[0]
     clips = rows // CLIP
     line = lambda width: pl.BlockSpec((CLIP, width), lambda i: (i, 0))
     probs = (1, 4, GROUPS, SPOT, PER * SPOT)
     shape = jax.ShapeDtypeStruct
+    sems = pltpu.SemaphoreType.DMA
     return pl.pallas_call(
         front_kernel,
         grid=(clips,),
         in_specs=[pl.BlockSpec(memory_space=pltpu.SMEM), line(D), line(D)]
-        + [whole(a.shape) for a in (wqkv, bqv, table, wproj, w1, b1, w2, rowp)],
+        + [whole(a.shape) for a in (qown, pown, aown, bown, sown, rowp)],
         out_specs=[
             line(D),
             line(1536),
@@ -386,6 +520,7 @@
             whole((512, D)),
             whole((4, 8, D)),
             whole((8, FF)),
+            whole((D, 1536)),
         ],
         out_shape=[
             shape((rows, D), F32),
@@ -398,14 +533,26 @@
             shape((512, D), F32),
             shape((4, 8, D), F32),
             shape((8, FF), F32),
+            shape((D, 1536), BF16),
         ],
         scratch_shapes=[
             pltpu.VMEM((GROUPS, SPOT, PER * SPOT), F32),
             pltpu.VMEM((4, SPOT, PER * SPOT), jnp.int32),
             pltpu.VMEM((CLIP, 512), BF16),
+            pltpu.VMEM((D, 1536), BF16),
+            pltpu.VMEM((512, D), BF16),
+            pltpu.VMEM((D, FF), BF16),
+            pltpu.VMEM((FF, D), BF16),
+            pltpu.VMEM((GROUPS, 8, D), F32),
+            pltpu.VMEM((8, 1536), F32),
+            pltpu.VMEM((8, FF), F32),
+            sems((4, 11, 3)),
+            sems((3, 3)),
         ],
-        compiler_params=pltpu.CompilerParams(vmem_limit_bytes=VMEM_LIMIT),
-    )(frames, tok, og, wqkv, bqv, table, wproj, w1, b1, w2, rowp)
+        compiler_params=pltpu.CompilerParams(
+            vmem_limit_bytes=VMEM_LIMIT, collective_id=0, has_side_effects=True
+        ),
+    )(frames, tok, og, qown, pown, aown, bown, sown, rowp)
 
 
 def back(frames, tok, qkv, probs, datt, dmid, wqkv, rowp):
@@ -430,14 +577,14 @@
             line(D),
             whole((D, 1536)),
             whole((2, 8, D)),
-            whole((8, 1024)),
+            whole((8, 1536)),
             whole((HEADS, 256)),
         ],
         out_shape=[
             shape((rows, D), F32),
             shape((D, 1536), F32),
             shape((2, 8, D), F32),
-            shape((8, 1024), F32),
+            shape((8, 1536), F32),
             shape((HEADS, 256), F32),
         ],
         scratch_shapes=[
@@ -490,25 +637,25 @@
     rows_first,
     rows_second,
 ):
-    gather = partial(lax.all_gather, axis_name="head", tiled=True)
     clips = tokens.shape[0] // CLIP
-    parts = lax.axis_size("head")
     local = rel_table.shape[1] * HDIM
-    groups = rel_table.shape[1] // PER
+    offsets = rel_table.shape[0]
     frames = lax.dynamic_slice(clip_frames, (lax.axis_index("head") * clips,), (clips,))
-    pad = LANES - PER * HDIM
-    wqkv = qkv_weight.astype(BF16).reshape(D, 3, groups, PER * HDIM)
-    wqkv = gather(jnp.pad(wqkv, ((0, 0), (0, 0), (0, 0), (0, pad))), axis=2).reshape(D, 1536)
-    bqv = jnp.pad(qv_bias.reshape(2, groups, PER * HDIM), ((0, 0), (0, 0), (0, pad)))
-    bqv = gather(bqv, axis=1).reshape(2, 512)
-    table = gather(jnp.pad(rel_table.T, ((0, 0), (0, 256 - rel_table.shape[0]))), axis=0)
-    wproj = proj_weight.astype(BF16).reshape(groups, PER * HDIM, D)
-    wproj = gather(jnp.pad(wproj, ((0, 0), (0, pad), (0, 0))), axis=0).reshape(512, D)
-    w1 = gather(fc1_weight.astype(BF16), axis=1)
-    b1 = gather(fc1_bias, axis=0).reshape(1, FF)
-    w2 = gather(fc2_weight.astype(BF16), axis=0)
-    output, qkv, probs, datt, dmid, g1, g2, gp, rows_f, gb = front(
-        frames, tokens, out_grad, wqkv, bqv, table, wproj, w1, b1, w2, row_params
+    pad = LANES - local
+    qown = jnp.pad(qkv_weight.astype(BF16), ((0, 0), (0, 0), (0, pad))).reshape(D, D)
+    pown = jnp.pad(proj_weight.astype(BF16), ((0, pad), (0, 0)))
+    aown, bown = fc1_weight.astype(BF16), fc2_weight.astype(BF16)
+    bias_row = jnp.pad(qv_bias, ((0, 1), (0, pad))).reshape(1, D)
+    sown = jnp.concatenate(
+        [
+            bias_row,
+            jnp.pad(rel_table.T, ((0, 0), (0, D - offsets))),
+            fc1_bias[None],
+            jnp.zeros((2, D), F32),
+        ]
+    )
+    output, qkv, probs, datt, dmid, g1, g2, gp, rows_f, gb, wqkv = front(
+        frames, tokens, out_grad, qown, pown, aown, bown, sown, row_params
     )
     input_grad, gq, rows_b, gqv, gt = back(
         frames, tokens, qkv, probs, datt, dmid, wqkv, row_params
@@ -516,10 +663,9 @@
     scatter = lambda v, dim: lax.psum(
         lax.psum_scatter(v, "head", scatter_dimension=dim, tiled=True), "win"
     )
-    qkv_summed = scatter(gq.reshape(D, 3, GROUPS, LANES), 2)[..., : PER * HDIM].reshape(D, 3, local)
-    gqv = jnp.sum(gqv, axis=0).reshape(2, GROUPS, LANES)
-    qvb_summed = scatter(gqv, 1)[..., : PER * HDIM].reshape(2, local)
-    table_summed = scatter(gt, 0)[:, : rel_table.shape[0]][:, ::-1].T
+    qkv_summed = scatter(gq, 1).reshape(D, 3, LANES)[..., :local]
+    qvb_summed = scatter(jnp.sum(gqv, axis=0), 0).reshape(3, LANES)[::2, :local]
+    table_summed = scatter(gt, 0)[:, : offsets][:, ::-1].T
     proj_summed = scatter(gp.reshape(GROUPS, LANES, D), 0)[:, : PER * HDIM].reshape(local, D)
     fc1_summed = scatter(g1, 1)
     fc1b_summed = scatter(jnp.sum(gb, axis=0), 0)

time: 482 us -> 449 us (0.932)
  blocking collectives: 141 us -> 78.8 us
  Pallas kernels: 96.2 us -> 128 us
  local copies, waits for them, and re-layouts: 33.8 us -> 27.1 us
    all_gather x4 -> x0, blocking collectives: 56.1 us -> none  [the longest x1 17.4 us: shards(): gather(jnp.pad(wproj, ((0, 0), (0, pad), (0, 0))), axis=0).reshape(512, D)]
    reduce_scatter x4, waiting for transfers between devices: 119 us -> 165 us  [shards(): lax.psum_scatter(v, 'head', scatter_dimension=dim, tiled=True)]
    all_gather x3 -> x0, waiting for transfers between devices: 37 us -> none  [the longest x1 31.8 us: shards(): w1 = gather(fc1_weight.astype(BF16), axis=1)]
    pallas_call x1, Pallas kernels: 58.1 us -> 89.1 us  [front(): pl.pallas_call(front_kernel, grid=(clips,), in_specs=[pl.BlockSpec(memory...]
    psum x1, waiting for transfers between devices: 6.78 us -> 0.01 us  [shards(): lax.psum(lax.psum_scatter(v, 'head', scatter_dimension=dim, tiled=True),...]
    reshape x4 -> x2, local copies, waits for them, and re-layouts: 6.57 us -> 0.97 us  [the longest x1 0.9 us: shards(): jnp.pad(qkv_weight.astype(BF16), ((0, 0), (0, 0), (0, pad))).reshape(D, D)]
  transfers between devices with their start and end apart: 8 -> 5, of which waited for: 6 -> 4; matrix products, arithmetic and copies ran while one was open for 5% -> 3% of each run, Pallas kernels for 8% -> 0%
where the time goes in v2:
time: 449 us; the launch traced here: 448 us
  waiting for transfers between devices  166 us (37%)
  Pallas kernels  128 us (29%)
  blocking collectives  78.8 us (18%)
  local copies, waits for them, and re-layouts  27.1 us (6%)
  other arithmetic  26.1 us (6%)
  between operations  22.5 us (5%)
    reduce_scatter x4, waiting for transfers between devices, shards(): lax.psum_scatter(v, 'head', scatter_dimension=dim, tiled=True)  165 us
    pallas_call x1, Pallas kernels, front(): pl.pallas_call(front_kernel, grid=(clips,), in_specs=[pl.BlockSpec(memory...  89.1 us
    pallas_call x1, Pallas kernels, back(): pl.pallas_call(back_kernel, grid=(clips,), in_specs=[pl.BlockSpec(memory_...  38.5 us
    psum x1, blocking collectives, shards(): lax.psum(jnp.sum(jnp.concatenate([rows_b, rows_f]), axis=1), ('win', 'hea...  37.6 us
    unnamed x89, local copies, waits for them, and re-layouts  19.4 us
    unnamed x1, blocking collectives  17.3 us
    psum x1, blocking collectives, shards(): lax.psum(lax.psum_scatter(v, 'head', scatter_dimension=dim, tiled=True),...  12.8 us
    sub x7, other arithmetic, adam_step(): weight - rate * (moment_hat / (jnp.sqrt(second_hat) + ADAM_EPS) + WEIGHT_...  11.3 us
  transfers between devices with their start and end apart: 5, of which 4 were waited for; matrix products, arithmetic and copies ran while one was open for 3% of the time, Pallas kernels for 0%

profile of v2, /device:TPU:0, one launch (start us, length us, event | category | flops | bytes accessed | tf_op | source)
XLA Modules:
  0.0 448.3 jit_solution(6589123877760772619)
XLA Ops:
  7.3 0.0 reduce-scatter.5.cloned.1.call-start
  7.3 1.1 convert_element_type.20
  8.5 0.9 copy.100.qown_ref
  9.4 1.8 convert_element_type.22.aown_ref
  11.2 0.7 convert_element_type.23.bown_ref
  11.9 0.7 pad.17.pown_ref
  12.6 0.6 dynamic_slice.3.frames_ref
  13.2 0.1 pad.25.clone
  13.3 0.7 fusion.6.sown_ref
  14.0 89.1 %shard_map.530 = (f32[2048,384]{1,0:T(8,128)}, bf16[2048,1536]{1,0:T(8,128)(2,1)}, bf16[8,4,4,64,256]{4,3,2,1,0:T(8,128)(2,1)}, bf16[2048,512]{1,0:T(8,128)(2,1)...) custom-call(s32[8]{0:T(128)} %dynamic_slice.3.frames_ref, ...), custom_call_target="tpu_custom_call" | custom-call | tf_op jit(solution)/shard_map/pallas_call | solution.py:507
  103.1 38.5 %shard_map.531 = (f32[2048,384]{1,0:T(8,128)}, f32[384,1536]{1,0:T(8,128)}, f32[2,8,384]{2,1,0:T(8,128)}, f32[8,1536]{1,0:T(8,128)}, f32[16,256]{1,0:T(8,128)}) custom-call(s32[8]{0:T(128)} %dynamic_slice.3.frames_ref, bf16[2048,384]{1,0:T(8,128)(2,1)} %tok_ref.3, bf16[2048,1536]{1,0:T(8,128)(2,1)} %get-tuple-element.52.qkv_ref, ...), custom_call_target="tpu_custom_call" | custom-call | tf_op jit(solution)/shard_map/pallas_call | solution.py:563
  141.7 0.0 reduce-scatter.7.cloned.1.call-start
  141.7 0.7 reduce-scatter.7.cloned.1.call-update
  142.4 0.0 reduce-scatter.9.cloned.1.call-start
  142.5 0.8 copy-done.7
  143.3 2.0 copy.102
  145.3 0.0 reduce-scatter.11.cloned.1.call-start
  145.3 0.5 reduce-scatter.11.cloned.1.call-update
  145.9 0.0 all-reduce.12.cloned.1.call-start
  145.9 42.3 %reduce-scatter.5.cloned.1.call-done = f32[384,384]{1,0:T(8,128)} async-done(((f32[384,1536]{1,0:T(8,128)}), f32[384,384]{1,0:T(8,128)}) %reduce-scatter.5.cloned.1.call-update) | async-done | bytes 589840 | tf_op jit(solution)/shard_map/reduce_scatter | solution.py:664
  188.2 2.1 copy.101
  190.3 23.0 %reduce-scatter.7.cloned.1.call-done = f32[1,128,384]{2,1,0:T(8,128)} async-done(((f32[4,128,384]{2,1,0:T(8,128)}), f32[1,128,384]{2,1,0:T(8,128)}) %reduce-scatter.7.cloned.1.call-update) | async-done | bytes 196624 | tf_op jit(solution)/shard_map/reduce_scatter | solution.py:664
  213.3 49.7 %reduce-scatter.9.cloned.1.call-done = f32[384,384]{0,1:T(8,128)} async-done(((f32[384,1536]{0,1:T(8,128)}), f32[384,384]{0,1:T(8,128)}) %reduce-scatter.9.cloned.1.call-update) | async-done | bytes 589840 | tf_op jit(solution)/shard_map/reduce_scatter | solution.py:664
  263.0 49.7 %reduce-scatter.11.cloned.1.call-done = f32[384,384]{1,0:T(8,128)} async-done(((f32[384,1536]{1,0:T(8,128)}), f32[384,384]{1,0:T(8,128)}) %reduce-scatter.11.cloned.1.call-update) | async-done | bytes 589840 | tf_op jit(solution)/shard_map/reduce_scatter | solution.py:664
  312.7 0.2 copy.106
  313.0 0.2 copy.110
  313.3 0.6 dynamic-slice
  315.2 17.3 %all-reduce.9 = (f32[1536]{0:T(1024)S(1)}, f32[16,256]{1,0:T(8,128)S(1)}, f32[1536]{0:T(1024)S(1)}) all-reduce(f32[1536]{0:T(1024)S(1)} %reduce_sum.100, f32[16,256]{1,0:T(8,128)S(1)} %copy-done.28, f32[1536]{0:T(1024)S(1)} %reduce_sum.105), channel_id=3, replica_groups=mesh['win'=8,'head'=4] {'head'}, use_global_device_ids=true, to_apply=%region_4.5.clone | all-reduce | flops 7168 | bytes 57344
  332.5 0.1 dynamic-slice.5
  332.6 0.1 dynamic-slice_bitcast_fusion
  332.7 12.8 %all-reduce.7 = (f32[3,128]{1,0:T(4,128)S(1)}, f32[4,256]{1,0:T(4,128)S(1)}, f32[384]{0:T(512)}) all-reduce(f32[3,128]{1,0:T(4,128)S(1)} %dynamic-slice_bitcast_fusion, f32[4,256]{1,0:T(4,128)S(1)} %constant_dynamic-slice_fusion, f32[384]{0:T(512)S(1)} %dynamic-slice.5), channel_id=1, replica_groups=mesh['win'=8,'head'=4] {'win'}, use_global_device_ids=true, to_apply=%region_5.6 | all-reduce | flops 1792 | bytes 14336 | tf_op jit(solution)/shard_map/psum | solution.py:663
  345.4 0.2 reverse
  345.6 0.6 slice.13
  346.2 0.2 copy.103
  346.5 0.2 copy.104
  346.7 2.1 copy.107
  348.9 1.0 copy.108
  349.9 37.6 %psum.71 = f32[6,384]{1,0:T(8,128)S(1)} all-reduce(f32[6,384]{1,0:T(8,128)S(1)} %maximum_reduce_fusion), channel_id=1, replica_groups=mesh['win'=8,'head'=4] {'win','head'}, use_global_device_ids=true, to_apply=%region_25.26 | all-reduce | flops 2304 | bytes 18432 | tf_op jit(solution)/shard_map/psum | solution.py:673
  387.6 0.6 multiply_reduce_fusion.7
  388.2 1.3 multiply_reduce_fusion.6
  389.5 0.7 multiply_reduce_fusion.5
  390.1 0.6 multiply_reduce_fusion.4
  390.7 0.7 slice_bitcast_fusion.2
  391.4 1.9 multiply_reduce_fusion.1
  393.3 2.1 copy.111
  395.4 2.4 multiply_reduce_fusion.2
  397.9 2.2 multiply_reduce_fusion.3
  400.0 0.7 multiply_reduce_fusion
  405.3 1.1 copy.115
  406.4 11.1 %psum.70 = f32[]{:T(128)} all-reduce(f32[]{:T(128)S(6)} %add.187), channel_id=1, replica_groups=mesh['win'=8,'head'=4] {'head'}, use_global_device_ids=true, to_apply=%region_23.24 | all-reduce | flops 1 | bytes 8 | tf_op jit(solution)/shard_map/psum | solution.py:685
  418.9 3.6 multiply_subtract_fusion
  422.5 2.2 copy.112
  424.8 2.2 copy.113
  427.0 1.1 copy.114
  428.0 1.1 copy.116
  429.1 1.0 copy.117
  430.2 1.0 copy.118
  431.2 1.5 multiply_subtract_fusion.4
  432.7 1.3 multiply_subtract_fusion.6
  434.1 1.4 multiply_subtract_fusion.5
  435.5 1.3 multiply_subtract_fusion.7
  436.8 0.8 multiply_subtract_fusion.3
  437.7 1.3 multiply_subtract_fusion.2
  438.9 1.7 copy.127
  (81 shorter events, 0.3 us)
Async XLA Ops:
  7.2 4.0 copy-start.9
  7.2 4.7 %copy-start.12 = (f32[96,384]{1,0:T(8,128)S(1)}, f32[96,384]{1,0:T(8,128)}, u32[]{:S(2)}) copy-start(f32[96,384]{1,0:T(8,128)} %param.33) | copy-start | bytes 442372
  7.2 5.4 %copy-start.30 = (f32[2,96]{1,0:T(2,128)S(1)}, f32[2,96]{1,0:T(2,128)}, u32[]{:S(2)}) copy-start(f32[2,96]{1,0:T(2,128)} %param.31) | copy-start | bytes 2308
  7.2 5.4 %copy-start.29 = (f32[384]{0:T(512)S(1)}, f32[384]{0:T(512)}, u32[]{:S(2)}) copy-start(f32[384]{0:T(512)} %param.35) | copy-start | bytes 4612
  7.3 5.4 %copy-start.32 = (s32[32]{0:T(128)S(1)}, s32[32]{0:T(128)}, u32[]{:S(2)}) copy-start(s32[32]{0:T(128)} %param.29) | copy-start | bytes 388
  7.3 6.0 %copy-start.27 = (f32[225,4]{0,1:T(4,128)S(1)}, f32[225,4]{0,1:T(4,128)}, u32[]{:S(2)}) copy-start(f32[225,4]{0,1:T(4,128)} %param.32) | copy-start | bytes 10804
  7.3 180.9 %reduce-scatter.5.cloned.1.call-start = ((), (), s32[]{:S(2)}) async-start(), calls=%async_computation.4 | async-start | bytes 2949120 | tf_op jit(solution)/shard_map/reduce_scatter | solution.py:664
  141.6 1.7 copy-start.7
  141.7 71.7 %reduce-scatter.7.cloned.1.call-start = ((), (), s32[]{:S(2)}) async-start(), calls=%async_computation.5 | async-start | bytes 983040 | tf_op jit(solution)/shard_map/reduce_scatter | solution.py:664
  142.4 120.6 %reduce-scatter.9.cloned.1.call-start = ((), (), s32[]{:S(2)}) async-start(), calls=%async_computation.6 | async-start | bytes 2949120 | tf_op jit(solution)/shard_map/reduce_scatter | solution.py:664
  145.3 167.4 %reduce-scatter.11.cloned.1.call-start = ((), (), s32[]{:S(2)}) async-start(), calls=%async_computation.7 | async-start | bytes 2949120 | tf_op jit(solution)/shard_map/reduce_scatter | solution.py:664
  145.3 167.4 %copy-start.8 = (f32[384,384]{1,0:T(8,128)S(1)}, f32[384,384]{1,0:T(8,128)}, u32[]{:S(2)}) copy-start(f32[384,384]{1,0:T(8,128)} %param.34) | copy-start | bytes 1769476
  145.9 245.6 %all-reduce.12.cloned.1.call-start = ((), (), s32[]{:S(2)}) async-start(), calls=%async_computation.8 | async-start | bytes 3932160 | tf_op jit(solution)/shard_map/psum | solution.py:663
  190.3 122.9 %copy-start.24 = (f32[8,1536]{1,0:T(8,128)S(1)}, f32[8,1536]{1,0:T(8,128)}, u32[]{:S(2)}) copy-start(f32[8,1536]{1,0:T(8,128)} %get-tuple-element.59) | copy-start | bytes 147460
  190.3 123.0 %copy-start.23 = (f32[8,1536]{1,0:T(8,128)S(1)}, f32[8,1536]{1,0:T(8,128)}, u32[]{:S(2)}) copy-start(f32[8,1536]{1,0:T(8,128)} %get-tuple-element.63) | copy-start | bytes 147460
  190.3 123.0 %copy-start.33 = (u32[32]{0:T(128)S(1)}, u32[32]{0:T(128)}, u32[]{:S(2)}) copy-start(u32[32]{0:T(128)} %constant.46) | copy-start | bytes 388
  190.3 124.9 %copy-start.28 = (f32[16,256]{1,0:T(8,128)S(1)}, f32[16,256]{1,0:T(8,128)}, u32[]{:S(2)}) copy-start(f32[16,256]{1,0:T(8,128)} %get-tuple-element.60) | copy-start | bytes 49156
  190.3 155.9 %copy-start.15 = (f32[384,384]{1,0:T(8,128)S(1)}, f32[384,384]{1,0:T(8,128)}, u32[]{:S(2)}) copy-start(f32[384,384]{1,0:T(8,128)} %param.46) | copy-start | bytes 1769476
  312.7 33.7 %copy-start.16 = (f32[384,384]{1,0:T(8,128)S(1)}, f32[384,384]{1,0:T(8,128)}, u32[]{:S(2)}) copy-start(f32[384,384]{1,0:T(8,128)} %param.47) | copy-start | bytes 1769476
  313.2 35.6 %copy-start.17 = (f32[384,384]{1,0:T(8,128)S(1)}, f32[384,384]{1,0:T(8,128)}, u32[]{:S(2)}) copy-start(f32[384,384]{1,0:T(8,128)} %param.51) | copy-start | bytes 1769476
  346.7 3.2 copy-start.25
  346.7 3.2 copy-start.26
  346.7 40.9 %copy-start.31 = (f32[2,96]{1,0:T(2,128)S(1)}, f32[2,96]{1,0:T(2,128)}, u32[]{:S(2)}) copy-start(f32[2,96]{1,0:T(2,128)} %slice.13) | copy-start | bytes 2308
  387.6 43.6 %copy-start.22 = (f32[6,384]{1,0:T(8,128)}, f32[6,384]{1,0:T(8,128)S(1)}, u32[]{:S(2)}) copy-start(f32[6,384]{1,0:T(8,128)S(1)} %psum.71) | copy-start | bytes 27652
  391.4 8.6 %copy-start.1 = (f32[384,384]{0,1:T(8,128)S(1)}, f32[384,384]{0,1:T(8,128)}, u32[]{:S(2)}) copy-start(f32[384,384]{0,1:T(8,128)} %get-tuple-element.178) | copy-start | bytes 1769476
  391.4 27.5 %copy-start = (f32[384,384]{0,1:T(8,128)S(1)}, f32[384,384]{0,1:T(8,128)}, u32[]{:S(2)}) copy-start(f32[384,384]{0,1:T(8,128)} %get-tuple-element.177) | copy-start | bytes 1769476
  422.5 4.4 copy-start.6
  422.5 5.5 %copy-start.5 = (f32[384,384]{0,1:T(8,128)S(1)}, f32[384,384]{0,1:T(8,128)}, u32[]{:S(2)}) copy-start(f32[384,384]{0,1:T(8,128)} %get-tuple-element.187) | copy-start | bytes 1769476
  422.5 6.6 %copy-start.4 = (f32[384,384]{0,1:T(8,128)S(1)}, f32[384,384]{0,1:T(8,128)}, u32[]{:S(2)}) copy-start(f32[384,384]{0,1:T(8,128)} %get-tuple-element.186) | copy-start | bytes 1769476
  424.8 5.4 %copy-start.3 = (f32[384,384]{0,1:T(8,128)S(1)}, f32[384,384]{0,1:T(8,128)}, u32[]{:S(2)}) copy-start(f32[384,384]{0,1:T(8,128)} %get-tuple-element.185) | copy-start | bytes 1769476
  427.0 9.8 %copy-start.13 = (f32[96,384]{1,0:T(8,128)S(1)}, f32[96,384]{1,0:T(8,128)}, u32[]{:S(2)}) copy-start(f32[96,384]{1,0:T(8,128)} %param.33) | copy-start | bytes 442372
  427.0 9.8 %copy-start.14 = (f32[96,384]{1,0:T(8,128)S(1)}, f32[96,384]{1,0:T(8,128)}, u32[]{:S(2)}) copy-start(f32[96,384]{1,0:T(8,128)} %get-tuple-element.263) | copy-start | bytes 442372
  427.0 9.8 %copy-start.20 = (f32[96,384]{1,0:T(8,128)S(1)}, f32[96,384]{1,0:T(8,128)}, u32[]{:S(2)}) copy-start(f32[96,384]{1,0:T(8,128)} %param.45) | copy-start | bytes 442372
  428.0 9.6 %copy-start.10 = (f32[384,3,96]{0,2,1:T(8,128)S(1)}, f32[384,3,96]{0,2,1:T(8,128)}, u32[]{:S(2)}) copy-start(f32[384,3,96]{0,2,1:T(8,128)} %get-tuple-element.251) | copy-start | bytes 1327108
  428.0 9.6 %copy-start.11 = (f32[384,3,96]{0,2,1:T(8,128)S(1)}, f32[384,3,96]{0,2,1:T(8,128)}, u32[]{:S(2)}) copy-start(f32[384,3,96]{0,2,1:T(8,128)} %param.30) | copy-start | bytes 1327108
  428.0 9.6 %copy-start.18 = (f32[384,3,96]{0,2,1:T(8,128)S(1)}, f32[384,3,96]{0,2,1:T(8,128)}, u32[]{:S(2)}) copy-start(f32[384,3,96]{0,2,1:T(8,128)} %param.39) | copy-start | bytes 1327108
  429.1 7.7 %copy-start.21 = (f32[96,384]{1,0:T(8,128)S(1)}, f32[96,384]{1,0:T(8,128)}, u32[]{:S(2)}) copy-start(f32[96,384]{1,0:T(8,128)} %param.44) | copy-start | bytes 442372
  429.1 8.6 %copy-start.19 = (f32[384,3,96]{0,2,1:T(8,128)S(1)}, f32[384,3,96]{0,2,1:T(8,128)}, u32[]{:S(2)}) copy-start(f32[384,3,96]{0,2,1:T(8,128)} %param.38) | copy-start | bytes 1327108
  431.2 7.7 %copy-start.2 = (f32[2048,384]{1,0:T(8,128)S(1)}, f32[2048,384]{1,0:T(8,128)}, u32[]{:S(2)}) copy-start(f32[2048,384]{1,0:T(8,128)} %get-tuple-element.248) | copy-start | bytes 9437188
Sparse Core Ops, SparseCore 0:
  141.8 46.3 reduce-scatter.4
  190.5 22.7 reduce-scatter.6
  215.6 47.2 reduce-scatter.8
  265.1 47.5 reduce-scatter.10
  316.8 60.7 all-reduce.11

commit v3 on v2

v3 whole, which is shorter than its diff:
```python
from functools import partial

import jax
import jax.numpy as jnp
from jax import lax
from jax.experimental import pallas as pl
from jax.experimental.pallas import tpu as pltpu
from jax.sharding import PartitionSpec as P

D = 384
HDIM = 24
HEADS = 16
GROUPS = 4
PER = 4
LANES = 128
FF = 1536
GRID = 16
WIN = 8
CLIP = GRID * GRID
SPOT = WIN * WIN
SHIFT = 4
STEP = 10
CHUNK = 384

NORM_EPS = 1e-05
MASKED = -1000000000.0
CLIP_LIMIT = 1.0
LEARN_RATE = 0.1
ROW_RATE = 0.5
BETA_ONE = 0.9
BETA_TWO = 0.999
ADAM_EPS = 1e-08
WEIGHT_DECAY = 0.01
SCALE = HDIM ** (-0.5)
F32 = jnp.float32
BF16 = jnp.bfloat16
VMEM_LIMIT = 58 * 1024 * 1024


def nn(a, b):
    return lax.dot_general(a, b, (((1,), (0,)), ((), ())), preferred_element_type=F32)


def nt(a, b):
    return lax.dot_general(a, b, (((1,), (1,)), ((), ())), preferred_element_type=F32)


def tn(a, b):
    return lax.dot_general(a, b, (((0,), (0,)), ((), ())), preferred_element_type=F32)


def iota(shape, axis):
    return lax.broadcasted_iota(jnp.int32, shape, axis)


def fold(x):
    return jnp.sum(x.reshape(x.shape[0] // 8, 8, x.shape[1]), axis=0)


def normalize(x):
    center = x - jnp.mean(x, axis=-1, keepdims=True)
    spread = jnp.mean(center * center, axis=-1, keepdims=True)
    inverse = lax.rsqrt(spread + NORM_EPS)
    return center * inverse, inverse


def norm_back(e, n, inverse, gain):
    q = e * gain
    return inverse * (
        q - jnp.mean(q, axis=-1, keepdims=True) - n * jnp.mean(q * n, axis=-1, keepdims=True)
    )


def to_windows(x):
    low = iota((8, x.shape[1]), 0) < 4
    first, second = [], []
    for t in range(GRID):
        a = x[16 * t : 16 * t + 8]
        b = x[16 * t + 8 : 16 * t + 16]
        first.append(pltpu.roll(jnp.where(low, b, a), 4, axis=0))
        second.append(pltpu.roll(jnp.where(low, a, b), 4, axis=0))
    pieces = []
    for wt in range(2):
        for side in (first, second):
            for a in range(WIN):
                pieces.append(side[(wt * WIN + a + SHIFT) % GRID])
    return jnp.concatenate(pieces, axis=0)


def from_windows(y):
    low = iota((8, y.shape[1]), 0) < 4
    pieces = []
    for t in range(GRID):
        rolled = (t - SHIFT) % GRID
        base = (rolled // WIN) * 128 + (rolled % WIN) * 8
        u = pltpu.roll(y[base : base + 8], 4, axis=0)
        v = pltpu.roll(y[base + 64 : base + 72], 4, axis=0)
        pieces.append(jnp.where(low, v, u))
        pieces.append(jnp.where(low, u, v))
    return jnp.concatenate(pieces, axis=0)


def head_masks(dtype):
    lane = iota((16, LANES), 1) // HDIM
    return [jnp.where(lane == h, 1.0, 0.0).astype(F32).astype(dtype) for h in range(PER)]


def stack_heads(x, masks):
    tiles = x.reshape(SPOT // 16, 16, LANES)
    return jnp.concatenate([(tiles * m[None]).reshape(SPOT, LANES) for m in masks], axis=0)


def pick_heads(r):
    lane = iota((SPOT, LANES), 1)
    out = r[3 * SPOT :]
    for h in (2, 1, 0):
        out = jnp.where(lane < (h + 1) * HDIM, r[h * SPOT : (h + 1) * SPOT], out)
    return out


def key_times(wt, wf):
    j = iota((SPOT, PER * SPOT), 0)
    i = iota((SPOT, PER * SPOT), 1) % SPOT
    time = (wt * WIN + j // WIN + SHIFT) % GRID
    same = j >= 0
    if wt:
        same = same & ((j // WIN < 4) == (i // WIN < 4))
    if wf:
        same = same & ((j % WIN < 4) == (i % WIN < 4))
    return jnp.where(same, time, 99)


def split_three(x):
    one = x.astype(BF16)
    rest = x - one.astype(F32)
    two = rest.astype(BF16)
    three = (rest - two.astype(F32)).astype(BF16)
    return one, two, three


def build_bias(table_ref, bias_ref):
    row = iota((256, 256), 0)
    lane = iota((256, 256), 1)
    spot = lane % SPOT
    base = spot // WIN * (2 * WIN - 1) + spot % WIN
    for g in range(GROUPS):
        total = None
        for h in range(PER):
            own = jnp.where((row == base) & (lane // SPOT == h), 1.0, 0.0).astype(F32).astype(BF16)
            line = jnp.broadcast_to(table_ref[g, 1 + h : 2 + h, :256], (8, 256))
            spread = jnp.concatenate(
                [
                    pltpu.roll(line, (15 * a + 144) % 256, axis=1, stride=1, stride_axis=0)
                    for a in range(WIN)
                ],
                axis=0,
            )
            for part in split_three(spread):
                term = nn(part, own)
                total = term if total is None else total + term
        bias_ref[g] = total


def gelu_parts(u):
    mag = jnp.abs(u) * (0.5**0.5)
    t = 1.0 / (1.0 + 0.3275911 * mag)
    bell = jnp.exp(-0.5 * (u * u))
    poly = t * (
        0.127414796
        + t * (-0.142248368 + t * (0.7107068705 + t * (-0.7265760135 + t * 0.5307027145)))
    )
    tail = poly * bell
    return jnp.where(u >= 0.0, 1.0 - tail, tail), bell * 0.3989422804014327


def place(win, head):
    return {"win": win, "head": head}


def remote(src, dst, send, recv, win, head):
    return pltpu.make_async_remote_copy(
        src_ref=src,
        dst_ref=dst,
        send_sem=send,
        recv_sem=recv,
        device_id=place(win, head),
        device_id_type=pl.DeviceIdType.MESH,
    )


def position():
    win, head = lax.axis_index("win"), lax.axis_index("head")
    core, cell = win % 2, (win // 2) % 4
    return win, head, core, cell, win - core - 2 * cell


def greet():
    win, head, core, cell, base = position()
    barrier = pltpu.get_barrier_semaphore()
    peers = [(win, (head + d) % 4) for d in (1, 2, 3)]
    peers += [(base + 2 * ((cell + d) % 4) + core, head) for d in (1, 2, 3)]
    peers += [(win + 1 - 2 * core, head)]
    for w, h in peers:
        pl.semaphore_signal(barrier, inc=1, device_id=place(w, h), device_id_type=pl.DeviceIdType.MESH)
    pl.semaphore_wait(barrier, len(peers))


def shard_view(ref, wide, head, start, count):
    if wide:
        return ref.at[pl.ds(start, count), pl.ds(pl.multiple_of(head * D, LANES), D)]
    rows = ref.shape[0] // 4
    return ref.at[pl.ds(pl.multiple_of(head * rows + start, 16), count), :]


def gather_stages(own, full, wide, sems):
    win, head, core, cell, base = position()
    rows = own.shape[0]
    half, part = rows // 2, rows // 8
    mine = pl.multiple_of(core * half + cell * part, 16)
    near = pl.multiple_of(core * half, 16)

    def over_head(d):
        view = shard_view(full, wide, head, mine, part)
        return remote(
            own.at[pl.ds(mine, part), :], view, sems.at[0, d], sems.at[1, d], win, (head + d + 1) % 4
        )

    def over_cell(d, c):
        view = shard_view(full, wide, (head + 3 - d) % 4, mine, part)
        peer = base + 2 * ((cell + c + 1) % 4) + core
        return remote(view, view, sems.at[2 + c, d], sems.at[5 + c, d], peer, head)

    def over_core(d):
        view = shard_view(full, wide, (head + 3 - d) % 4, near, half)
        return remote(view, view, sems.at[8, d], sems.at[9, d], win + 1 - 2 * core, head)

    local = pltpu.make_async_copy(own, shard_view(full, wide, head, 0, rows), sems.at[10, 0])

    def first():
        local.start()
        for d in range(3):
            over_head(d).start()

    def second():
        for d in range(3):
            over_head(d).wait_recv()
            for c in range(3):
                over_cell(d, c).start()

    def third():
        for d in range(3):
            for c in range(3):
                over_cell(d, c).wait_recv()
            over_core(d).start()

    def last():
        for d in range(3):
            over_core(d).wait_recv()
        local.wait()
        for d in range(3):
            over_head(d).wait_send()
            for c in range(3):
                over_cell(d, c).wait_send()
            over_core(d).wait_send()

    return first, second, third, last


def reduce_stages(buf, from_core, from_cell, from_upper, from_head, final, sems):
    win, head, core, cell, base = position()
    rows = buf.shape[0]
    half, part = rows // 2, rows // 8
    near = pl.multiple_of(core * half, 16)
    far = pl.multiple_of((1 - core) * half, 16)
    mine = pl.multiple_of(core * half + cell * part, 16)
    other = win + 1 - 2 * core
    own = pl.ds(mine, part)

    def lanes(h):
        return pl.ds(pl.multiple_of(h * D, LANES), D)

    def to_core():
        return remote(
            buf.at[pl.ds(far, half), :], from_core, sems.at[0, 0], sems.at[1, 0], other, head
        )

    def to_cell(c):
        peer = (cell + c + 1) % 4
        start = pl.multiple_of(core * half + peer * part, 16)
        return remote(
            buf.at[pl.ds(start, part), :],
            from_cell.at[c],
            sems.at[0, 1 + c],
            sems.at[1, 1 + c],
            base + 2 * peer + core,
            head,
        )

    def to_upper(b):
        peer = win + (8 << b) - 2 * (8 << b) * (win // (8 << b) % 2)
        return remote(
            buf.at[own, :], from_upper.at[b], sems.at[0, 14 + b], sems.at[1, 14 + b], peer, head
        )

    def to_head(d):
        peer = (head + d + 1) % 4
        return remote(
            buf.at[own, lanes(peer)],
            from_head.at[d],
            sems.at[0, 4 + d],
            sems.at[1, 4 + d],
            win,
            peer,
        )

    def back_cell(c):
        peer = (cell + c + 1) % 4
        return remote(
            final.at[own, :],
            final.at[own, :],
            sems.at[0, 7 + c],
            sems.at[1, 7 + c],
            base + 2 * peer + core,
            head,
        )

    def back_core():
        view = final.at[pl.ds(near, half), :]
        return remote(view, view, sems.at[0, 10], sems.at[1, 10], other, head)

    def first():
        to_core().start()

    def second():
        to_core().wait_recv()
        for k in range(4):
            start = pl.multiple_of(core * half + k * part, 16)
            block = pl.ds(start, part)
            total = buf[block, :].astype(F32) + from_core[k * part : k * part + part].astype(F32)
            buf[block, :] = total.astype(BF16)
        for c in range(3):
            to_cell(c).start()

    def third():
        for c in range(3):
            to_cell(c).wait_recv()
        total = buf[own, :].astype(F32)
        for c in range(3):
            total = total + from_cell[c].astype(F32)
        buf[own, :] = total.astype(BF16)
        for b in range(from_upper.shape[0] - 1):
            to_upper(b).start()
            to_upper(b).wait()
            buf[own, :] = (buf[own, :].astype(F32) + from_upper[b].astype(F32)).astype(BF16)
        for d in range(3):
            to_head(d).start()

    def fourth():
        for d in range(3):
            to_head(d).wait_recv()
        total = buf[own, lanes(head)].astype(F32)
        for d in range(3):
            total = total + from_head[d].astype(F32)
        final[own, :] = total.astype(BF16)
        for c in range(3):
            back_cell(c).start()

    def fifth():
        for c in range(3):
            back_cell(c).wait_recv()
        back_core().start()

    def last():
        back_core().wait_recv()
        to_core().wait_send()
        for c in range(3):
            to_cell(c).wait_send()
            to_head(c).wait_send()
            back_cell(c).wait_send()
        back_core().wait_send()

    return first, second, third, fourth, fifth, last


def small_stages(buf, from_core, cells, from_upper, heads, final, sems):
    win, head, core, cell, base = position()
    other = win + 1 - 2 * core

    def lanes(h):
        return pl.ds(pl.multiple_of(h * D, LANES), D)

    def to_core():
        return remote(buf, from_core, sems.at[0, 0], sems.at[1, 0], other, head)

    def to_cell(c):
        view = cells.at[cell]
        peer = base + 2 * ((cell + c + 1) % 4) + core
        return remote(view, view, sems.at[0, 1 + c], sems.at[1, 1 + c], peer, head)

    def to_upper(b):
        peer = win + (8 << b) - 2 * (8 << b) * (win // (8 << b) % 2)
        return remote(buf, from_upper.at[b], sems.at[0, 14 + b], sems.at[1, 14 + b], peer, head)

    def to_head(d):
        peer = (head + d + 1) % 4
        return remote(
            buf.at[:, lanes(peer)], heads.at[head], sems.at[0, 4 + d], sems.at[1, 4 + d], win, peer
        )

    def first():
        to_core().start()

    def second():
        to_core().wait()
        cells[cell] = buf[...] + from_core[...]
        for c in range(3):
            to_cell(c).start()

    def third():
        for c in range(3):
            to_cell(c).wait()
        buf[...] = (cells[0] + cells[1]) + (cells[2] + cells[3])
        for b in range(from_upper.shape[0] - 1):
            to_upper(b).start()
            to_upper(b).wait()
            buf[...] = buf[...] + from_upper[b]
        heads[head] = buf[:, lanes(head)]
        for d in range(3):
            to_head(d).start()

    def last():
        for d in range(3):
            to_head(d).wait()
        final[...] = (heads[0] + heads[1]) + (heads[2] + heads[3])

    return first, second, third, last


def clip_rows(c, count=CLIP):
    return pl.ds(pl.multiple_of(c * count, count), count)


def block_kernel(
    clips,
    frames_ref,
    tok_hbm,
    og_hbm,
    qown_ref,
    pown_ref,
    aown_ref,
    bown_ref,
    sown_ref,
    rowp_ref,
    out_hbm,
    din_hbm,
    early_ref,
    late_ref,
    esmall_ref,
    lsmall_ref,
    norm_ref,
    tok_ref,
    og_ref,
    out_ref,
    dmid_ref,
    qkv_ref,
    probs_ref,
    att_ref,
    wqkv_ref,
    wproj_ref,
    w1_ref,
    w2_ref,
    small_ref,
    bqkv_ref,
    b1_ref,
    bias_ref,
    time_ref,
    g1_ref,
    g2_ref,
    gp_ref,
    rows_ref,
    gb_ref,
    gqv_ref,
    tacc_ref,
    ebuf,
    lbuf,
    esbuf,
    lsbuf,
    core_e,
    core_l,
    core_es,
    core_ls,
    cell_e,
    cell_l,
    cell_es,
    cell_ls,
    up_e,
    up_l,
    up_es,
    up_ls,
    head_e,
    head_l,
    head_es,
    head_ls,
    efinal,
    lfinal,
    nslots,
    wsems,
    ssems,
    rsems,
    nsems,
    osems,
):
    win, head, core, cell, base = position()
    load_tok = pltpu.make_async_copy(tok_hbm, tok_ref, osems.at[2, 0])
    load_og = pltpu.make_async_copy(og_hbm, og_ref, osems.at[2, 1])
    load_tok.start()
    load_og.start()
    greet()
    small = [
        remote(sown_ref, small_ref.at[head], ssems.at[0, d], ssems.at[1, d], win, (head + d + 1) % 4)
        for d in range(3)
    ]
    own_small = pltpu.make_async_copy(sown_ref, small_ref.at[head], ssems.at[2, 0])
    gq_w = gather_stages(qown_ref, wqkv_ref, True, wsems.at[0])
    others = [
        gather_stages(own, full, wide, wsems.at[1 + i])
        for i, (own, full, wide) in enumerate(
            ((pown_ref, wproj_ref, False), (aown_ref, w1_ref, True), (bown_ref, w2_ref, False))
        )
    ]
    gq_w[0]()
    own_small.start()
    for copy in small:
        copy.start()
    for wt in range(2):
        for wf in range(2):
            time_ref[wt * 2 + wf] = key_times(wt, wf)
    for ref in (g1_ref, g2_ref, gp_ref, rows_ref, gb_ref, gqv_ref, tacc_ref, esbuf, lsbuf):
        ref[...] = jnp.zeros_like(ref)
    gq_w[1]()
    own_small.wait()
    for copy in small:
        copy.wait()
    for g in range(4):
        bqkv_ref[0:1, g * D : g * D + LANES] = small_ref[g, 0:1, :LANES]
        bqkv_ref[0:1, g * D + LANES : g * D + 2 * LANES] = jnp.zeros((1, LANES), F32)
        bqkv_ref[0:1, g * D + 2 * LANES : g * D + D] = small_ref[g, 0:1, LANES : 2 * LANES]
        b1_ref[0:1, g * D : g * D + D] = small_ref[g, 5:6, :]
    build_bias(small_ref, bias_ref)
    gq_w[2]()
    for k in others:
        k[0]()
    gq_w[3]()
    load_tok.wait()

    def attend(c, carry):
        rows = clip_rows(c)
        frames = frames_ref[c]
        x = to_windows(tok_ref[rows, :].astype(F32))
        n1, _ = normalize(x)
        n1 = (n1 * rowp_ref[0:1] + rowp_ref[1:2]).astype(BF16)
        for part in range(3):
            cols = slice(part * 512, part * 512 + 512)
            y = nn(n1, wqkv_ref[:, cols]) + bqkv_ref[0:1, cols]
            qkv_ref[rows, cols] = y.astype(BF16)
        masks = head_masks(BF16)
        for w in range(4):
            spots = pl.ds(pl.multiple_of(c * CLIP + w * SPOT, SPOT), SPOT)
            for g in range(GROUPS):
                q = qkv_ref[spots, g * D : g * D + LANES]
                k = qkv_ref[spots, g * D + LANES : g * D + 2 * LANES]
                v = qkv_ref[spots, g * D + 2 * LANES : g * D + D]
                s = nt(k, stack_heads(q, masks)) * SCALE + bias_ref[g]
                s = jnp.where(time_ref[w] < frames, s, MASKED)
                e = jnp.exp(s - jnp.max(s, axis=0, keepdims=True))
                p = (e * (1.0 / jnp.sum(e, axis=0, keepdims=True))).astype(BF16)
                probs_ref[c, w, g] = p
                o = pick_heads(tn(p, v))
                att_ref[spots, g * LANES : g * LANES + LANES] = o.astype(BF16)
        return carry

    def feed(c, carry):
        rows = clip_rows(c)
        x = to_windows(tok_ref[rows, :].astype(F32))
        og = to_windows(og_ref[rows, :].astype(F32))
        att = att_ref[rows, :]
        middle = x + nn(att, wproj_ref[...]) + rowp_ref[4:5]
        nrm, inv = normalize(middle)
        n2 = (nrm * rowp_ref[2:3] + rowp_ref[3:4]).astype(BF16)
        n2t = n2.T
        ogb = og.astype(BF16)
        ogt = ogb.T
        ffn = None
        dn2 = None
        for j in range(FF // CHUNK):
            cols = slice(j * CHUNK, j * CHUNK + CHUNK)
            u = nn(n2, w1_ref[:, cols]) + b1_ref[0:1, cols]
            phi, dens = gelu_parts(u)
            hid = (u * phi).astype(BF16)
            du = ((phi + u * dens) * nt(ogb, w2_ref[cols, :])).astype(BF16)
            gb_ref[:, cols] += fold(du.astype(F32))
            g1_ref[:, cols] += nn(n2t, du)
            g2_ref[:, cols] += nn(ogt, hid)
            a = nn(hid, w2_ref[cols, :])
            b = nt(du, w1_ref[:, cols])
            ffn = a if ffn is None else ffn + a
            dn2 = b if dn2 is None else dn2 + b
        out_ref[rows, :] = from_windows(middle + ffn + rowp_ref[5:6])
        pltpu.make_async_copy(out_ref.at[rows, :], out_hbm.at[rows, :], osems.at[0, c]).start()
        dmid = og + norm_back(dn2, nrm, inv, rowp_ref[2:3])
        dmid_ref[rows, :] = dmid
        dbr = dmid.astype(BF16)
        rows_ref[2] += fold(dn2 * nrm)
        rows_ref[3] += fold(dn2)
        rows_ref[4] += fold(dbr.astype(F32))
        rows_ref[5] += fold(og)
        attt = att.T
        for g in range(GROUPS):
            gp_ref[:, g * D : g * D + D] += nn(attt[g * LANES : g * LANES + LANES], dbr)
        att_ref[rows, :] = nt(dbr, wproj_ref[...]).astype(BF16)
        return carry

    def attend_back(c, carry):
        rows = clip_rows(c)
        frames = frames_ref[c]
        masks = head_masks(BF16)
        for g in range(GROUPS):
            tacc = None
            for w in range(4):
                spots = pl.ds(pl.multiple_of(c * CLIP + w * SPOT, SPOT), SPOT)
                cq = slice(g * D, g * D + LANES)
                ck = slice(g * D + LANES, g * D + 2 * LANES)
                cv = slice(g * D + 2 * LANES, g * D + D)
                q = qkv_ref[spots, cq]
                k = qkv_ref[spots, ck]
                v = qkv_ref[spots, cv]
                do = stack_heads(att_ref[spots, g * LANES : g * LANES + LANES], masks)
                p = probs_ref[c, w, g]
                pf = p.astype(F32)
                dp = nt(v, do)
                inner = jnp.sum(pf * dp, axis=0, keepdims=True)
                ds = jnp.where(time_ref[w] < frames, pf * (dp - inner), 0.0)
                tacc = ds if tacc is None else tacc + ds
                ds = ds.astype(BF16)
                qkv_ref[spots, cq] = (pick_heads(tn(ds, k)) * SCALE).astype(BF16)
                qkv_ref[spots, ck] = (nn(ds, stack_heads(q, masks)) * SCALE).astype(BF16)
                qkv_ref[spots, cv] = nn(p, do).astype(BF16)
            tacc_ref[g] += tacc
        gqv_ref[...] += fold(qkv_ref[rows, :].astype(F32))
        n, _ = normalize(to_windows(tok_ref[rows, :].astype(F32)))
        n1t = (n * rowp_ref[0:1] + rowp_ref[1:2]).astype(BF16).T
        g1_ref[...] += nn(n1t, qkv_ref[rows, :])
        return carry

    def entry_back(c, carry):
        rows = clip_rows(c)
        n, inv = normalize(to_windows(tok_ref[rows, :].astype(F32)))
        dn1 = nt(qkv_ref[rows, :], wqkv_ref[...])
        rows_ref[0] += fold(dn1 * n)
        rows_ref[1] += fold(dn1)
        din = dmid_ref[rows, :] + norm_back(dn1, n, inv, rowp_ref[0:1])
        dmid_ref[rows, :] = from_windows(din)
        pltpu.make_async_copy(dmid_ref.at[rows, :], din_hbm.at[rows, :], osems.at[1, c]).start()
        return carry

    def span(share):
        return clips * share // 8

    lax.fori_loop(0, span(2), attend, 0)
    for k in others:
        k[1]()
    lax.fori_loop(span(2), span(5), attend, 0)
    for k in others:
        k[2]()
    lax.fori_loop(span(5), span(8), attend, 0)
    for k in others:
        k[3]()
    load_og.wait()
    lax.fori_loop(0, clips, feed, 0)

    early = reduce_stages(ebuf, core_e, cell_e, up_e, head_e, efinal, rsems.at[0])
    early_small = small_stages(esbuf, core_es, cell_es, up_es, head_es, esmall_ref, rsems.at[1])
    late = reduce_stages(lbuf, core_l, cell_l, up_l, head_l, lfinal, rsems.at[2])
    late_small = small_stages(lsbuf, core_ls, cell_ls, up_ls, head_ls, lsmall_ref, rsems.at[3])
    ebuf[0:D, :] = g1_ref[...].astype(BF16)
    ebuf[D : 2 * D, :] = g2_ref[...].astype(BF16)
    ebuf[2 * D : 2 * D + LANES, :] = gp_ref[...].astype(BF16)
    early[0]()
    g1_ref[...] = jnp.zeros_like(g1_ref)
    esbuf[0:1, :] = jnp.sum(gb_ref[...], axis=0, keepdims=True)
    for r in range(4):
        line = jnp.sum(rows_ref[2 + r], axis=0, keepdims=True)
        for g in range(GROUPS):
            esbuf[1 + r : 2 + r, g * D : g * D + D] = line
    early_small[0]()
    lax.fori_loop(0, span(1), attend_back, 0)
    early[1]()
    early_small[1]()
    lax.fori_loop(span(1), span(4), attend_back, 0)
    early[2]()
    early_small[2]()
    lax.fori_loop(span(4), span(6), attend_back, 0)
    early[3]()
    early_small[3]()
    lax.fori_loop(span(6), span(7), attend_back, 0)
    early[4]()
    lax.fori_loop(span(7), span(8), attend_back, 0)
    lbuf[...] = g1_ref[...].astype(BF16)
    late[0]()
    for g in range(GROUPS):
        cols = slice(g * D, g * D + LANES)
        lsbuf[0:1, cols] = jnp.sum(gqv_ref[:, cols], axis=0, keepdims=True)
        cols = slice(g * D + 2 * LANES, g * D + D)
        lsbuf[0:1, cols] = jnp.sum(gqv_ref[:, cols], axis=0, keepdims=True)
    fold_table(tacc_ref, lsbuf)
    late[1]()
    early[5]()
    lax.fori_loop(0, span(6), entry_back, 0)
    late[2]()
    lax.fori_loop(span(6), span(8), entry_back, 0)
    for r in range(2):
        line = jnp.sum(rows_ref[r], axis=0, keepdims=True)
        for g in range(GROUPS):
            lsbuf[4 + r : 5 + r, g * D : g * D + D] = line
    late_small[0]()
    late[3]()
    late_small[1]()
    late[4]()
    late_small[2]()
    late[5]()
    late_small[3]()
    early_ref[...] = efinal[...]
    late_ref[...] = lfinal[...]
    square = jnp.zeros((8, D), F32)
    for ref in (efinal, lfinal):
        value = ref[...].astype(F32)
        square = square + fold(value * value)
    es, ls = esmall_ref[...], lsmall_ref[...]
    row = iota((8, D), 0)
    square = square + jnp.where(row < 1, es * es, 0.0) + jnp.where(row < 4, ls * ls, 0.0)
    common = jnp.where((row >= 1) & (row < 5), es * es, 0.0)
    common = common + jnp.where((row >= 4) & (row < 6), ls * ls, 0.0)
    nslots[head] = jnp.broadcast_to(jnp.sum(square, keepdims=True), (8, LANES))
    sends = [
        remote(
            nslots.at[head], nslots.at[head], nsems.at[0, d], nsems.at[1, d], win, (head + d + 1) % 4
        )
        for d in range(3)
    ]
    for copy in sends:
        copy.start()
    for copy in sends:
        copy.wait()
    total = (nslots[0] + nslots[1]) + (nslots[2] + nslots[3])
    norm_ref[...] = jnp.sqrt(total + jnp.sum(common, keepdims=True))

    def finish(c, carry):
        rows = clip_rows(c)
        pltpu.make_async_copy(out_ref.at[rows, :], out_hbm.at[rows, :], osems.at[0, c]).wait()
        pltpu.make_async_copy(dmid_ref.at[rows, :], din_hbm.at[rows, :], osems.at[1, c]).wait()
        return carry

    lax.fori_loop(0, clips, finish, 0)


def fold_table(tacc_ref, lsbuf):
    row = iota((256, 256), 0)
    lane = iota((256, 256), 1)
    spot = row % SPOT
    base = 112 - (spot // WIN * (2 * WIN - 1) + spot % WIN)
    for h in range(PER):
        own = jnp.where((lane == base) & (row // SPOT == h), 1.0, 0.0).astype(F32).astype(BF16)
        for g in range(GROUPS):
            spread = None
            for part in split_three(tacc_ref[g]):
                term = nn(part, own)
                spread = term if spread is None else spread + term
            total = None
            for a in range(WIN):
                piece = pltpu.roll(
                    spread[a * 8 : a * 8 + 8], 15 * a, axis=1, stride=1, stride_axis=0
                )
                total = piece if total is None else total + piece
            line = jnp.sum(total, axis=0, keepdims=True)
            for half in range(2):
                at = h * 256 + half * LANES
                lsbuf[1 + at // D : 2 + at // D, g * D + at % D : g * D + at % D + LANES] = line[
                    :, half * LANES : half * LANES + LANES
                ]


def block(frames, tok, og, qown, pown, aown, bown, sown, rowp):
    rows = tok.shape[0]
    clips = rows // CLIP
    upper = max(lax.axis_size("win") // 8, 1).bit_length() - 1
    shape = jax.ShapeDtypeStruct
    sems = pltpu.SemaphoreType.DMA
    vmem = pltpu.VMEM
    spec = pl.BlockSpec
    inside = lambda: spec(memory_space=vmem)
    outside = lambda: spec(memory_space=pl.ANY)
    early, late = 2 * D + LANES, D
    return pl.pallas_call(
        partial(block_kernel, clips),
        in_specs=[spec(memory_space=pltpu.SMEM), outside(), outside()] + [inside()] * 6,
        out_specs=[outside(), outside()] + [inside()] * 5,
        out_shape=[
            shape((rows, D), F32),
            shape((rows, D), F32),
            shape((early, D), BF16),
            shape((late, D), BF16),
            shape((8, D), F32),
            shape((8, D), F32),
            shape((8, LANES), F32),
        ],
        scratch_shapes=[
            vmem((rows, D), BF16),
            vmem((rows, D), BF16),
            vmem((rows, D), F32),
            vmem((rows, D), F32),
            vmem((rows, 1536), BF16),
            vmem((clips, 4, GROUPS, SPOT, PER * SPOT), BF16),
            vmem((rows, 512), BF16),
            vmem((D, 1536), BF16),
            vmem((512, D), BF16),
            vmem((D, FF), BF16),
            vmem((FF, D), BF16),
            vmem((GROUPS, 8, D), F32),
            vmem((8, 1536), F32),
            vmem((8, FF), F32),
            vmem((GROUPS, SPOT, PER * SPOT), F32),
            vmem((4, SPOT, PER * SPOT), jnp.int32),
            vmem((D, FF), F32),
            vmem((D, FF), F32),
            vmem((LANES, 1536), F32),
            vmem((6, 8, D), F32),
            vmem((8, FF), F32),
            vmem((8, 1536), F32),
            vmem((GROUPS, SPOT, PER * SPOT), F32),
            vmem((early, 1536), BF16),
            vmem((late, 1536), BF16),
            vmem((8, 1536), F32),
            vmem((8, 1536), F32),
            vmem((early // 2, 1536), BF16),
            vmem((late // 2, 1536), BF16),
            vmem((8, 1536), F32),
            vmem((8, 1536), F32),
            vmem((3, early // 8, 1536), BF16),
            vmem((3, late // 8, 1536), BF16),
            vmem((4, 8, 1536), F32),
            vmem((4, 8, 1536), F32),
            vmem((upper + 1, early // 8, 1536), BF16),
            vmem((upper + 1, late // 8, 1536), BF16),
            vmem((upper + 1, 8, 1536), F32),
            vmem((upper + 1, 8, 1536), F32),
            vmem((3, early // 8, D), BF16),
            vmem((3, late // 8, D), BF16),
            vmem((4, 8, D), F32),
            vmem((4, 8, D), F32),
            vmem((early, D), BF16),
            vmem((late, D), BF16),
            vmem((4, 8, LANES), F32),
            sems((4, 11, 3)),
            sems((3, 3)),
            sems((4, 2, 14 + upper)),
            sems((2, 3)),
            sems((3, max(clips, 2))),
        ],
        compiler_params=pltpu.CompilerParams(
            vmem_limit_bytes=VMEM_LIMIT, collective_id=0, has_side_effects=True
        ),
    )(frames, tok, og, qown, pown, aown, bown, sown, rowp)


def adam_step(weight, gradient, moment, second, factor, rate):
    clipped = gradient * factor
    moment_new = BETA_ONE * moment + (1.0 - BETA_ONE) * clipped
    second_new = BETA_TWO * second + (1.0 - BETA_TWO) * clipped * clipped
    moment_hat = moment_new / (1.0 - BETA_ONE**STEP)
    second_hat = second_new / (1.0 - BETA_TWO**STEP)
    master = weight - rate * (
        moment_hat / (jnp.sqrt(second_hat) + ADAM_EPS) + WEIGHT_DECAY * weight
    )
    return (gradient, moment_new, second_new, master)


def shards(
    tokens,
    out_grad,
    clip_frames,
    qkv_weight,
    qv_bias,
    rel_table,
    proj_weight,
    fc1_weight,
    fc1_bias,
    fc2_weight,
    row_params,
    qkv_first,
    qkv_second,
    qvb_first,
    qvb_second,
    table_first,
    table_second,
    proj_first,
    proj_second,
    fc1_first,
    fc1_second,
    fc1b_first,
    fc1b_second,
    fc2_first,
    fc2_second,
    rows_first,
    rows_second,
):
    clips = tokens.shape[0] // CLIP
    local = rel_table.shape[1] * HDIM
    offsets = rel_table.shape[0]
    frames = lax.dynamic_slice(clip_frames, (lax.axis_index("head") * clips,), (clips,))
    pad = LANES - local
    qown = jnp.pad(qkv_weight.astype(BF16), ((0, 0), (0, 0), (0, pad))).reshape(D, D)
    pown = jnp.pad(proj_weight.astype(BF16), ((0, pad), (0, 0)))
    aown, bown = fc1_weight.astype(BF16), fc2_weight.astype(BF16)
    bias_row = jnp.pad(qv_bias, ((0, 1), (0, pad))).reshape(1, D)
    sown = jnp.concatenate(
        [
            bias_row,
            jnp.pad(rel_table.T, ((0, 0), (0, D - offsets))),
            fc1_bias[None],
            jnp.zeros((2, D), F32),
        ]
    )
    output, input_grad, early, late, esmall, lsmall, norm = block(
        frames, tokens, out_grad, qown, pown, aown, bown, sown, row_params
    )
    early, late = early.astype(F32), late.astype(F32)
    grad_norm = norm[0, 0]
    factor = jnp.minimum(1.0, CLIP_LIMIT / (grad_norm + 1e-06))
    table = lsmall[1:4].reshape(-1)[: PER * 256].reshape(PER, 256)
    gradients = (
        late.reshape(D, 3, LANES)[..., :local],
        lsmall[0].reshape(3, LANES)[::2, :local],
        table[:, :offsets][:, ::-1].T,
        early[2 * D : 2 * D + local],
        early[:D],
        esmall[0],
        early[D : 2 * D].T,
        jnp.concatenate([lsmall[4:6], esmall[1:5]]),
    )
    weights = (
        qkv_weight,
        qv_bias,
        rel_table,
        proj_weight,
        fc1_weight,
        fc1_bias,
        fc2_weight,
        row_params,
    )
    firsts = (
        qkv_first,
        qvb_first,
        table_first,
        proj_first,
        fc1_first,
        fc1b_first,
        fc2_first,
        rows_first,
    )
    seconds = (
        qkv_second,
        qvb_second,
        table_second,
        proj_second,
        fc1_second,
        fc1b_second,
        fc2_second,
        rows_second,
    )
    rates = (
        LEARN_RATE,
        LEARN_RATE,
        ROW_RATE,
        LEARN_RATE,
        LEARN_RATE,
        LEARN_RATE,
        LEARN_RATE,
        ROW_RATE,
    )
    updated = []
    for weight, gradient, moment, second, rate in zip(weights, gradients, firsts, seconds, rates):
        updated.extend(adam_step(weight, gradient, moment, second, factor, rate))
    return (output, input_grad, grad_norm, *updated)


def solution(mesh):
    rows = P(("win", "head"), None)
    last3, last2, first2, first1 = P(None, None, "head"), P(None, "head"), P("head", None), P("head")
    each = (last3, last2, last2, first2, last2, first1, first2, P())
    return jax.shard_map(
        shards,
        mesh=mesh,
        in_specs=(rows, rows, P("win")) + each + tuple(s for s in each for _ in range(2)),
        out_specs=(rows, rows, P()) + tuple(s for s in each for _ in range(4)),
        check_vma=False,
    )
```

time: 449 us -> 209 us (0.47)
  waiting for transfers between devices: 166 us -> 0 us
  blocking collectives: 78.8 us -> 0 us
  Pallas kernels: 128 us -> 159 us
  between operations: 22.5 us -> 1.68 us
  other arithmetic: 26.1 us -> 13.2 us
  local copies, waits for them, and re-layouts: 27.1 us -> 34.5 us
    reduce_scatter x4 -> x0, waiting for transfers between devices: 165 us -> none  [shards(): lax.psum_scatter(v, 'head', scatter_dimension=dim, tiled=True)]
    psum x3 -> x0, blocking collectives: 61.6 us -> none  [the longest x1 37.6 us: shards(): lax.psum(jnp.sum(jnp.concatenate([rows_b, rows_f]), axis=1), ('win', 'hea...]
    pallas_call x2 -> x1, Pallas kernels: 128 us -> 159 us  [block(): pl.pallas_call(partial(block_kernel, clips), in_specs=[spec(memory_space=...]
    unnamed x1 -> x0, blocking collectives: 17.3 us -> none
    reduce_sum x11 -> x0, other arithmetic: 10.5 us -> none  [the longest x8 10.4 us: shards(): square = lambda v: jnp.sum(v * v)]
    unnamed x89 -> x77, local copies, waits for them, and re-layouts: 19.4 us -> 26.8 us
  transfers between devices with their start and end apart: 5 -> 0, of which waited for: 4 -> 0; matrix products, arithmetic and copies ran while one was open for 3% -> 0% of each run, Pallas kernels for 0% -> 0%
where the time goes in v3:
time: 209 us; the launch traced here: 208 us
  Pallas kernels  159 us (76%)
  local copies, waits for them, and re-layouts  34.5 us (17%)
  other arithmetic  13.2 us (6%)
    pallas_call x1, Pallas kernels, block(): pl.pallas_call(partial(block_kernel, clips), in_specs=[spec(memory_space=...  159 us
    unnamed x77, local copies, waits for them, and re-layouts  26.8 us
    sub x7, other arithmetic, adam_step(): weight - rate * (moment_hat / (jnp.sqrt(second_hat) + ADAM_EPS) + WEIGHT_...  9.86 us

profile of v3, /device:TPU:0, one launch (start us, length us, event | category | flops | bytes accessed | tf_op | source)
XLA Modules:
  0.0 208.5 jit_solution(15495309023496447045)
XLA Ops:
  0.7 0.0 copy-start.8
  0.7 0.0 copy-start.4
  0.7 1.3 dynamic_slice.3.frames_ref
  2.1 1.0 convert_element_type.24
  3.1 0.0 copy-start.18
  3.1 0.0 copy-start.23
  3.1 0.0 copy-start.13
  3.2 0.9 copy.81.qown_ref
  4.1 0.0 copy-done.8
  4.1 0.7 pad.17.pown_ref
  4.7 0.7 convert_element_type.26.aown_ref
  5.5 0.0 copy-done.3
  5.5 0.7 convert_element_type.27.bown_ref
  6.3 0.1 pad.25.clone
  6.4 0.7 fusion.6.sown_ref
  7.0 159.2 %shard_map.530 = (f32[2048,384]{1,0:T(8,128)}, f32[2048,384]{1,0:T(8,128)}, bf16[896,384]{1,0:T(8,128)(2,1)}, bf16[384,384]{1,0:T(8,128)(2,1)}, f32[8,384]{1,0:T...) custom-call(s32[8]{0:T(128)} %dynamic_slice.3.frames_ref, bf16[2048,384]{1,0:T(8,128)(2,1)} %tok_hbm.1, ...), custom_call_target="tpu_custom_call" | custom-call | tf_op jit(solution)/shard_map/pallas_call | solution.py:803
  166.2 1.2 slice.42
  168.1 1.2 copy.82
  169.2 0.0 copy-done.6
  169.3 0.0 copy-done.9
  169.3 0.0 copy-start.16
  169.3 0.0 copy-start.27
  169.3 0.0 copy-start.28
  169.3 0.0 copy-start.21
  169.3 0.0 copy-start.22
  169.3 0.0 copy-start.10
  169.3 0.0 copy-start.11
  169.4 2.4 %multiply_subtract_fusion.2 = (f32[384,3,96]{0,2,1:T(8,128)}, f32[384,3,96]{0,2,1:T(8,128)}, f32[384,3,96]{0,2,1:T(8,128)}, f32[384,3,96]{0,2,1:T(8,128)}) fusion(f32[384,3,96]{0,2,1:T(8,128)S(1)} %copy-done.6, f32[]{:T(128)S(6)} %min.3, f32[384,3,96]{0,2,1:T(8,128)S(1)} %copy-done.9, f32[384,3,96]{0,2,1:T(8,128)} %param.38, bf16[384,3,128]{0,2,1:T(8,128)(2,1)S(1)} %bitcast.26), kind=kLoop, calls=%fused_computation.11 | loop fusion | flops 1880064 | bytes 3317764 | tf_op jit(solution)/shard_map/sub | solution.py:881
  171.8 0.7 slice_reduce_fusion
  172.5 0.0 copy-start.17
  172.5 0.0 copy-done.28
  172.5 0.0 copy-start.24
  172.6 0.6 multiply_subtract_fusion.7
  173.2 0.3 reverse
  173.5 0.7 slice_bitcast_fusion.1
  174.2 0.0 copy-done.21
  174.2 0.7 multiply_subtract_fusion.5
  174.9 0.8 multiply_subtract_fusion.3
  175.7 0.9 slice.60
  176.6 0.2 copy.91
  176.8 0.1 convert_element_type.28
  176.9 2.1 %copy.89 = f32[384,384]{0,1:T(8,128)} copy(f32[384,384]{1,0:T(8,128)} %param.51) | data formatting | bytes 1179648 | tf_op args[24]
  179.0 2.2 %copy.88 = f32[384,384]{0,1:T(8,128)} copy(f32[384,384]{1,0:T(8,128)} %param.50) | data formatting | bytes 1179648 | tf_op args[23]
  181.2 1.0 copy.87
  182.3 2.2 %copy.85 = f32[384,384]{0,1:T(8,128)} copy(f32[384,384]{1,0:T(8,128)} %param.47) | data formatting | bytes 1179648 | tf_op args[20]
  184.4 0.0 copy-done.5
  184.4 1.0 copy.100
  185.5 1.0 copy.84
  186.6 4.1 %multiply_subtract_fusion = (f32[384,384]{0,1:T(8,128)}, f32[384,384]{0,1:T(8,128)}, f32[384,384]{0,1:T(8,128)}, f32[384,384]{0,1:T(8,128)S(1)}, f32[384,384]{0,1:T(8,128)S(1)}, /*index=5*/f32[384,384]{0,1:T(8,128)}) fusion(f32[384,384]{0,1:T(8,128)S(1)} %copy.91, f32[]{:T(128)S(6)} %min.3, f32[896,384]{1,0:T(8,128)S(1)} %convert_element_type.28, ...), kind=kLoop, calls=%fused_computation.6 | loop fusion | flops 4718592 | bytes 8257540 | tf_op jit(solution)/shard_map/sub | solution.py:881
  190.6 0.0 copy-start.26
  190.7 2.1 %copy.93 = f32[384,384]{1,0:T(8,128)} copy(f32[384,384]{0,1:T(8,128)} %get-tuple-element.150) | data formatting | bytes 1179648
  192.8 1.0 copy.94
  193.8 1.0 copy.95
  194.9 0.0 copy-done.17
  194.9 0.6 multiply_subtract_fusion.6
  195.6 1.1 copy.96
  196.6 0.0 copy-start.1
  196.6 2.3 %copy.97 = f32[384,384]{1,0:T(8,128)} copy(f32[384,384]{0,1:T(8,128)} %get-tuple-element.125) | data formatting | bytes 1179648
  198.9 2.1 %copy.98 = f32[384,384]{1,0:T(8,128)} copy(f32[384,384]{0,1:T(8,128)} %get-tuple-element.124) | data formatting | bytes 1179648
  201.0 2.1 %copy.99 = f32[384,384]{1,0:T(8,128)} copy(f32[384,384]{0,1:T(8,128)} %get-tuple-element.123) | data formatting | bytes 1179648
  203.2 0.6 multiply_subtract_fusion.4
  203.8 1.7 copy.106
  205.5 1.4 copy-done
  206.8 1.7 copy.107
  (47 shorter events, 0.2 us)
Async XLA Ops:
  0.7 3.4 %copy-start.8 = (f32[96,384]{1,0:T(8,128)S(1)}, f32[96,384]{1,0:T(8,128)}, u32[]{:S(2)}) copy-start(f32[96,384]{1,0:T(8,128)} %param.33) | copy-start | bytes 442372
  0.7 4.0 %copy-start.4 = (f32[384,384]{1,0:T(8,128)S(1)}, f32[384,384]{1,0:T(8,128)}, u32[]{:S(2)}) copy-start(f32[384,384]{1,0:T(8,128)} %param.34) | copy-start | bytes 1769476
  0.7 4.8 %copy-start.3 = (f32[384,384]{1,0:T(8,128)S(1)}, f32[384,384]{1,0:T(8,128)}, u32[]{:S(2)}) copy-start(f32[384,384]{1,0:T(8,128)} %param.36) | copy-start | bytes 1769476
  3.1 3.1 %copy-start.18 = (f32[384]{0:T(512)S(1)}, f32[384]{0:T(512)}, u32[]{:S(2)}) copy-start(f32[384]{0:T(512)} %param.35) | copy-start | bytes 4612
  3.1 3.1 %copy-start.23 = (f32[2,96]{1,0:T(2,128)S(1)}, f32[2,96]{1,0:T(2,128)}, u32[]{:S(2)}) copy-start(f32[2,96]{1,0:T(2,128)} %param.31) | copy-start | bytes 2308
  3.1 3.2 %copy-start.13 = (f32[225,4]{0,1:T(4,128)S(1)}, f32[225,4]{0,1:T(4,128)}, u32[]{:S(2)}) copy-start(f32[225,4]{0,1:T(4,128)} %param.32) | copy-start | bytes 10804
  7.0 162.2 %copy-start.6 = (f32[384,3,96]{0,2,1:T(8,128)S(1)}, f32[384,3,96]{0,2,1:T(8,128)}, u32[]{:S(2)}) copy-start(f32[384,3,96]{0,2,1:T(8,128)} %param.30) | copy-start | bytes 1327108
  7.0 162.2 %copy-start.9 = (f32[384,3,96]{0,2,1:T(8,128)S(1)}, f32[384,3,96]{0,2,1:T(8,128)}, u32[]{:S(2)}) copy-start(f32[384,3,96]{0,2,1:T(8,128)} %param.39) | copy-start | bytes 1327108
  169.3 2.5 %copy-start.16 = (f32[8,384]{1,0:T(8,128)S(1)}, f32[8,384]{1,0:T(8,128)}, u32[]{:S(2)}) copy-start(f32[8,384]{1,0:T(8,128)} %get-tuple-element.46) | copy-start | bytes 36868
  169.3 3.3 %copy-start.27 = (f32[2,96]{1,0:T(2,128)S(1)}, f32[2,96]{1,0:T(2,128)}, u32[]{:S(2)}) copy-start(f32[2,96]{1,0:T(2,128)} %param.41) | copy-start | bytes 2308
  169.3 3.2 %copy-start.28 = (f32[2,96]{1,0:T(2,128)S(1)}, f32[2,96]{1,0:T(2,128)}, u32[]{:S(2)}) copy-start(f32[2,96]{1,0:T(2,128)} %param.40) | copy-start | bytes 2308
  169.3 4.9 %copy-start.21 = (f32[225,4]{0,1:T(4,128)S(1)}, f32[225,4]{0,1:T(4,128)}, u32[]{:S(2)}) copy-start(f32[225,4]{0,1:T(4,128)} %param.43) | copy-start | bytes 10804
  169.3 4.9 %copy-start.22 = (f32[225,4]{0,1:T(4,128)S(1)}, f32[225,4]{0,1:T(4,128)}, u32[]{:S(2)}) copy-start(f32[225,4]{0,1:T(4,128)} %param.42) | copy-start | bytes 10804
  169.3 5.6 %copy-start.2 = (bf16[896,384]{1,0:T(8,128)(2,1)S(1)}, bf16[896,384]{1,0:T(8,128)(2,1)}, u32[]{:S(2)}) copy-start(bf16[896,384]{1,0:T(8,128)(2,1)} %get-tuple-element.47) | copy-start | bytes 2064388
  169.3 5.6 %copy-start.10 = (f32[96,384]{1,0:T(8,128)S(1)}, f32[96,384]{1,0:T(8,128)}, u32[]{:S(2)}) copy-start(f32[96,384]{1,0:T(8,128)} %param.45) | copy-start | bytes 442372
  169.3 5.5 %copy-start.11 = (f32[96,384]{1,0:T(8,128)S(1)}, f32[96,384]{1,0:T(8,128)}, u32[]{:S(2)}) copy-start(f32[96,384]{1,0:T(8,128)} %param.44) | copy-start | bytes 442372
  172.5 22.4 %copy-start.17 = (f32[384]{0:T(512)}, f32[384]{0:T(512)S(1)}, u32[]{:S(2)}) copy-start(f32[384]{0:T(512)S(1)} %get-tuple-element.209) | copy-start | bytes 4612
  172.5 3.2 %copy-start.24 = (f32[2,96]{1,0:T(2,128)}, f32[2,96]{1,0:T(2,128)S(1)}, u32[]{:S(2)}) copy-start(f32[2,96]{1,0:T(2,128)S(1)} %slice.46) | copy-start | bytes 2308
  179.0 5.4 %copy-start.5 = (f32[384,384]{1,0:T(8,128)S(1)}, f32[384,384]{1,0:T(8,128)}, u32[]{:S(2)}) copy-start(f32[384,384]{1,0:T(8,128)} %slice.60) | copy-start | bytes 1769476
  182.3 3.2 %copy-start.7 = (f32[384,384]{1,0:T(8,128)S(1)}, f32[384,384]{1,0:T(8,128)}, u32[]{:S(2)}) copy-start(f32[384,384]{1,0:T(8,128)} %param.46) | copy-start | bytes 1769476
  190.6 4.3 %copy-start.19 = (f32[384]{0:T(512)S(1)}, f32[384]{0:T(512)}, u32[]{:S(2)}) copy-start(f32[384]{0:T(512)} %param.35) | copy-start | bytes 4612
  190.6 4.3 %copy-start.25 = (f32[384]{0:T(512)S(1)}, f32[384]{0:T(512)}, u32[]{:S(2)}) copy-start(f32[384]{0:T(512)} %param.49) | copy-start | bytes 4612
  190.6 4.3 %copy-start.26 = (f32[384]{0:T(512)S(1)}, f32[384]{0:T(512)}, u32[]{:S(2)}) copy-start(f32[384]{0:T(512)} %param.48) | copy-start | bytes 4612
  196.6 6.5 %copy-start.20 = (f32[8,384]{1,0:T(8,128)S(1)}, f32[8,384]{1,0:T(8,128)}, u32[]{:S(2)}) copy-start(f32[8,384]{1,0:T(8,128)} %get-tuple-element.48) | copy-start | bytes 36868
  196.6 6.5 %copy-start.12 = (f32[6,384]{1,0:T(8,128)S(1)}, f32[6,384]{1,0:T(8,128)}, u32[]{:S(2)}) copy-start(f32[6,384]{1,0:T(8,128)} %rowp_ref.1) | copy-start | bytes 27652
  196.6 6.5 %copy-start.14 = (f32[6,384]{1,0:T(8,128)S(1)}, f32[6,384]{1,0:T(8,128)}, u32[]{:S(2)}) copy-start(f32[6,384]{1,0:T(8,128)} %param.53) | copy-start | bytes 27652
  196.6 6.5 %copy-start.15 = (f32[6,384]{1,0:T(8,128)S(1)}, f32[6,384]{1,0:T(8,128)}, u32[]{:S(2)}) copy-start(f32[6,384]{1,0:T(8,128)} %param.52) | copy-start | bytes 27652
  196.6 7.2 %copy-start.1 = (f32[2048,384]{1,0:T(8,128)S(1)}, f32[2048,384]{1,0:T(8,128)}, u32[]{:S(2)}) copy-start(f32[2048,384]{1,0:T(8,128)} %get-tuple-element.186) | copy-start | bytes 9437188
  203.8 3.0 %copy-start = (f32[2048,384]{1,0:T(8,128)S(1)}, f32[2048,384]{1,0:T(8,128)}, u32[]{:S(2)}) copy-start(f32[2048,384]{1,0:T(8,128)} %get-tuple-element.187) | copy-start | bytes 9437188

commit v4 on v3

--- a/solution.py
+++ b/solution.py
@@ -20,7 +20,8 @@
 SPOT = WIN * WIN
 SHIFT = 4
 STEP = 10
-CHUNK = 384
+CHUNK = 768
+PAIR = 2 * CLIP
 
 NORM_EPS = 1e-05
 MASKED = -1000000000.0
@@ -34,7 +35,7 @@
 SCALE = HDIM ** (-0.5)
 F32 = jnp.float32
 BF16 = jnp.bfloat16
-VMEM_LIMIT = 58 * 1024 * 1024
+VMEM_LIMIT = 60 * 1024 * 1024
 
 
 def nn(a, b):
@@ -212,18 +213,15 @@
     return ref.at[pl.ds(pl.multiple_of(head * rows + start, 16), count), :]
 
 
-def gather_stages(own, full, wide, sems):
+def gather_stages(rows, full, wide, sems):
     win, head, core, cell, base = position()
-    rows = own.shape[0]
     half, part = rows // 2, rows // 8
     mine = pl.multiple_of(core * half + cell * part, 16)
     near = pl.multiple_of(core * half, 16)
 
     def over_head(d):
         view = shard_view(full, wide, head, mine, part)
-        return remote(
-            own.at[pl.ds(mine, part), :], view, sems.at[0, d], sems.at[1, d], win, (head + d + 1) % 4
-        )
+        return remote(view, view, sems.at[0, d], sems.at[1, d], win, (head + d + 1) % 4)
 
     def over_cell(d, c):
         view = shard_view(full, wide, (head + 3 - d) % 4, mine, part)
@@ -234,10 +232,7 @@
         view = shard_view(full, wide, (head + 3 - d) % 4, near, half)
         return remote(view, view, sems.at[8, d], sems.at[9, d], win + 1 - 2 * core, head)
 
-    local = pltpu.make_async_copy(own, shard_view(full, wide, head, 0, rows), sems.at[10, 0])
-
     def first():
-        local.start()
         for d in range(3):
             over_head(d).start()
 
@@ -256,7 +251,6 @@
     def last():
         for d in range(3):
             over_core(d).wait_recv()
-        local.wait()
         for d in range(3):
             over_head(d).wait_send()
             for c in range(3):
@@ -445,11 +439,13 @@
     frames_ref,
     tok_hbm,
     og_hbm,
-    qown_ref,
-    pown_ref,
-    aown_ref,
-    bown_ref,
-    sown_ref,
+    qraw_ref,
+    praw_ref,
+    araw_ref,
+    braw_ref,
+    qvb_ref,
+    table_ref,
+    fc1b_ref,
     rowp_ref,
     out_hbm,
     din_hbm,
@@ -458,11 +454,18 @@
     esmall_ref,
     lsmall_ref,
     norm_ref,
+    sown_ref,
+    turn_ref,
     tok_ref,
     og_ref,
     out_ref,
     dmid_ref,
+    n1t_ref,
+    n2t_ref,
+    ogt_ref,
     qkv_ref,
+    dj_ref,
+    du_ref,
     probs_ref,
     att_ref,
     wqkv_ref,
@@ -474,9 +477,6 @@
     b1_ref,
     bias_ref,
     time_ref,
-    g1_ref,
-    g2_ref,
-    gp_ref,
     rows_ref,
     gb_ref,
     gqv_ref,
@@ -501,8 +501,6 @@
     head_l,
     head_es,
     head_ls,
-    efinal,
-    lfinal,
     nslots,
     wsems,
     ssems,
@@ -511,32 +509,209 @@
     osems,
 ):
     win, head, core, cell, base = position()
+    first_clip = head * clips
+
+    def enter(c, carry):
+        for part in range(2):
+            rows = clip_rows(2 * c + part)
+            n1, _ = normalize(to_windows(tok_ref[rows, :].astype(F32)))
+            n1 = (n1 * rowp_ref[0:1] + rowp_ref[1:2]).astype(BF16)
+            att_ref[rows, :D] = n1
+            n1t_ref[:, rows] = n1.T
+        return carry
+
+    def project(c, carry):
+        rows = clip_rows(c, PAIR)
+        for part in range(3):
+            cols = slice(part * 512, part * 512 + 512)
+            y = nn(att_ref[rows, :D], wqkv_ref[:, cols]) + bqkv_ref[0:1, cols]
+            qkv_ref[rows, cols] = y.astype(BF16)
+        return carry
+
+    def attend(c, carry):
+        frames = frames_ref[first_clip + c]
+        masks = head_masks(BF16)
+        for w in range(4):
+            spots = pl.ds(pl.multiple_of(c * CLIP + w * SPOT, SPOT), SPOT)
+            for g in range(GROUPS):
+                q = qkv_ref[spots, g * D : g * D + LANES]
+                k = qkv_ref[spots, g * D + LANES : g * D + 2 * LANES]
+                s = nt(k, stack_heads(q, masks)) * SCALE + bias_ref[g]
+                s = jnp.where(time_ref[w] < frames, s, MASKED)
+                e = jnp.exp(s - jnp.max(s, axis=0, keepdims=True))
+                p = (e * (1.0 / jnp.sum(e, axis=0, keepdims=True))).astype(BF16)
+                probs_ref[c, w, g] = p
+        for w in range(4):
+            spots = pl.ds(pl.multiple_of(c * CLIP + w * SPOT, SPOT), SPOT)
+            for g in range(GROUPS):
+                v = qkv_ref[spots, g * D + 2 * LANES : g * D + D]
+                o = pick_heads(tn(probs_ref[c, w, g], v))
+                att_ref[spots, g * LANES : g * LANES + LANES] = o.astype(BF16)
+        return carry
+
+    def send_out(c):
+        return pltpu.make_async_copy(
+            out_ref.at[clip_rows(c % 2, PAIR), :], out_hbm.at[clip_rows(c, PAIR), :], osems.at[0, c]
+        )
+
+    def feed(c, carry):
+        rows = clip_rows(c, PAIR)
+        clip = [clip_rows(2 * c + part) for part in range(2)]
+        x = jnp.concatenate([to_windows(tok_ref[r, :].astype(F32)) for r in clip], axis=0)
+        og = jnp.concatenate([to_windows(og_ref[r, :].astype(F32)) for r in clip], axis=0)
+        middle = x + nn(att_ref[rows, :], wproj_ref[...]) + rowp_ref[4:5]
+        nrm, inv = normalize(middle)
+        n2 = (nrm * rowp_ref[2:3] + rowp_ref[3:4]).astype(BF16)
+        n2t_ref[:, rows] = n2.T
+        ogb = og.astype(BF16)
+        ogt_ref[:, rows] = ogb.T
+        for j in range(FF // CHUNK):
+            cols = slice(j * CHUNK, j * CHUNK + CHUNK)
+            u = nn(n2, w1_ref[:, cols]) + b1_ref[0:1, cols]
+            phi, dens = gelu_parts(u)
+            dj_ref[rows, cols] = (u * phi).astype(BF16)
+            du = ((phi + u * dens) * nt(ogb, w2_ref[cols, :])).astype(BF16)
+            du_ref[rows, cols] = du
+            gb_ref[:, cols] += fold(du.astype(F32))
+        dmid_ref[rows, :] = middle
+        og_ref[rows, :] = ogb
+        return carry
+
+    def feed_out(c, carry):
+        rows = clip_rows(c, PAIR)
+        middle = dmid_ref[rows, :]
+        og = og_ref[rows, :].astype(F32)
+        result = middle + nn(dj_ref[rows, :], w2_ref[...]) + rowp_ref[5:6]
+
+        @pl.when(c >= 2)
+        def _():
+            send_out(c - 2).wait()
+
+        for part in range(2):
+            r = pl.ds(pl.multiple_of(c % 2 * PAIR + part * CLIP, CLIP), CLIP)
+            out_ref[r, :] = from_windows(result[part * CLIP : part * CLIP + CLIP])
+        send_out(c).start()
+        dn2 = nt(du_ref[rows, :], w1_ref[...])
+        nrm, inv = normalize(middle)
+        dmid = og + norm_back(dn2, nrm, inv, rowp_ref[2:3])
+        dmid_ref[rows, :] = dmid
+        dbr = dmid.astype(BF16)
+        rows_ref[2] += fold(dn2 * nrm)
+        rows_ref[3] += fold(dn2)
+        rows_ref[4] += fold(dbr.astype(F32))
+        rows_ref[5] += fold(og)
+        og_ref[rows, :] = dbr
+        return carry
+
+    def feed_grads():
+        for j in range(FF // 512):
+            cols = slice(j * 512, j * 512 + 512)
+            ebuf[0:D, cols] = nn(n2t_ref[...], du_ref[:, cols]).astype(BF16)
+            ebuf[D : 2 * D, cols] = nn(ogt_ref[...], dj_ref[:, cols]).astype(BF16)
+
+    def branch_grads():
+        for g in range(GROUPS):
+            part = tn(att_ref[:, g * LANES : g * LANES + LANES], og_ref[...])
+            lbuf[D : D + LANES, g * D : g * D + D] = part.astype(BF16)
+        for j in range(clips // 2):
+            r = slice(j * PAIR, j * PAIR + PAIR)
+            att_ref[r, :] = nt(og_ref[r, :], wproj_ref[...]).astype(BF16)
+
+    def attend_back(c, carry):
+        rows = clip_rows(c)
+        frames = frames_ref[first_clip + c]
+        masks = head_masks(BF16)
+        for g in range(GROUPS):
+            tacc = None
+            for w in range(4):
+                spots = pl.ds(pl.multiple_of(c * CLIP + w * SPOT, SPOT), SPOT)
+                v = qkv_ref[spots, g * D + 2 * LANES : g * D + D]
+                do = stack_heads(att_ref[spots, g * LANES : g * LANES + LANES], masks)
+                p = probs_ref[c, w, g]
+                pf = p.astype(F32)
+                dp = nt(v, do)
+                inner = jnp.sum(pf * dp, axis=0, keepdims=True)
+                ds = jnp.where(time_ref[w] < frames, pf * (dp - inner), 0.0)
+                tacc = ds if tacc is None else tacc + ds
+                du_ref[w * SPOT : w * SPOT + SPOT, g * 256 : g * 256 + 256] = ds.astype(BF16)
+                dj_ref[spots, g * D + 2 * LANES : g * D + D] = nn(p, do).astype(BF16)
+            tacc_ref[g] += tacc
+        for g in range(GROUPS):
+            for w in range(4):
+                spots = pl.ds(pl.multiple_of(c * CLIP + w * SPOT, SPOT), SPOT)
+                cq = slice(g * D, g * D + LANES)
+                ck = slice(g * D + LANES, g * D + 2 * LANES)
+                q = qkv_ref[spots, cq]
+                k = qkv_ref[spots, ck]
+                ds = du_ref[w * SPOT : w * SPOT + SPOT, g * 256 : g * 256 + 256]
+                dj_ref[spots, cq] = (pick_heads(tn(ds, k)) * SCALE).astype(BF16)
+                dj_ref[spots, ck] = (nn(ds, stack_heads(q, masks)) * SCALE).astype(BF16)
+        gqv_ref[...] += fold(dj_ref[rows, :].astype(F32))
+        return carry
+
+    def entry_back(c, carry):
+        rows = clip_rows(c, PAIR)
+        clip = [clip_rows(2 * c + part) for part in range(2)]
+        x = jnp.concatenate([to_windows(tok_ref[r, :].astype(F32)) for r in clip], axis=0)
+        n, inv = normalize(x)
+        dn1 = nt(dj_ref[rows, :], wqkv_ref[...])
+        rows_ref[0] += fold(dn1 * n)
+        rows_ref[1] += fold(dn1)
+        din = dmid_ref[rows, :] + norm_back(dn1, n, inv, rowp_ref[0:1])
+        for part in range(2):
+            r = clip[part]
+            dmid_ref[r, :] = from_windows(din[part * CLIP : part * CLIP + CLIP])
+        pltpu.make_async_copy(dmid_ref.at[rows, :], din_hbm.at[rows, :], osems.at[1, c]).start()
+        return carry
+
     load_tok = pltpu.make_async_copy(tok_hbm, tok_ref, osems.at[2, 0])
     load_og = pltpu.make_async_copy(og_hbm, og_ref, osems.at[2, 1])
     load_tok.start()
     load_og.start()
-    greet()
     small = [
         remote(sown_ref, small_ref.at[head], ssems.at[0, d], ssems.at[1, d], win, (head + d + 1) % 4)
         for d in range(3)
     ]
     own_small = pltpu.make_async_copy(sown_ref, small_ref.at[head], ssems.at[2, 0])
-    gq_w = gather_stages(qown_ref, wqkv_ref, True, wsems.at[0])
+    gq_w = gather_stages(D, wqkv_ref, True, wsems.at[0])
     others = [
-        gather_stages(own, full, wide, wsems.at[1 + i])
-        for i, (own, full, wide) in enumerate(
-            ((pown_ref, wproj_ref, False), (aown_ref, w1_ref, True), (bown_ref, w2_ref, False))
+        gather_stages(rows, full, wide, wsems.at[1 + i])
+        for i, (rows, full, wide) in enumerate(
+            ((LANES, wproj_ref, False), (D, w1_ref, True), (D, w2_ref, False))
         )
     ]
+    for p in range(3):
+        part = qraw_ref[:, p, :].astype(BF16).astype(F32)
+        part = jnp.concatenate([part, jnp.zeros((D, LANES - part.shape[1]), F32)], axis=1)
+        wqkv_ref[:, pl.ds(pl.multiple_of(head * D + p * LANES, LANES), LANES)] = part.astype(BF16)
+    greet()
     gq_w[0]()
+    width = qvb_ref.shape[1]
+    sown_ref[...] = jnp.zeros_like(sown_ref)
+    sown_ref[0:1, :width] = qvb_ref[0:1, :]
+    sown_ref[0:1, LANES : LANES + width] = qvb_ref[1:2, :]
+    turn_ref[...] = jnp.zeros_like(turn_ref)
+    turn_ref[: table_ref.shape[0], :PER] = table_ref[...]
+    sown_ref[1 : 1 + PER, :256] = turn_ref[...].T[:PER, :]
+    sown_ref[5:6, :] = fc1b_ref[...]
     own_small.start()
     for copy in small:
         copy.start()
+    width = praw_ref.shape[0]
+    tall = jnp.concatenate([praw_ref[...], jnp.zeros((LANES - width, D), F32)])
+    wproj_ref[pl.ds(pl.multiple_of(head * LANES, LANES), LANES), :] = tall.astype(BF16)
+    shard = pl.ds(pl.multiple_of(head * D, LANES), D)
+    w1_ref[:, shard] = araw_ref[...].astype(BF16)
+    w2_ref[shard, :] = braw_ref[...].astype(BF16)
+    for k in others:
+        k[0]()
     for wt in range(2):
         for wf in range(2):
             time_ref[wt * 2 + wf] = key_times(wt, wf)
-    for ref in (g1_ref, g2_ref, gp_ref, rows_ref, gb_ref, gqv_ref, tacc_ref, esbuf, lsbuf):
+    for ref in (rows_ref, gb_ref, gqv_ref, tacc_ref, esbuf, lsbuf):
         ref[...] = jnp.zeros_like(ref)
+    load_tok.wait()
+    lax.fori_loop(0, clips // 2, enter, 0)
     gq_w[1]()
     own_small.wait()
     for copy in small:
@@ -548,165 +723,50 @@
         b1_ref[0:1, g * D : g * D + D] = small_ref[g, 5:6, :]
     build_bias(small_ref, bias_ref)
     gq_w[2]()
+    gq_w[3]()
     for k in others:
-        k[0]()
-    gq_w[3]()
-    load_tok.wait()
-
-    def attend(c, carry):
-        rows = clip_rows(c)
-        frames = frames_ref[c]
-        x = to_windows(tok_ref[rows, :].astype(F32))
-        n1, _ = normalize(x)
-        n1 = (n1 * rowp_ref[0:1] + rowp_ref[1:2]).astype(BF16)
-        for part in range(3):
-            cols = slice(part * 512, part * 512 + 512)
-            y = nn(n1, wqkv_ref[:, cols]) + bqkv_ref[0:1, cols]
-            qkv_ref[rows, cols] = y.astype(BF16)
-        masks = head_masks(BF16)
-        for w in range(4):
-            spots = pl.ds(pl.multiple_of(c * CLIP + w * SPOT, SPOT), SPOT)
-            for g in range(GROUPS):
-                q = qkv_ref[spots, g * D : g * D + LANES]
-                k = qkv_ref[spots, g * D + LANES : g * D + 2 * LANES]
-                v = qkv_ref[spots, g * D + 2 * LANES : g * D + D]
-                s = nt(k, stack_heads(q, masks)) * SCALE + bias_ref[g]
-                s = jnp.where(time_ref[w] < frames, s, MASKED)
-                e = jnp.exp(s - jnp.max(s, axis=0, keepdims=True))
-                p = (e * (1.0 / jnp.sum(e, axis=0, keepdims=True))).astype(BF16)
-                probs_ref[c, w, g] = p
-                o = pick_heads(tn(p, v))
-                att_ref[spots, g * LANES : g * LANES + LANES] = o.astype(BF16)
-        return carry
-
-    def feed(c, carry):
-        rows = clip_rows(c)
-        x = to_windows(tok_ref[rows, :].astype(F32))
-        og = to_windows(og_ref[rows, :].astype(F32))
-        att = att_ref[rows, :]
-        middle = x + nn(att, wproj_ref[...]) + rowp_ref[4:5]
-        nrm, inv = normalize(middle)
-        n2 = (nrm * rowp_ref[2:3] + rowp_ref[3:4]).astype(BF16)
-        n2t = n2.T
-        ogb = og.astype(BF16)
-        ogt = ogb.T
-        ffn = None
-        dn2 = None
-        for j in range(FF // CHUNK):
-            cols = slice(j * CHUNK, j * CHUNK + CHUNK)
-            u = nn(n2, w1_ref[:, cols]) + b1_ref[0:1, cols]
-            phi, dens = gelu_parts(u)
-            hid = (u * phi).astype(BF16)
-            du = ((phi + u * dens) * nt(ogb, w2_ref[cols, :])).astype(BF16)
-            gb_ref[:, cols] += fold(du.astype(F32))
-            g1_ref[:, cols] += nn(n2t, du)
-            g2_ref[:, cols] += nn(ogt, hid)
-            a = nn(hid, w2_ref[cols, :])
-            b = nt(du, w1_ref[:, cols])
-            ffn = a if ffn is None else ffn + a
-            dn2 = b if dn2 is None else dn2 + b
-        out_ref[rows, :] = from_windows(middle + ffn + rowp_ref[5:6])
-        pltpu.make_async_copy(out_ref.at[rows, :], out_hbm.at[rows, :], osems.at[0, c]).start()
-        dmid = og + norm_back(dn2, nrm, inv, rowp_ref[2:3])
-        dmid_ref[rows, :] = dmid
-        dbr = dmid.astype(BF16)
-        rows_ref[2] += fold(dn2 * nrm)
-        rows_ref[3] += fold(dn2)
-        rows_ref[4] += fold(dbr.astype(F32))
-        rows_ref[5] += fold(og)
-        attt = att.T
-        for g in range(GROUPS):
-            gp_ref[:, g * D : g * D + D] += nn(attt[g * LANES : g * LANES + LANES], dbr)
-        att_ref[rows, :] = nt(dbr, wproj_ref[...]).astype(BF16)
-        return carry
-
-    def attend_back(c, carry):
-        rows = clip_rows(c)
-        frames = frames_ref[c]
-        masks = head_masks(BF16)
-        for g in range(GROUPS):
-            tacc = None
-            for w in range(4):
-                spots = pl.ds(pl.multiple_of(c * CLIP + w * SPOT, SPOT), SPOT)
-                cq = slice(g * D, g * D + LANES)
-                ck = slice(g * D + LANES, g * D + 2 * LANES)
-                cv = slice(g * D + 2 * LANES, g * D + D)
-                q = qkv_ref[spots, cq]
-                k = qkv_ref[spots, ck]
-                v = qkv_ref[spots, cv]
-                do = stack_heads(att_ref[spots, g * LANES : g * LANES + LANES], masks)
-                p = probs_ref[c, w, g]
-                pf = p.astype(F32)
-                dp = nt(v, do)
-                inner = jnp.sum(pf * dp, axis=0, keepdims=True)
-                ds = jnp.where(time_ref[w] < frames, pf * (dp - inner), 0.0)
-                tacc = ds if tacc is None else tacc + ds
-                ds = ds.astype(BF16)
-                qkv_ref[spots, cq] = (pick_heads(tn(ds, k)) * SCALE).astype(BF16)
-                qkv_ref[spots, ck] = (nn(ds, stack_heads(q, masks)) * SCALE).astype(BF16)
-                qkv_ref[spots, cv] = nn(p, do).astype(BF16)
-            tacc_ref[g] += tacc
-        gqv_ref[...] += fold(qkv_ref[rows, :].astype(F32))
-        n, _ = normalize(to_windows(tok_ref[rows, :].astype(F32)))
-        n1t = (n * rowp_ref[0:1] + rowp_ref[1:2]).astype(BF16).T
-        g1_ref[...] += nn(n1t, qkv_ref[rows, :])
-        return carry
-
-    def entry_back(c, carry):
-        rows = clip_rows(c)
-        n, inv = normalize(to_windows(tok_ref[rows, :].astype(F32)))
-        dn1 = nt(qkv_ref[rows, :], wqkv_ref[...])
-        rows_ref[0] += fold(dn1 * n)
-        rows_ref[1] += fold(dn1)
-        din = dmid_ref[rows, :] + norm_back(dn1, n, inv, rowp_ref[0:1])
-        dmid_ref[rows, :] = from_windows(din)
-        pltpu.make_async_copy(dmid_ref.at[rows, :], din_hbm.at[rows, :], osems.at[1, c]).start()
-        return carry
+        k[1]()
 
     def span(share):
         return clips * share // 8
 
-    lax.fori_loop(0, span(2), attend, 0)
-    for k in others:
-        k[1]()
-    lax.fori_loop(span(2), span(5), attend, 0)
+    lax.fori_loop(0, clips // 2, project, 0)
+    lax.fori_loop(0, clips, attend, 0)
     for k in others:
         k[2]()
-    lax.fori_loop(span(5), span(8), attend, 0)
     for k in others:
         k[3]()
     load_og.wait()
-    lax.fori_loop(0, clips, feed, 0)
-
-    early = reduce_stages(ebuf, core_e, cell_e, up_e, head_e, efinal, rsems.at[0])
+    lax.fori_loop(0, clips // 2, feed, 0)
+    feed_grads()
+
+    early = reduce_stages(ebuf, core_e, cell_e, up_e, head_e, early_ref, rsems.at[0])
     early_small = small_stages(esbuf, core_es, cell_es, up_es, head_es, esmall_ref, rsems.at[1])
-    late = reduce_stages(lbuf, core_l, cell_l, up_l, head_l, lfinal, rsems.at[2])
+    late = reduce_stages(lbuf, core_l, cell_l, up_l, head_l, late_ref, rsems.at[2])
     late_small = small_stages(lsbuf, core_ls, cell_ls, up_ls, head_ls, lsmall_ref, rsems.at[3])
-    ebuf[0:D, :] = g1_ref[...].astype(BF16)
-    ebuf[D : 2 * D, :] = g2_ref[...].astype(BF16)
-    ebuf[2 * D : 2 * D + LANES, :] = gp_ref[...].astype(BF16)
     early[0]()
-    g1_ref[...] = jnp.zeros_like(g1_ref)
+    lax.fori_loop(0, span(4) // 2, feed_out, 0)
+    early[1]()
+    lax.fori_loop(span(4) // 2, clips // 2, feed_out, 0)
+    branch_grads()
     esbuf[0:1, :] = jnp.sum(gb_ref[...], axis=0, keepdims=True)
     for r in range(4):
         line = jnp.sum(rows_ref[2 + r], axis=0, keepdims=True)
         for g in range(GROUPS):
             esbuf[1 + r : 2 + r, g * D : g * D + D] = line
     early_small[0]()
-    lax.fori_loop(0, span(1), attend_back, 0)
-    early[1]()
+    lax.fori_loop(0, span(2), attend_back, 0)
     early_small[1]()
-    lax.fori_loop(span(1), span(4), attend_back, 0)
+    lax.fori_loop(span(2), span(4), attend_back, 0)
     early[2]()
     early_small[2]()
-    lax.fori_loop(span(4), span(6), attend_back, 0)
+    lax.fori_loop(span(4), span(8), attend_back, 0)
+    for j in range(3):
+        cols = slice(j * 512, j * 512 + 512)
+        lbuf[0:D, cols] = nn(n1t_ref[...], dj_ref[:, cols]).astype(BF16)
     early[3]()
+    late[0]()
     early_small[3]()
-    lax.fori_loop(span(6), span(7), attend_back, 0)
-    early[4]()
-    lax.fori_loop(span(7), span(8), attend_back, 0)
-    lbuf[...] = g1_ref[...].astype(BF16)
-    late[0]()
     for g in range(GROUPS):
         cols = slice(g * D, g * D + LANES)
         lsbuf[0:1, cols] = jnp.sum(gqv_ref[:, cols], axis=0, keepdims=True)
@@ -714,25 +774,24 @@
         lsbuf[0:1, cols] = jnp.sum(gqv_ref[:, cols], axis=0, keepdims=True)
     fold_table(tacc_ref, lsbuf)
     late[1]()
-    early[5]()
-    lax.fori_loop(0, span(6), entry_back, 0)
-    late[2]()
-    lax.fori_loop(span(6), span(8), entry_back, 0)
+    lax.fori_loop(0, span(4) // 2, entry_back, 0)
+    early[4]()
+    lax.fori_loop(span(4) // 2, clips // 2, entry_back, 0)
     for r in range(2):
         line = jnp.sum(rows_ref[r], axis=0, keepdims=True)
         for g in range(GROUPS):
             lsbuf[4 + r : 5 + r, g * D : g * D + D] = line
     late_small[0]()
+    early[5]()
+    late[2]()
+    late_small[1]()
     late[3]()
-    late_small[1]()
+    late_small[2]()
     late[4]()
-    late_small[2]()
+    late_small[3]()
     late[5]()
-    late_small[3]()
-    early_ref[...] = efinal[...]
-    late_ref[...] = lfinal[...]
     square = jnp.zeros((8, D), F32)
-    for ref in (efinal, lfinal):
+    for ref in (early_ref, late_ref):
         value = ref[...].astype(F32)
         square = square + fold(value * value)
     es, ls = esmall_ref[...], lsmall_ref[...]
@@ -755,12 +814,13 @@
     norm_ref[...] = jnp.sqrt(total + jnp.sum(common, keepdims=True))
 
     def finish(c, carry):
-        rows = clip_rows(c)
-        pltpu.make_async_copy(out_ref.at[rows, :], out_hbm.at[rows, :], osems.at[0, c]).wait()
+        rows = clip_rows(c, PAIR)
         pltpu.make_async_copy(dmid_ref.at[rows, :], din_hbm.at[rows, :], osems.at[1, c]).wait()
         return carry
 
-    lax.fori_loop(0, clips, finish, 0)
+    lax.fori_loop(0, clips // 2, finish, 0)
+    for c in range(max(clips // 2 - 2, 0), clips // 2):
+        send_out(c).wait()
 
 
 def fold_table(tacc_ref, lsbuf):
@@ -789,7 +849,7 @@
                 ]
 
 
-def block(frames, tok, og, qown, pown, aown, bown, sown, rowp):
+def block(frames, tok, og, qraw, praw, araw, braw, qvb, table, fc1b, rowp):
     rows = tok.shape[0]
     clips = rows // CLIP
     upper = max(lax.axis_size("win") // 8, 1).bit_length() - 1
@@ -799,10 +859,10 @@
     spec = pl.BlockSpec
     inside = lambda: spec(memory_space=vmem)
     outside = lambda: spec(memory_space=pl.ANY)
-    early, late = 2 * D + LANES, D
+    early, late = 2 * D, D + LANES
     return pl.pallas_call(
         partial(block_kernel, clips),
-        in_specs=[spec(memory_space=pltpu.SMEM), outside(), outside()] + [inside()] * 6,
+        in_specs=[spec(memory_space=pltpu.SMEM), outside(), outside()] + [inside()] * 8,
         out_specs=[outside(), outside()] + [inside()] * 5,
         out_shape=[
             shape((rows, D), F32),
@@ -814,11 +874,18 @@
             shape((8, LANES), F32),
         ],
         scratch_shapes=[
+            vmem((8, D), F32),
+            vmem((256, LANES), F32),
             vmem((rows, D), BF16),
             vmem((rows, D), BF16),
+            vmem((2 * PAIR, D), F32),
             vmem((rows, D), F32),
-            vmem((rows, D), F32),
+            vmem((D, rows), BF16),
+            vmem((D, rows), BF16),
+            vmem((D, rows), BF16),
             vmem((rows, 1536), BF16),
+            vmem((rows, 1536), BF16),
+            vmem((rows, FF), BF16),
             vmem((clips, 4, GROUPS, SPOT, PER * SPOT), BF16),
             vmem((rows, 512), BF16),
             vmem((D, 1536), BF16),
@@ -830,9 +897,6 @@
             vmem((8, FF), F32),
             vmem((GROUPS, SPOT, PER * SPOT), F32),
             vmem((4, SPOT, PER * SPOT), jnp.int32),
-            vmem((D, FF), F32),
-            vmem((D, FF), F32),
-            vmem((LANES, 1536), F32),
             vmem((6, 8, D), F32),
             vmem((8, FF), F32),
             vmem((8, 1536), F32),
@@ -857,8 +921,6 @@
             vmem((3, late // 8, D), BF16),
             vmem((4, 8, D), F32),
             vmem((4, 8, D), F32),
-            vmem((early, D), BF16),
-            vmem((late, D), BF16),
             vmem((4, 8, LANES), F32),
             sems((4, 11, 3)),
             sems((3, 3)),
@@ -869,19 +931,98 @@
         compiler_params=pltpu.CompilerParams(
             vmem_limit_bytes=VMEM_LIMIT, collective_id=0, has_side_effects=True
         ),
-    )(frames, tok, og, qown, pown, aown, bown, sown, rowp)
+    )(frames, tok, og, qraw, praw, araw, braw, qvb, table, fc1b, rowp)
 
 
 def adam_step(weight, gradient, moment, second, factor, rate):
     clipped = gradient * factor
     moment_new = BETA_ONE * moment + (1.0 - BETA_ONE) * clipped
     second_new = BETA_TWO * second + (1.0 - BETA_TWO) * clipped * clipped
-    moment_hat = moment_new / (1.0 - BETA_ONE**STEP)
-    second_hat = second_new / (1.0 - BETA_TWO**STEP)
+    moment_hat = moment_new * (1.0 / (1.0 - BETA_ONE**STEP))
+    second_hat = second_new * (1.0 / (1.0 - BETA_TWO**STEP))
     master = weight - rate * (
         moment_hat / (jnp.sqrt(second_hat) + ADAM_EPS) + WEIGHT_DECAY * weight
     )
     return (gradient, moment_new, second_new, master)
+
+
+def step_kernel(*refs):
+    norm_ref, e1_ref, e2_ref, ep_ref, late_ref, es_ref, ls_ref = refs[:7]
+    weights, firsts, seconds = refs[7:15], refs[15:23], refs[23:31]
+    gn_ref, outs = refs[31], refs[32:]
+    norm = norm_ref[0:1, 0:1]
+    factor = jnp.minimum(1.0, CLIP_LIMIT / (norm + 1e-06))
+
+    def put(i, gradient, rate, at=(slice(None), slice(None))):
+        values = adam_step(weights[i][at], gradient, firsts[i][at], seconds[i][at], factor, rate)
+        for k in range(4):
+            outs[4 * i + k][at] = values[k]
+
+    late = late_ref[...].astype(F32)
+    width = weights[0].shape[2]
+    for p in range(3):
+        at = (slice(None), p, slice(None))
+        put(0, late[:, p * LANES : p * LANES + width], LEARN_RATE, at)
+    put(3, ep_ref[...].astype(F32), LEARN_RATE)
+    put(4, e1_ref[...].astype(F32), LEARN_RATE)
+    put(6, e2_ref[...].astype(F32).T, LEARN_RATE)
+
+    @pl.when(pl.program_id(0) == 0)
+    def _():
+        gn_ref[...] = norm
+        both = jnp.concatenate([ls_ref[0:1, :width], ls_ref[0:1, 2 * LANES : 2 * LANES + width]])
+        put(1, both, LEARN_RATE)
+        lines = []
+        for h in range(PER):
+            pieces = []
+            for half in range(2):
+                at = h * 256 + half * LANES
+                pieces.append(ls_ref[1 + at // D : 2 + at // D, at % D : at % D + LANES])
+            lines.append(jnp.concatenate(pieces, axis=1))
+        lines = jnp.concatenate(lines + [jnp.zeros((8 - PER, 256), F32)])
+        offsets = weights[2].shape[0]
+        flip = iota((256, 256), 0) + iota((256, 256), 1) == offsets - 1
+        flip = jnp.where(flip, 1.0, 0.0).astype(F32).astype(BF16)
+        table = None
+        for part in split_three(lines):
+            term = nt(flip, part)
+            table = term if table is None else table + term
+        put(2, table[:offsets, :PER], ROW_RATE)
+        put(5, es_ref[0:1, :], LEARN_RATE)
+        put(7, jnp.concatenate([ls_ref[4:6, :], es_ref[1:5, :]]), ROW_RATE)
+
+
+def take_step(norm, early, late, esmall, lsmall, weights, firsts, seconds):
+    cuts = 3
+    spec = pl.BlockSpec
+    full = lambda a: spec(a.shape, lambda i: (0,) * a.ndim)
+    third = lambda a: spec(
+        (a.shape[0] // cuts,) + a.shape[1:], lambda i: (i,) + (0,) * (a.ndim - 1)
+    )
+    each = [
+        third(a) if k in (0, 3, 4, 6) else full(a) for k, a in enumerate(weights)
+    ]
+    rows = D // cuts
+    tall = weights[3].shape[0] // cuts
+    shape = jax.ShapeDtypeStruct
+    outs = pl.pallas_call(
+        step_kernel,
+        grid=(cuts,),
+        in_specs=[
+            full(norm),
+            spec((rows, D), lambda i: (i, 0)),
+            spec((D, rows), lambda i: (1, i)),
+            spec((tall, D), lambda i: (D // tall + i, 0)),
+            spec((rows, D), lambda i: (i, 0)),
+            full(esmall),
+            full(lsmall),
+        ]
+        + each * 3,
+        out_specs=[spec((1, 1), lambda i: (0, 0))] + [e for e in each for _ in range(4)],
+        out_shape=[shape((1, 1), F32)] + [shape(a.shape, F32) for a in weights for _ in range(4)],
+        compiler_params=pltpu.CompilerParams(vmem_limit_bytes=VMEM_LIMIT),
+    )(norm, early, early, late, late, esmall, lsmall, *weights, *firsts, *seconds)
+    return outs[0], outs[1:]
 
 
 def shards(
@@ -913,39 +1054,19 @@
     rows_first,
     rows_second,
 ):
-    clips = tokens.shape[0] // CLIP
-    local = rel_table.shape[1] * HDIM
-    offsets = rel_table.shape[0]
-    frames = lax.dynamic_slice(clip_frames, (lax.axis_index("head") * clips,), (clips,))
-    pad = LANES - local
-    qown = jnp.pad(qkv_weight.astype(BF16), ((0, 0), (0, 0), (0, pad))).reshape(D, D)
-    pown = jnp.pad(proj_weight.astype(BF16), ((0, pad), (0, 0)))
-    aown, bown = fc1_weight.astype(BF16), fc2_weight.astype(BF16)
-    bias_row = jnp.pad(qv_bias, ((0, 1), (0, pad))).reshape(1, D)
-    sown = jnp.concatenate(
-        [
-            bias_row,
-            jnp.pad(rel_table.T, ((0, 0), (0, D - offsets))),
-            fc1_bias[None],
-            jnp.zeros((2, D), F32),
-        ]
-    )
+    line = lambda v: v.reshape(1, -1)
     output, input_grad, early, late, esmall, lsmall, norm = block(
-        frames, tokens, out_grad, qown, pown, aown, bown, sown, row_params
-    )
-    early, late = early.astype(F32), late.astype(F32)
-    grad_norm = norm[0, 0]
-    factor = jnp.minimum(1.0, CLIP_LIMIT / (grad_norm + 1e-06))
-    table = lsmall[1:4].reshape(-1)[: PER * 256].reshape(PER, 256)
-    gradients = (
-        late.reshape(D, 3, LANES)[..., :local],
-        lsmall[0].reshape(3, LANES)[::2, :local],
-        table[:, :offsets][:, ::-1].T,
-        early[2 * D : 2 * D + local],
-        early[:D],
-        esmall[0],
-        early[D : 2 * D].T,
-        jnp.concatenate([lsmall[4:6], esmall[1:5]]),
+        clip_frames,
+        tokens,
+        out_grad,
+        qkv_weight,
+        proj_weight,
+        fc1_weight,
+        fc2_weight,
+        qv_bias,
+        rel_table,
+        line(fc1_bias),
+        row_params,
     )
     weights = (
         qkv_weight,
@@ -953,7 +1074,7 @@
         rel_table,
         proj_weight,
         fc1_weight,
-        fc1_bias,
+        line(fc1_bias),
         fc2_weight,
         row_params,
     )
@@ -963,7 +1084,7 @@
         table_first,
         proj_first,
         fc1_first,
-        fc1b_first,
+        line(fc1b_first),
         fc2_first,
         rows_first,
     )
@@ -973,24 +1094,13 @@
         table_second,
         proj_second,
         fc1_second,
-        fc1b_second,
+        line(fc1b_second),
         fc2_second,
         rows_second,
     )
-    rates = (
-        LEARN_RATE,
-        LEARN_RATE,
-        ROW_RATE,
-        LEARN_RATE,
-        LEARN_RATE,
-        LEARN_RATE,
-        LEARN_RATE,
-        ROW_RATE,
-    )
-    updated = []
-    for weight, gradient, moment, second, rate in zip(weights, gradients, firsts, seconds, rates):
-        updated.extend(adam_step(weight, gradient, moment, second, factor, rate))
-    return (output, input_grad, grad_norm, *updated)
+    grad_norm, updated = take_step(norm, early, late, esmall, lsmall, weights, firsts, seconds)
+    updated = [v.reshape(-1) if 20 <= k < 24 else v for k, v in enumerate(updated)]
+    return (output, input_grad, grad_norm.reshape(()), *updated)
 
 
 def solution(mesh):

time: 209 us -> 174 us (0.83)
  Pallas kernels: 159 us -> 133 us
  other arithmetic: 13.2 us -> 5.09 us
    pallas_call x1, Pallas kernels: 159 us -> 121 us  [block(): pl.pallas_call(partial(block_kernel, clips), in_specs=[spec(memory_space=...]
    pallas_call x0 -> x1, Pallas kernels: none -> 11.8 us  [take_step(): pl.pallas_call(step_kernel, grid=(cuts,), in_specs=[full(norm), spec((row...]
    sub x7 -> x0, other arithmetic: 9.86 us -> none  [adam_step(): weight - rate * (moment_hat / (jnp.sqrt(second_hat) + ADAM_EPS) + WEIGHT_...]
    pallas_call x0 -> x4, other arithmetic: none -> 5.09 us  [take_step(): pl.pallas_call(step_kernel, grid=(cuts,), in_specs=[full(norm), spec((row...]
    unnamed x77 -> x20, local copies, waits for them, and re-layouts: 26.8 us -> 30.5 us
    slice x8 -> x0, local copies, waits for them, and re-layouts: 2.82 us -> none  [the longest x1 1.19 us: shards(): grad_norm = norm[0, 0]]
    reshape x3, local copies, waits for them, and re-layouts: 0.92 us -> 3.73 us  [shards(): line = lambda v: v.reshape(1, -1)]
    convert_element_type x5 -> x0, other arithmetic: 2.64 us -> none  [the longest x2 1.49 us: shards(): aown, bown = (fc1_weight.astype(BF16), fc2_weight.astype(BF16))]
where the time goes in v4:
time: 174 us; the launch traced here: 173 us
  Pallas kernels  133 us (76%)
  local copies, waits for them, and re-layouts  34.2 us (20%)
  other arithmetic  5.09 us (3%)
    pallas_call x1, Pallas kernels, block(): pl.pallas_call(partial(block_kernel, clips), in_specs=[spec(memory_space=...  121 us
    unnamed x20, local copies, waits for them, and re-layouts  30.5 us
    pallas_call x1, Pallas kernels, take_step(): pl.pallas_call(step_kernel, grid=(cuts,), in_specs=[full(norm), spec((row...  11.8 us
    pallas_call x4, other arithmetic, take_step(): pl.pallas_call(step_kernel, grid=(cuts,), in_specs=[full(norm), spec((row...  5.09 us
    reshape x3, local copies, waits for them, and re-layouts, shards(): line = lambda v: v.reshape(1, -1)  3.73 us

profile of v4, /device:TPU:0, one launch (start us, length us, event | category | flops | bytes accessed | tf_op | source)
XLA Modules:
  0.0 172.9 jit_solution(5883911946818209654)
XLA Ops:
  0.7 1.2 reshape.95.fc1b_ref.refs_12_
  1.9 1.2 reshape.96.refs_20_
  3.2 1.2 reshape.97.refs_28_
  4.4 1.5 copy.63.table_ref.refs_9_
  5.9 1.5 copy.67.refs_17_
  7.3 1.5 copy.69.refs_25_
  8.8 2.2 %copy.62.qraw_ref.refs_7_ = f32[384,3,96]{2,1,0:T(4,128)} copy(f32[384,3,96]{0,2,1:T(8,128)} %param.30) | data formatting | bytes 884736 | tf_op args[3]
  11.0 2.2 %copy.66.refs_15_ = f32[384,3,96]{2,1,0:T(4,128)} copy(f32[384,3,96]{0,2,1:T(8,128)} %param.38) | data formatting | bytes 884736 | tf_op args[11]
  13.1 2.2 %copy.68.refs_23_ = f32[384,3,96]{2,1,0:T(4,128)} copy(f32[384,3,96]{0,2,1:T(8,128)} %param.39) | data formatting | bytes 884736 | tf_op args[12]
  15.3 121.0 %shard_map.530 = (f32[2048,384]{1,0:T(8,128)}, f32[2048,384]{1,0:T(8,128)}, bf16[768,384]{1,0:T(8,128)(2,1)}, bf16[512,384]{1,0:T(8,128)(2,1)}, f32[8,384]{1,0:T...) custom-call(s32[32]{0:T(128)} %frames_ref.1, bf16[2048,384]{1,0:T(8,128)(2,1)} %tok_hbm.1, bf16[2048,384]{1,0:T(8,128)(2,1)} %og_hbm.1, ...), custom_call_target="tpu_custom_call" | custom-call | tf_op jit(solution)/shard_map/pallas_call | solution.py:863
  136.3 11.8 %shard_map.531 = (f32[1,1]{1,0:T(1,128)}, f32[384,3,96]{2,1,0:T(4,128)}, f32[384,3,96]{2,1,0:T(4,128)}, f32[384,3,96]{2,1,0:T(4,128)}, f32[384,3,96]{2,1,0:T(4,1...) custom-call(f32[8,128]{1,0:T(8,128)} %get-tuple-element.77.refs_0_, ...), custom_call_target="tpu_custom_call" | custom-call | tf_op jit(solution)/shard_map/pallas_call | solution.py:1008
  148.1 0.0 copy-start.1
  148.1 2.3 %copy.70 = f32[384,3,96]{0,2,1:T(8,128)} copy(f32[384,3,96]{2,1,0:T(4,128)} %get-tuple-element.118) | data formatting | bytes 884736
  150.4 1.3 reduce
  151.7 1.3 reduce.1
  153.0 1.3 reduce.2
  154.2 1.3 reduce.3
  155.5 1.6 copy.74
  157.1 1.6 copy.75
  158.7 1.6 copy.76
  160.2 1.6 copy.77
  161.8 2.1 %copy.71 = f32[384,3,96]{0,2,1:T(8,128)} copy(f32[384,3,96]{2,1,0:T(4,128)} %get-tuple-element.119) | data formatting | bytes 884736
  163.9 2.1 %copy.72 = f32[384,3,96]{0,2,1:T(8,128)} copy(f32[384,3,96]{2,1,0:T(4,128)} %get-tuple-element.120) | data formatting | bytes 884736
  166.0 2.1 %copy.73 = f32[384,3,96]{0,2,1:T(8,128)} copy(f32[384,3,96]{2,1,0:T(4,128)} %get-tuple-element.121) | data formatting | bytes 884736
  168.2 0.0 copy-done.1
  168.2 0.0 copy-start
  168.2 1.7 copy.80
  169.8 1.4 copy-done
  171.2 1.7 copy.81
Async XLA Ops:
  148.1 20.0 %copy-start.1 = (f32[2048,384]{1,0:T(8,128)S(1)}, f32[2048,384]{1,0:T(8,128)}, u32[]{:S(2)}) copy-start(f32[2048,384]{1,0:T(8,128)} %get-tuple-element.185) | copy-start | bytes 9437188
  168.2 3.0 %copy-start = (f32[2048,384]{1,0:T(8,128)S(1)}, f32[2048,384]{1,0:T(8,128)}, u32[]{:S(2)}) copy-start(f32[2048,384]{1,0:T(8,128)} %get-tuple-element.186) | copy-start | bytes 9437188

commit v5 on v4

--- a/solution.py
+++ b/solution.py
@@ -449,23 +449,22 @@
     rowp_ref,
     out_hbm,
     din_hbm,
-    early_ref,
+    one_ref,
+    two_ref,
     late_ref,
     esmall_ref,
     lsmall_ref,
     norm_ref,
     sown_ref,
-    turn_ref,
     tok_ref,
     og_ref,
-    out_ref,
+    mid_ref,
     dmid_ref,
     n1t_ref,
-    n2t_ref,
-    ogt_ref,
+    n2_ref,
     qkv_ref,
     dj_ref,
-    du_ref,
+    hid_ref,
     probs_ref,
     att_ref,
     wqkv_ref,
@@ -481,23 +480,28 @@
     gb_ref,
     gqv_ref,
     tacc_ref,
-    ebuf,
+    buf_1,
+    buf_2,
     lbuf,
     esbuf,
     lsbuf,
-    core_e,
+    core_1,
+    core_2,
     core_l,
     core_es,
     core_ls,
-    cell_e,
+    cell_1,
+    cell_2,
     cell_l,
     cell_es,
     cell_ls,
-    up_e,
+    up_1,
+    up_2,
     up_l,
     up_es,
     up_ls,
-    head_e,
+    head_1,
+    head_2,
     head_l,
     head_es,
     head_ls,
@@ -524,7 +528,7 @@
         rows = clip_rows(c, PAIR)
         for part in range(3):
             cols = slice(part * 512, part * 512 + 512)
-            y = nn(att_ref[rows, :D], wqkv_ref[:, cols]) + bqkv_ref[0:1, cols]
+            y = nt(att_ref[rows, :D], wqkv_ref[cols, :]) + bqkv_ref[0:1, cols]
             qkv_ref[rows, cols] = y.astype(BF16)
         return carry
 
@@ -550,72 +554,83 @@
         return carry
 
     def send_out(c):
-        return pltpu.make_async_copy(
-            out_ref.at[clip_rows(c % 2, PAIR), :], out_hbm.at[clip_rows(c, PAIR), :], osems.at[0, c]
-        )
-
-    def feed(c, carry):
+        rows = clip_rows(c, PAIR)
+        return pltpu.make_async_copy(mid_ref.at[rows, :], out_hbm.at[rows, :], osems.at[0, c])
+
+    def widen(c, carry):
         rows = clip_rows(c, PAIR)
         clip = [clip_rows(2 * c + part) for part in range(2)]
         x = jnp.concatenate([to_windows(tok_ref[r, :].astype(F32)) for r in clip], axis=0)
         og = jnp.concatenate([to_windows(og_ref[r, :].astype(F32)) for r in clip], axis=0)
+        og_ref[rows, :] = og.astype(BF16)
+        rows_ref[5] += fold(og)
         middle = x + nn(att_ref[rows, :], wproj_ref[...]) + rowp_ref[4:5]
-        nrm, inv = normalize(middle)
+        mid_ref[rows, :] = middle
+        nrm, _ = normalize(middle)
         n2 = (nrm * rowp_ref[2:3] + rowp_ref[3:4]).astype(BF16)
-        n2t_ref[:, rows] = n2.T
-        ogb = og.astype(BF16)
-        ogt_ref[:, rows] = ogb.T
+        n2_ref[rows, :] = n2
         for j in range(FF // CHUNK):
             cols = slice(j * CHUNK, j * CHUNK + CHUNK)
             u = nn(n2, w1_ref[:, cols]) + b1_ref[0:1, cols]
             phi, dens = gelu_parts(u)
-            dj_ref[rows, cols] = (u * phi).astype(BF16)
-            du = ((phi + u * dens) * nt(ogb, w2_ref[cols, :])).astype(BF16)
-            du_ref[rows, cols] = du
+            hid_ref[rows, cols] = (u * phi).astype(BF16)
+            dj_ref[rows, cols] = (phi + u * dens).astype(BF16)
+        return carry
+
+    def narrow_back(c, carry):
+        rows = clip_rows(c, PAIR)
+        for j in range(FF // CHUNK):
+            cols = slice(j * CHUNK, j * CHUNK + CHUNK)
+            dh = nt(og_ref[rows, :], w2_ref[cols, :])
+            du = (dj_ref[rows, cols].astype(F32) * dh).astype(BF16)
+            dj_ref[rows, cols] = du
             gb_ref[:, cols] += fold(du.astype(F32))
-        dmid_ref[rows, :] = middle
-        og_ref[rows, :] = ogb
         return carry
 
-    def feed_out(c, carry):
+    def widen_back(c, carry):
         rows = clip_rows(c, PAIR)
-        middle = dmid_ref[rows, :]
-        og = og_ref[rows, :].astype(F32)
-        result = middle + nn(dj_ref[rows, :], w2_ref[...]) + rowp_ref[5:6]
-
-        @pl.when(c >= 2)
-        def _():
-            send_out(c - 2).wait()
-
-        for part in range(2):
-            r = pl.ds(pl.multiple_of(c % 2 * PAIR + part * CLIP, CLIP), CLIP)
-            out_ref[r, :] = from_windows(result[part * CLIP : part * CLIP + CLIP])
-        send_out(c).start()
-        dn2 = nt(du_ref[rows, :], w1_ref[...])
-        nrm, inv = normalize(middle)
-        dmid = og + norm_back(dn2, nrm, inv, rowp_ref[2:3])
+        dn2 = nt(dj_ref[rows, :], w1_ref[...])
+        nrm, inv = normalize(mid_ref[rows, :])
+        dmid = og_ref[rows, :].astype(F32) + norm_back(dn2, nrm, inv, rowp_ref[2:3])
         dmid_ref[rows, :] = dmid
         dbr = dmid.astype(BF16)
         rows_ref[2] += fold(dn2 * nrm)
         rows_ref[3] += fold(dn2)
         rows_ref[4] += fold(dbr.astype(F32))
-        rows_ref[5] += fold(og)
         og_ref[rows, :] = dbr
         return carry
 
-    def feed_grads():
+    def narrow(c, carry):
+        rows = clip_rows(c, PAIR)
+        result = mid_ref[rows, :] + nn(hid_ref[rows, :], w2_ref[...]) + rowp_ref[5:6]
+        for part in range(2):
+            result_part = from_windows(result[part * CLIP : part * CLIP + CLIP])
+            mid_ref[clip_rows(2 * c + part), :] = result_part
+        send_out(c).start()
+        return carry
+
+    def wide_grads(buf, given, back):
         for j in range(FF // 512):
             cols = slice(j * 512, j * 512 + 512)
-            ebuf[0:D, cols] = nn(n2t_ref[...], du_ref[:, cols]).astype(BF16)
-            ebuf[D : 2 * D, cols] = nn(ogt_ref[...], dj_ref[:, cols]).astype(BF16)
+            buf[:, cols] = tn(given[...], back[:, cols]).astype(BF16)
 
     def branch_grads():
+        width = praw_ref.shape[0]
         for g in range(GROUPS):
             part = tn(att_ref[:, g * LANES : g * LANES + LANES], og_ref[...])
-            lbuf[D : D + LANES, g * D : g * D + D] = part.astype(BF16)
+            lbuf[3 * width :, g * D : g * D + D] = part[:width].astype(BF16)
         for j in range(clips // 2):
             r = slice(j * PAIR, j * PAIR + PAIR)
             att_ref[r, :] = nt(og_ref[r, :], wproj_ref[...]).astype(BF16)
+
+    def qkv_grads():
+        width = praw_ref.shape[0]
+        for j in range(3):
+            value = nn(n1t_ref[...], dj_ref[:, j * 512 : j * 512 + 512])
+            for k in range(4):
+                g, p = (4 * j + k) // 3, (4 * j + k) % 3
+                turned = value[:, k * LANES : k * LANES + LANES].T
+                lbuf[p * width : p * width + width, g * D : g * D + D] = turned[:width].astype(BF16)
 
     def attend_back(c, carry):
         rows = clip_rows(c)
@@ -633,7 +648,7 @@
                 inner = jnp.sum(pf * dp, axis=0, keepdims=True)
                 ds = jnp.where(time_ref[w] < frames, pf * (dp - inner), 0.0)
                 tacc = ds if tacc is None else tacc + ds
-                du_ref[w * SPOT : w * SPOT + SPOT, g * 256 : g * 256 + 256] = ds.astype(BF16)
+                probs_ref[c, w, g] = ds.astype(BF16)
                 dj_ref[spots, g * D + 2 * LANES : g * D + D] = nn(p, do).astype(BF16)
             tacc_ref[g] += tacc
         for g in range(GROUPS):
@@ -643,7 +658,7 @@
                 ck = slice(g * D + LANES, g * D + 2 * LANES)
                 q = qkv_ref[spots, cq]
                 k = qkv_ref[spots, ck]
-                ds = du_ref[w * SPOT : w * SPOT + SPOT, g * 256 : g * 256 + 256]
+                ds = probs_ref[c, w, g]
                 dj_ref[spots, cq] = (pick_heads(tn(ds, k)) * SCALE).astype(BF16)
                 dj_ref[spots, ck] = (nn(ds, stack_heads(q, masks)) * SCALE).astype(BF16)
         gqv_ref[...] += fold(dj_ref[rows, :].astype(F32))
@@ -654,7 +669,7 @@
         clip = [clip_rows(2 * c + part) for part in range(2)]
         x = jnp.concatenate([to_windows(tok_ref[r, :].astype(F32)) for r in clip], axis=0)
         n, inv = normalize(x)
-        dn1 = nt(dj_ref[rows, :], wqkv_ref[...])
+        dn1 = nn(dj_ref[rows, :], wqkv_ref[...])
         rows_ref[0] += fold(dn1 * n)
         rows_ref[1] += fold(dn1)
         din = dmid_ref[rows, :] + norm_back(dn1, n, inv, rowp_ref[0:1])
@@ -673,7 +688,7 @@
         for d in range(3)
     ]
     own_small = pltpu.make_async_copy(sown_ref, small_ref.at[head], ssems.at[2, 0])
-    gq_w = gather_stages(D, wqkv_ref, True, wsems.at[0])
+    gq_w = gather_stages(D, wqkv_ref, False, wsems.at[0])
     others = [
         gather_stages(rows, full, wide, wsems.at[1 + i])
         for i, (rows, full, wide) in enumerate(
@@ -681,19 +696,18 @@
         )
     ]
     for p in range(3):
-        part = qraw_ref[:, p, :].astype(BF16).astype(F32)
-        part = jnp.concatenate([part, jnp.zeros((D, LANES - part.shape[1]), F32)], axis=1)
-        wqkv_ref[:, pl.ds(pl.multiple_of(head * D + p * LANES, LANES), LANES)] = part.astype(BF16)
+        part = qraw_ref[p]
+        part = jnp.concatenate([part, jnp.zeros((LANES - part.shape[0], D), F32)], axis=0)
+        start = pl.multiple_of(head * D + p * LANES, LANES)
+        wqkv_ref[pl.ds(start, LANES), :] = part.astype(BF16)
     greet()
     gq_w[0]()
     width = qvb_ref.shape[1]
     sown_ref[...] = jnp.zeros_like(sown_ref)
     sown_ref[0:1, :width] = qvb_ref[0:1, :]
     sown_ref[0:1, LANES : LANES + width] = qvb_ref[1:2, :]
-    turn_ref[...] = jnp.zeros_like(turn_ref)
-    turn_ref[: table_ref.shape[0], :PER] = table_ref[...]
-    sown_ref[1 : 1 + PER, :256] = turn_ref[...].T[:PER, :]
-    sown_ref[5:6, :] = fc1b_ref[...]
+    sown_ref[1 : 1 + PER, : table_ref.shape[1]] = table_ref[...]
+    sown_ref[5:6, :] = fc1b_ref[...].reshape(1, D)
     own_small.start()
     for copy in small:
         copy.start()
@@ -731,24 +745,35 @@
         return clips * share // 8
 
     lax.fori_loop(0, clips // 2, project, 0)
-    lax.fori_loop(0, clips, attend, 0)
-    for k in others:
-        k[2]()
-    for k in others:
-        k[3]()
+    lax.fori_loop(0, span(4), attend, 0)
+    others[0][2]()
+    others[1][2]()
+    lax.fori_loop(span(4), span(8), attend, 0)
+    others[0][3]()
+    others[1][3]()
     load_og.wait()
-    lax.fori_loop(0, clips // 2, feed, 0)
-    feed_grads()
-
-    early = reduce_stages(ebuf, core_e, cell_e, up_e, head_e, early_ref, rsems.at[0])
-    early_small = small_stages(esbuf, core_es, cell_es, up_es, head_es, esmall_ref, rsems.at[1])
+    lax.fori_loop(0, span(4) // 2, widen, 0)
+    others[2][2]()
+    lax.fori_loop(span(4) // 2, clips // 2, widen, 0)
+    others[2][3]()
+    one = reduce_stages(buf_1, core_1, cell_1, up_1, head_1, one_ref, rsems.at[0])
+    two = reduce_stages(buf_2, core_2, cell_2, up_2, head_2, two_ref, rsems.at[1])
     late = reduce_stages(lbuf, core_l, cell_l, up_l, head_l, late_ref, rsems.at[2])
-    late_small = small_stages(lsbuf, core_ls, cell_ls, up_ls, head_ls, lsmall_ref, rsems.at[3])
-    early[0]()
-    lax.fori_loop(0, span(4) // 2, feed_out, 0)
-    early[1]()
-    lax.fori_loop(span(4) // 2, clips // 2, feed_out, 0)
+    early_small = small_stages(esbuf, core_es, cell_es, up_es, head_es, esmall_ref, rsems.at[3])
+    late_small = small_stages(lsbuf, core_ls, cell_ls, up_ls, head_ls, lsmall_ref, rsems.at[4])
+    wide_grads(buf_2, og_ref, hid_ref)
+    two[0]()
+    lax.fori_loop(0, span(4) // 2, narrow_back, 0)
+    two[1]()
+    lax.fori_loop(span(4) // 2, clips // 2, narrow_back, 0)
+    wide_grads(buf_1, n2_ref, dj_ref)
+    one[0]()
+    lax.fori_loop(0, span(4) // 2, widen_back, 0)
+    one[1]()
+    two[2]()
+    lax.fori_loop(span(4) // 2, clips // 2, widen_back, 0)
     branch_grads()
+    two[3]()
     esbuf[0:1, :] = jnp.sum(gb_ref[...], axis=0, keepdims=True)
     for r in range(4):
         line = jnp.sum(rows_ref[2 + r], axis=0, keepdims=True)
@@ -756,42 +781,44 @@
             esbuf[1 + r : 2 + r, g * D : g * D + D] = line
     early_small[0]()
     lax.fori_loop(0, span(2), attend_back, 0)
+    two[4]()
+    one[2]()
     early_small[1]()
-    lax.fori_loop(span(2), span(4), attend_back, 0)
-    early[2]()
+    lax.fori_loop(span(2), span(5), attend_back, 0)
+    one[3]()
+    two[5]()
     early_small[2]()
-    lax.fori_loop(span(4), span(8), attend_back, 0)
-    for j in range(3):
-        cols = slice(j * 512, j * 512 + 512)
-        lbuf[0:D, cols] = nn(n1t_ref[...], dj_ref[:, cols]).astype(BF16)
-    early[3]()
+    lax.fori_loop(span(5), span(7), attend_back, 0)
+    one[4]()
+    lax.fori_loop(span(7), span(8), attend_back, 0)
+    qkv_grads()
     late[0]()
+    one[5]()
     early_small[3]()
     for g in range(GROUPS):
         cols = slice(g * D, g * D + LANES)
         lsbuf[0:1, cols] = jnp.sum(gqv_ref[:, cols], axis=0, keepdims=True)
         cols = slice(g * D + 2 * LANES, g * D + D)
         lsbuf[0:1, cols] = jnp.sum(gqv_ref[:, cols], axis=0, keepdims=True)
+    late[1]()
     fold_table(tacc_ref, lsbuf)
-    late[1]()
-    lax.fori_loop(0, span(4) // 2, entry_back, 0)
-    early[4]()
-    lax.fori_loop(span(4) // 2, clips // 2, entry_back, 0)
+    lax.fori_loop(0, clips // 2, entry_back, 0)
     for r in range(2):
         line = jnp.sum(rows_ref[r], axis=0, keepdims=True)
         for g in range(GROUPS):
             lsbuf[4 + r : 5 + r, g * D : g * D + D] = line
     late_small[0]()
-    early[5]()
+    lax.fori_loop(0, span(4) // 2, narrow, 0)
     late[2]()
     late_small[1]()
+    lax.fori_loop(span(4) // 2, clips // 2, narrow, 0)
+    late_small[2]()
     late[3]()
-    late_small[2]()
+    late_small[3]()
     late[4]()
-    late_small[3]()
     late[5]()
     square = jnp.zeros((8, D), F32)
-    for ref in (early_ref, late_ref):
+    for ref in (one_ref, two_ref, late_ref):
         value = ref[...].astype(F32)
         square = square + fold(value * value)
     es, ls = esmall_ref[...], lsmall_ref[...]
@@ -815,12 +842,11 @@
 
     def finish(c, carry):
         rows = clip_rows(c, PAIR)
+        send_out(c).wait()
         pltpu.make_async_copy(dmid_ref.at[rows, :], din_hbm.at[rows, :], osems.at[1, c]).wait()
         return carry
 
     lax.fori_loop(0, clips // 2, finish, 0)
-    for c in range(max(clips // 2 - 2, 0), clips // 2):
-        send_out(c).wait()
 
 
 def fold_table(tacc_ref, lsbuf):
@@ -859,36 +885,35 @@
     spec = pl.BlockSpec
     inside = lambda: spec(memory_space=vmem)
     outside = lambda: spec(memory_space=pl.ANY)
-    early, late = 2 * D, D + LANES
+    half, part = D // 2, D // 8
     return pl.pallas_call(
         partial(block_kernel, clips),
         in_specs=[spec(memory_space=pltpu.SMEM), outside(), outside()] + [inside()] * 8,
-        out_specs=[outside(), outside()] + [inside()] * 5,
+        out_specs=[outside(), outside()] + [inside()] * 6,
         out_shape=[
             shape((rows, D), F32),
             shape((rows, D), F32),
-            shape((early, D), BF16),
-            shape((late, D), BF16),
+            shape((D, D), BF16),
+            shape((D, D), BF16),
+            shape((D, D), BF16),
             shape((8, D), F32),
             shape((8, D), F32),
             shape((8, LANES), F32),
         ],
         scratch_shapes=[
             vmem((8, D), F32),
-            vmem((256, LANES), F32),
             vmem((rows, D), BF16),
             vmem((rows, D), BF16),
-            vmem((2 * PAIR, D), F32),
+            vmem((rows, D), F32),
             vmem((rows, D), F32),
             vmem((D, rows), BF16),
-            vmem((D, rows), BF16),
-            vmem((D, rows), BF16),
+            vmem((rows, D), BF16),
             vmem((rows, 1536), BF16),
             vmem((rows, 1536), BF16),
             vmem((rows, FF), BF16),
             vmem((clips, 4, GROUPS, SPOT, PER * SPOT), BF16),
             vmem((rows, 512), BF16),
-            vmem((D, 1536), BF16),
+            vmem((1536, D), BF16),
             vmem((512, D), BF16),
             vmem((D, FF), BF16),
             vmem((FF, D), BF16),
@@ -901,30 +926,35 @@
             vmem((8, FF), F32),
             vmem((8, 1536), F32),
             vmem((GROUPS, SPOT, PER * SPOT), F32),
-            vmem((early, 1536), BF16),
-            vmem((late, 1536), BF16),
+            vmem((D, 1536), BF16),
+            vmem((D, 1536), BF16),
+            vmem((D, 1536), BF16),
             vmem((8, 1536), F32),
             vmem((8, 1536), F32),
-            vmem((early // 2, 1536), BF16),
-            vmem((late // 2, 1536), BF16),
+            vmem((half, 1536), BF16),
+            vmem((half, 1536), BF16),
+            vmem((half, 1536), BF16),
             vmem((8, 1536), F32),
             vmem((8, 1536), F32),
-            vmem((3, early // 8, 1536), BF16),
-            vmem((3, late // 8, 1536), BF16),
+            vmem((3, part, 1536), BF16),
+            vmem((3, part, 1536), BF16),
+            vmem((3, part, 1536), BF16),
             vmem((4, 8, 1536), F32),
             vmem((4, 8, 1536), F32),
-            vmem((upper + 1, early // 8, 1536), BF16),
-            vmem((upper + 1, late // 8, 1536), BF16),
+            vmem((upper + 1, part, 1536), BF16),
+            vmem((upper + 1, part, 1536), BF16),
+            vmem((upper + 1, part, 1536), BF16),
             vmem((upper + 1, 8, 1536), F32),
             vmem((upper + 1, 8, 1536), F32),
-            vmem((3, early // 8, D), BF16),
-            vmem((3, late // 8, D), BF16),
+            vmem((3, part, D), BF16),
+            vmem((3, part, D), BF16),
+            vmem((3, part, D), BF16),
             vmem((4, 8, D), F32),
             vmem((4, 8, D), F32),
             vmem((4, 8, LANES), F32),
             sems((4, 11, 3)),
             sems((3, 3)),
-            sems((4, 2, 14 + upper)),
+            sems((5, 2, 14 + upper)),
             sems((2, 3)),
             sems((3, max(clips, 2))),
         ],
@@ -946,23 +976,42 @@
     return (gradient, moment_new, second_new, master)
 
 
-def step_kernel(*refs):
-    norm_ref, e1_ref, e2_ref, ep_ref, late_ref, es_ref, ls_ref = refs[:7]
-    weights, firsts, seconds = refs[7:15], refs[15:23], refs[23:31]
-    gn_ref, outs = refs[31], refs[32:]
+def step_kernel(cuts, *refs):
+    norm_ref, e1_ref, e2_ref, ep_ref, late_ref, es_ref, ls_ref, one_hbm, two_hbm = refs[:9]
+    weights, firsts, seconds = refs[9:17], refs[17:25], refs[25:33]
+    gn_ref, one_out, two_out, outs, sems = refs[33], refs[34], refs[35], refs[36:68], refs[68]
+    bounce = refs[69:71]
+    pulls = [
+        pltpu.make_async_copy(one_hbm, bounce[0], sems.at[0]),
+        pltpu.make_async_copy(two_hbm, bounce[1], sems.at[1]),
+    ]
+    pushes = [
+        pltpu.make_async_copy(bounce[0], one_out, sems.at[2]),
+        pltpu.make_async_copy(bounce[1], two_out, sems.at[3]),
+    ]
+
+    @pl.when(pl.program_id(0) == 0)
+    def _():
+        for pull in pulls:
+            pull.start()
+
+    @pl.when(pl.program_id(0) == 1)
+    def _():
+        for pull, push in zip(pulls, pushes):
+            pull.wait()
+            push.start()
+
     norm = norm_ref[0:1, 0:1]
     factor = jnp.minimum(1.0, CLIP_LIMIT / (norm + 1e-06))
 
     def put(i, gradient, rate, at=(slice(None), slice(None))):
-        values = adam_step(weights[i][at], gradient, firsts[i][at], seconds[i][at], factor, rate)
+        given = [ref[i][at].reshape(gradient.shape) for ref in (weights, firsts, seconds)]
+        values = adam_step(given[0], gradient, given[1], given[2], factor, rate)
         for k in range(4):
-            outs[4 * i + k][at] = values[k]
-
-    late = late_ref[...].astype(F32)
-    width = weights[0].shape[2]
-    for p in range(3):
-        at = (slice(None), p, slice(None))
-        put(0, late[:, p * LANES : p * LANES + width], LEARN_RATE, at)
+            outs[4 * i + k][at] = values[k].reshape(outs[4 * i + k][at].shape)
+
+    width = weights[0].shape[1]
+    put(0, late_ref[...].astype(F32), LEARN_RATE, (0, slice(None), slice(None)))
     put(3, ep_ref[...].astype(F32), LEARN_RATE)
     put(4, e1_ref[...].astype(F32), LEARN_RATE)
     put(6, e2_ref[...].astype(F32).T, LEARN_RATE)
@@ -980,19 +1029,24 @@
                 pieces.append(ls_ref[1 + at // D : 2 + at // D, at % D : at % D + LANES])
             lines.append(jnp.concatenate(pieces, axis=1))
         lines = jnp.concatenate(lines + [jnp.zeros((8 - PER, 256), F32)])
-        offsets = weights[2].shape[0]
+        offsets = weights[2].shape[1]
         flip = iota((256, 256), 0) + iota((256, 256), 1) == offsets - 1
         flip = jnp.where(flip, 1.0, 0.0).astype(F32).astype(BF16)
         table = None
         for part in split_three(lines):
-            term = nt(flip, part)
+            term = nn(part, flip)
             table = term if table is None else table + term
-        put(2, table[:offsets, :PER], ROW_RATE)
-        put(5, es_ref[0:1, :], LEARN_RATE)
+        put(2, table[:PER, :offsets], ROW_RATE)
+        put(5, es_ref[0:1, :], LEARN_RATE, (slice(None),))
         put(7, jnp.concatenate([ls_ref[4:6, :], es_ref[1:5, :]]), ROW_RATE)
 
-
-def take_step(norm, early, late, esmall, lsmall, weights, firsts, seconds):
+    @pl.when(pl.program_id(0) == cuts - 1)
+    def _():
+        for push in pushes:
+            push.wait()
+
+
+def take_step(norm, g1, g2, late, esmall, lsmall, one, two, weights, firsts, seconds):
     cuts = 3
     spec = pl.BlockSpec
     full = lambda a: spec(a.shape, lambda i: (0,) * a.ndim)
@@ -1006,23 +1060,33 @@
     tall = weights[3].shape[0] // cuts
     shape = jax.ShapeDtypeStruct
     outs = pl.pallas_call(
-        step_kernel,
+        partial(step_kernel, cuts),
         grid=(cuts,),
         in_specs=[
             full(norm),
             spec((rows, D), lambda i: (i, 0)),
-            spec((D, rows), lambda i: (1, i)),
-            spec((tall, D), lambda i: (D // tall + i, 0)),
-            spec((rows, D), lambda i: (i, 0)),
+            spec((D, rows), lambda i: (0, i)),
+            spec((tall, D), lambda i: (cuts * (cuts * tall) // tall + i, 0)),
+            spec((cuts * tall, D), lambda i: (i, 0)),
             full(esmall),
             full(lsmall),
+            spec(memory_space=pl.ANY),
+            spec(memory_space=pl.ANY),
         ]
         + each * 3,
-        out_specs=[spec((1, 1), lambda i: (0, 0))] + [e for e in each for _ in range(4)],
-        out_shape=[shape((1, 1), F32)] + [shape(a.shape, F32) for a in weights for _ in range(4)],
+        out_specs=[spec((1, 1), lambda i: (0, 0))]
+        + [spec(memory_space=pl.ANY)] * 2
+        + [e for e in each for _ in range(4)],
+        out_shape=[shape((1, 1), F32), shape(one.shape, F32), shape(two.shape, F32)]
+        + [shape(a.shape, F32) for a in weights for _ in range(4)],
+        scratch_shapes=[
+            pltpu.SemaphoreType.DMA((4,)),
+            pltpu.VMEM(one.shape, F32),
+            pltpu.VMEM(two.shape, F32),
+        ],
         compiler_params=pltpu.CompilerParams(vmem_limit_bytes=VMEM_LIMIT),
-    )(norm, early, early, late, late, esmall, lsmall, *weights, *firsts, *seconds)
-    return outs[0], outs[1:]
+    )(norm, g1, g2, late, late, esmall, lsmall, one, two, *weights, *firsts, *seconds)
+    return outs[0], outs[1], outs[2], outs[3:]
 
 
 def shards(
@@ -1054,52 +1118,56 @@
     rows_first,
     rows_second,
 ):
-    line = lambda v: v.reshape(1, -1)
-    output, input_grad, early, late, esmall, lsmall, norm = block(
+    parts = lambda v: v.transpose(1, 2, 0)
+    weights = (
+        parts(qkv_weight),
+        qv_bias,
+        rel_table.T,
+        proj_weight,
+        fc1_weight,
+        fc1_bias,
+        fc2_weight,
+        row_params,
+    )
+    firsts = (
+        parts(qkv_first),
+        qvb_first,
+        table_first.T,
+        proj_first,
+        fc1_first,
+        fc1b_first,
+        fc2_first,
+        rows_first,
+    )
+    seconds = (
+        parts(qkv_second),
+        qvb_second,
+        table_second.T,
+        proj_second,
+        fc1_second,
+        fc1b_second,
+        fc2_second,
+        rows_second,
+    )
+    output, input_grad, g1, g2, late, esmall, lsmall, norm = block(
         clip_frames,
         tokens,
         out_grad,
-        qkv_weight,
+        weights[0],
         proj_weight,
         fc1_weight,
         fc2_weight,
         qv_bias,
-        rel_table,
-        line(fc1_bias),
+        weights[2],
+        fc1_bias,
         row_params,
     )
-    weights = (
-        qkv_weight,
-        qv_bias,
-        rel_table,
-        proj_weight,
-        fc1_weight,
-        line(fc1_bias),
-        fc2_weight,
-        row_params,
+    grad_norm, output, input_grad, updated = take_step(
+        norm, g1, g2, late, esmall, lsmall, output, input_grad, weights, firsts, seconds
     )
-    firsts = (
-        qkv_first,
-        qvb_first,
-        table_first,
-        proj_first,
-        fc1_first,
-        line(fc1b_first),
-        fc2_first,
-        rows_first,
-    )
-    seconds = (
-        qkv_second,
-        qvb_second,
-        table_second,
-        proj_second,
-        fc1_second,
-        line(fc1b_second),
-        fc2_second,
-        rows_second,
-    )
-    grad_norm, updated = take_step(norm, early, late, esmall, lsmall, weights, firsts, seconds)
-    updated = [v.reshape(-1) if 20 <= k < 24 else v for k, v in enumerate(updated)]
+    updated = [
+        v.transpose(2, 0, 1) if k < 4 else v.T if 8 <= k < 12 else v for k, v in enumerate(updated)
+    ]
     return (output, input_grad, grad_norm.reshape(()), *updated)
 
 

time: 174 us -> 122 us (0.70)
  local copies, waits for them, and re-layouts: 34.2 us -> 0 us
  Pallas kernels: 133 us -> 121 us
  other arithmetic: 5.09 us -> 0 us
    unnamed x20 -> x0, local copies, waits for them, and re-layouts: 30.5 us -> none
    pallas_call x1, Pallas kernels: 121 us -> 111 us  [block(): pl.pallas_call(partial(block_kernel, clips), in_specs=[spec(memory_space=...]
    pallas_call x4 -> x0, other arithmetic: 5.09 us -> none  [take_step(): pl.pallas_call(step_kernel, grid=(cuts,), in_specs=[full(norm), spec((row...]
    reshape x3 -> x0, local copies, waits for them, and re-layouts: 3.73 us -> none  [shards(): line = lambda v: v.reshape(1, -1)]
where the time goes in v5:
time: 122 us
  Pallas kernels  121 us (99%)
    pallas_call x1, Pallas kernels, block(): pl.pallas_call(partial(block_kernel, clips), in_specs=[spec(memory_space=...  111 us
    pallas_call x1, Pallas kernels, take_step(): pl.pallas_call(partial(step_kernel, cuts), grid=(cuts,), in_specs=[full(n...  10.2 us

profile of v5, /device:TPU:0, one launch (start us, length us, event | category | flops | bytes accessed | tf_op | source)
XLA Modules:
  0.0 121.9 jit_solution(9263415244534393802)
XLA Ops:
  0.7 110.9 %shard_map.530 = (f32[2048,384]{1,0:T(8,128)}, f32[2048,384]{1,0:T(8,128)}, bf16[384,384]{1,0:T(8,128)(2,1)}, bf16[384,384]{1,0:T(8,128)(2,1)}, bf16[384,384]{1,...) custom-call(s32[32]{0:T(128)} %frames_ref.1, bf16[2048,384]{1,0:T(8,128)(2,1)} %tok_hbm.1, ...), custom_call_target="tpu_custom_call" | custom-call | tf_op jit(solution)/shard_map/pallas_call | solution.py:889
  111.5 10.2 %shard_map.531 = (f32[1,1]{1,0:T(1,128)}, f32[2048,384]{1,0:T(8,128)}, f32[2048,384]{1,0:T(8,128)}, f32[3,96,384]{2,1,0:T(8,128)}, f32[3,96,384]{2,1,0:T(8,128)}...) custom-call(f32[8,128]{1,0:T(8,128)} %get-tuple-element.78.refs_0_, ...), custom_call_target="tpu_custom_call" | custom-call | tf_op jit(solution)/shard_map/pallas_call | solution.py:1062

commit v6 on v5

--- a/solution.py
+++ b/solution.py
@@ -163,15 +163,8 @@
 
 
 def gelu_parts(u):
-    mag = jnp.abs(u) * (0.5**0.5)
-    t = 1.0 / (1.0 + 0.3275911 * mag)
     bell = jnp.exp(-0.5 * (u * u))
-    poly = t * (
-        0.127414796
-        + t * (-0.142248368 + t * (0.7107068705 + t * (-0.7265760135 + t * 0.5307027145)))
-    )
-    tail = poly * bell
-    return jnp.where(u >= 0.0, 1.0 - tail, tail), bell * 0.3989422804014327
+    return 0.5 + 0.5 * lax.erf(u * (0.5**0.5)), bell * 0.3989422804014327
 
 
 def place(win, head):
@@ -199,8 +192,7 @@
     win, head, core, cell, base = position()
     barrier = pltpu.get_barrier_semaphore()
     peers = [(win, (head + d) % 4) for d in (1, 2, 3)]
-    peers += [(base + 2 * ((cell + d) % 4) + core, head) for d in (1, 2, 3)]
-    peers += [(win + 1 - 2 * core, head)]
+    peers += [(base + 2 * ((cell + k % 4) % 4) + (core + k // 4) % 2, head) for k in range(1, 8)]
     for w, h in peers:
         pl.semaphore_signal(barrier, inc=1, device_id=place(w, h), device_id_type=pl.DeviceIdType.MESH)
     pl.semaphore_wait(barrier, len(peers))
@@ -307,20 +299,10 @@
             peer,
         )
 
-    def back_cell(c):
-        peer = (cell + c + 1) % 4
-        return remote(
-            final.at[own, :],
-            final.at[own, :],
-            sems.at[0, 7 + c],
-            sems.at[1, 7 + c],
-            base + 2 * peer + core,
-            head,
-        )
-
-    def back_core():
-        view = final.at[pl.ds(near, half), :]
-        return remote(view, view, sems.at[0, 10], sems.at[1, 10], other, head)
+    def back(k):
+        peer = base + 2 * ((cell + k % 4) % 4) + (core + k // 4) % 2
+        view = final.at[own, :]
+        return remote(view, view, sems.at[0, 6 + k], sems.at[1, 6 + k], peer, head)
 
     def first():
         to_core().start()
@@ -356,24 +338,20 @@
         for d in range(3):
             total = total + from_head[d].astype(F32)
         final[own, :] = total.astype(BF16)
-        for c in range(3):
-            back_cell(c).start()
-
-    def fifth():
-        for c in range(3):
-            back_cell(c).wait_recv()
-        back_core().start()
+        for k in range(1, 8):
+            back(k).start()
 
     def last():
-        back_core().wait_recv()
+        for k in range(1, 8):
+            back(k).wait_recv()
         to_core().wait_send()
         for c in range(3):
             to_cell(c).wait_send()
             to_head(c).wait_send()
-            back_cell(c).wait_send()
-        back_core().wait_send()
-
-    return first, second, third, fourth, fifth, last
+        for k in range(1, 8):
+            back(k).wait_send()
+
+    return first, second, third, fourth, last
 
 
 def small_stages(buf, from_core, cells, from_upper, heads, final, sems):
@@ -478,7 +456,6 @@
     time_ref,
     rows_ref,
     gb_ref,
-    gqv_ref,
     tacc_ref,
     buf_1,
     buf_2,
@@ -521,7 +498,7 @@
             n1, _ = normalize(to_windows(tok_ref[rows, :].astype(F32)))
             n1 = (n1 * rowp_ref[0:1] + rowp_ref[1:2]).astype(BF16)
             att_ref[rows, :D] = n1
-            n1t_ref[:, rows] = n1.T
+            n1t_ref[:D, rows] = n1.T
         return carry
 
     def project(c, carry):
@@ -629,7 +606,10 @@
             value = nn(n1t_ref[...], dj_ref[:, j * 512 : j * 512 + 512])
             for k in range(4):
                 g, p = (4 * j + k) // 3, (4 * j + k) % 3
-                turned = value[:, k * LANES : k * LANES + LANES].T
+                turned = value[:D, k * LANES : k * LANES + LANES].T
+                if p != 1:
+                    cols = slice(g * D + p * LANES, g * D + p * LANES + LANES)
+                    lsbuf[0:1, cols] = value[D : D + 1, k * LANES : k * LANES + LANES]
                 lbuf[p * width : p * width + width, g * D : g * D + D] = turned[:width].astype(BF16)
 
     def attend_back(c, carry):
@@ -661,7 +641,6 @@
                 ds = probs_ref[c, w, g]
                 dj_ref[spots, cq] = (pick_heads(tn(ds, k)) * SCALE).astype(BF16)
                 dj_ref[spots, ck] = (nn(ds, stack_heads(q, masks)) * SCALE).astype(BF16)
-        gqv_ref[...] += fold(dj_ref[rows, :].astype(F32))
         return carry
 
     def entry_back(c, carry):
@@ -722,8 +701,9 @@
     for wt in range(2):
         for wf in range(2):
             time_ref[wt * 2 + wf] = key_times(wt, wf)
-    for ref in (rows_ref, gb_ref, gqv_ref, tacc_ref, esbuf, lsbuf):
+    for ref in (rows_ref, gb_ref, tacc_ref, esbuf, lsbuf):
         ref[...] = jnp.zeros_like(ref)
+    n1t_ref[D:, :] = jnp.ones((16, n1t_ref.shape[1]), F32).astype(BF16)
     load_tok.wait()
     lax.fori_loop(0, clips // 2, enter, 0)
     gq_w[1]()
@@ -738,13 +718,14 @@
     build_bias(small_ref, bias_ref)
     gq_w[2]()
     gq_w[3]()
-    for k in others:
-        k[1]()
+    others[0][1]()
+    others[1][1]()
 
     def span(share):
         return clips * share // 8
 
     lax.fori_loop(0, clips // 2, project, 0)
+    others[2][1]()
     lax.fori_loop(0, span(4), attend, 0)
     others[0][2]()
     others[1][2]()
@@ -781,46 +762,39 @@
             esbuf[1 + r : 2 + r, g * D : g * D + D] = line
     early_small[0]()
     lax.fori_loop(0, span(2), attend_back, 0)
-    two[4]()
     one[2]()
     early_small[1]()
     lax.fori_loop(span(2), span(5), attend_back, 0)
+    two[4]()
     one[3]()
-    two[5]()
     early_small[2]()
-    lax.fori_loop(span(5), span(7), attend_back, 0)
-    one[4]()
-    lax.fori_loop(span(7), span(8), attend_back, 0)
+    lax.fori_loop(span(5), span(8), attend_back, 0)
     qkv_grads()
     late[0]()
-    one[5]()
+    one[4]()
     early_small[3]()
-    for g in range(GROUPS):
-        cols = slice(g * D, g * D + LANES)
-        lsbuf[0:1, cols] = jnp.sum(gqv_ref[:, cols], axis=0, keepdims=True)
-        cols = slice(g * D + 2 * LANES, g * D + D)
-        lsbuf[0:1, cols] = jnp.sum(gqv_ref[:, cols], axis=0, keepdims=True)
+    fold_table(tacc_ref, lsbuf)
     late[1]()
-    fold_table(tacc_ref, lsbuf)
     lax.fori_loop(0, clips // 2, entry_back, 0)
     for r in range(2):
         line = jnp.sum(rows_ref[r], axis=0, keepdims=True)
         for g in range(GROUPS):
             lsbuf[4 + r : 5 + r, g * D : g * D + D] = line
     late_small[0]()
+    late[2]()
     lax.fori_loop(0, span(4) // 2, narrow, 0)
-    late[2]()
     late_small[1]()
     lax.fori_loop(span(4) // 2, clips // 2, narrow, 0)
+    late[3]()
     late_small[2]()
-    late[3]()
+    square = jnp.zeros((8, D), F32)
+    for ref in (one_ref, two_ref):
+        value = ref[...].astype(F32)
+        square = square + fold(value * value)
     late_small[3]()
     late[4]()
-    late[5]()
-    square = jnp.zeros((8, D), F32)
-    for ref in (one_ref, two_ref, late_ref):
-        value = ref[...].astype(F32)
-        square = square + fold(value * value)
+    value = late_ref[...].astype(F32)
+    square = square + fold(value * value)
     es, ls = esmall_ref[...], lsmall_ref[...]
     row = iota((8, D), 0)
     square = square + jnp.where(row < 1, es * es, 0.0) + jnp.where(row < 4, ls * ls, 0.0)
@@ -906,7 +880,7 @@
             vmem((rows, D), BF16),
             vmem((rows, D), F32),
             vmem((rows, D), F32),
-            vmem((D, rows), BF16),
+            vmem((D + 16, rows), BF16),
             vmem((rows, D), BF16),
             vmem((rows, 1536), BF16),
             vmem((rows, 1536), BF16),
@@ -924,7 +898,6 @@
             vmem((4, SPOT, PER * SPOT), jnp.int32),
             vmem((6, 8, D), F32),
             vmem((8, FF), F32),
-            vmem((8, 1536), F32),
             vmem((GROUPS, SPOT, PER * SPOT), F32),
             vmem((D, 1536), BF16),
             vmem((D, 1536), BF16),

time: 122 us -> 116 us (0.951)
  Pallas kernels: 121 us -> 115 us
    pallas_call x1, Pallas kernels: 111 us -> 105 us  [block(): pl.pallas_call(partial(block_kernel, clips), in_specs=[spec(memory_space=...]
where the time goes in v6:
time: 116 us
  Pallas kernels  115 us (99%)
    pallas_call x1, Pallas kernels, block(): pl.pallas_call(partial(block_kernel, clips), in_specs=[spec(memory_space=...  105 us
    pallas_call x1, Pallas kernels, take_step(): pl.pallas_call(partial(step_kernel, cuts), grid=(cuts,), in_specs=[full(n...  10.2 us

profile of v6, /device:TPU:0, one launch (start us, length us, event | category | flops | bytes accessed | tf_op | source)
XLA Modules:
  0.0 116.2 jit_solution(1571830426607264834)
XLA Ops:
  0.7 105.1 %shard_map.530 = (f32[2048,384]{1,0:T(8,128)}, f32[2048,384]{1,0:T(8,128)}, bf16[384,384]{1,0:T(8,128)(2,1)}, bf16[384,384]{1,0:T(8,128)(2,1)}, bf16[384,384]{1,...) custom-call(s32[32]{0:T(128)} %frames_ref.1, bf16[2048,384]{1,0:T(8,128)(2,1)} %tok_hbm.1, ...), custom_call_target="tpu_custom_call" | custom-call | tf_op jit(solution)/shard_map/pallas_call | solution.py:863
  105.8 10.2 %shard_map.531 = (f32[1,1]{1,0:T(1,128)}, f32[2048,384]{1,0:T(8,128)}, f32[2048,384]{1,0:T(8,128)}, f32[3,96,384]{2,1,0:T(8,128)}, f32[3,96,384]{2,1,0:T(8,128)}...) custom-call(f32[8,128]{1,0:T(8,128)} %get-tuple-element.78.refs_0_, ...), custom_call_target="tpu_custom_call" | custom-call | tf_op jit(solution)/shard_map/pallas_call | solution.py:1035

commit v7 on v6

--- a/solution.py
+++ b/solution.py
@@ -35,7 +35,8 @@
 SCALE = HDIM ** (-0.5)
 F32 = jnp.float32
 BF16 = jnp.bfloat16
-VMEM_LIMIT = 60 * 1024 * 1024
+VMEM_LIMIT = 50 * 1024 * 1024
+TAIL_LIMIT = 30 * 1024 * 1024
 
 
 def nn(a, b):
@@ -195,7 +196,7 @@
     peers += [(base + 2 * ((cell + k % 4) % 4) + (core + k // 4) % 2, head) for k in range(1, 8)]
     for w, h in peers:
         pl.semaphore_signal(barrier, inc=1, device_id=place(w, h), device_id_type=pl.DeviceIdType.MESH)
-    pl.semaphore_wait(barrier, len(peers))
+    return lambda: pl.semaphore_wait(barrier, len(peers))
 
 
 def shard_view(ref, wide, head, start, count):
@@ -412,21 +413,23 @@
     return pl.ds(pl.multiple_of(c * count, count), count)
 
 
-def block_kernel(
+def block_kernel(clips, *refs):
+    block_body(clips, refs[3:27], refs[39:63], *refs[:3], *refs[27:39], *refs[63:])
+
+
+def block_body(
     clips,
+    held,
+    kept,
     frames_ref,
     tok_hbm,
     og_hbm,
-    qraw_ref,
-    praw_ref,
-    araw_ref,
-    braw_ref,
     qvb_ref,
     table_ref,
     fc1b_ref,
     rowp_ref,
-    out_hbm,
-    din_hbm,
+    mid_ref,
+    dmid_ref,
     one_ref,
     two_ref,
     late_ref,
@@ -436,8 +439,6 @@
     sown_ref,
     tok_ref,
     og_ref,
-    mid_ref,
-    dmid_ref,
     n1t_ref,
     n2_ref,
     qkv_ref,
@@ -459,22 +460,19 @@
     tacc_ref,
     buf_1,
     buf_2,
-    lbuf,
+    gp_ref,
     esbuf,
     lsbuf,
     core_1,
     core_2,
-    core_l,
     core_es,
     core_ls,
     cell_1,
     cell_2,
-    cell_l,
     cell_es,
     cell_ls,
     up_1,
     up_2,
-    up_l,
     up_es,
     up_ls,
     head_1,
@@ -491,6 +489,7 @@
 ):
     win, head, core, cell, base = position()
     first_clip = head * clips
+    lbuf = buf_2
 
     def enter(c, carry):
         for part in range(2):
@@ -530,10 +529,6 @@
                 att_ref[spots, g * LANES : g * LANES + LANES] = o.astype(BF16)
         return carry
 
-    def send_out(c):
-        rows = clip_rows(c, PAIR)
-        return pltpu.make_async_copy(mid_ref.at[rows, :], out_hbm.at[rows, :], osems.at[0, c])
-
     def widen(c, carry):
         rows = clip_rows(c, PAIR)
         clip = [clip_rows(2 * c + part) for part in range(2)]
@@ -583,7 +578,6 @@
         for part in range(2):
             result_part = from_windows(result[part * CLIP : part * CLIP + CLIP])
             mid_ref[clip_rows(2 * c + part), :] = result_part
-        send_out(c).start()
         return carry
 
     def wide_grads(buf, given, back):
@@ -595,13 +589,14 @@
         width = praw_ref.shape[0]
         for g in range(GROUPS):
             part = tn(att_ref[:, g * LANES : g * LANES + LANES], og_ref[...])
-            lbuf[3 * width :, g * D : g * D + D] = part[:width].astype(BF16)
+            gp_ref[:, g * D : g * D + D] = part[:width].astype(BF16)
         for j in range(clips // 2):
             r = slice(j * PAIR, j * PAIR + PAIR)
             att_ref[r, :] = nt(og_ref[r, :], wproj_ref[...]).astype(BF16)
 
     def qkv_grads():
         width = praw_ref.shape[0]
+        lbuf[3 * width :, :] = gp_ref[...]
         for j in range(3):
             value = nn(n1t_ref[...], dj_ref[:, j * 512 : j * 512 + 512])
             for k in range(4):
@@ -655,13 +650,16 @@
         for part in range(2):
             r = clip[part]
             dmid_ref[r, :] = from_windows(din[part * CLIP : part * CLIP + CLIP])
-        pltpu.make_async_copy(dmid_ref.at[rows, :], din_hbm.at[rows, :], osems.at[1, c]).start()
         return carry
 
-    load_tok = pltpu.make_async_copy(tok_hbm, tok_ref, osems.at[2, 0])
-    load_og = pltpu.make_async_copy(og_hbm, og_ref, osems.at[2, 1])
+    qraw_ref, praw_ref, araw_ref, braw_ref = kept[0], kept[3], kept[6], kept[9]
+    keeps = [pltpu.make_async_copy(a, b, osems.at[0, 2 + i]) for i, (a, b) in enumerate(zip(held, kept))]
+    for i in (0, 3, 6, 9):
+        keeps[i].start()
+    load_tok = pltpu.make_async_copy(tok_hbm, tok_ref, osems.at[0, 0])
+    load_og = pltpu.make_async_copy(og_hbm, og_ref, osems.at[0, 1])
     load_tok.start()
-    load_og.start()
+    greeting = greet()
     small = [
         remote(sown_ref, small_ref.at[head], ssems.at[0, d], ssems.at[1, d], win, (head + d + 1) % 4)
         for d in range(3)
@@ -674,13 +672,15 @@
             ((LANES, wproj_ref, False), (D, w1_ref, True), (D, w2_ref, False))
         )
     ]
+    keeps[0].wait()
     for p in range(3):
         part = qraw_ref[p]
         part = jnp.concatenate([part, jnp.zeros((LANES - part.shape[0], D), F32)], axis=0)
         start = pl.multiple_of(head * D + p * LANES, LANES)
         wqkv_ref[pl.ds(start, LANES), :] = part.astype(BF16)
-    greet()
+    greeting()
     gq_w[0]()
+    load_og.start()
     width = qvb_ref.shape[1]
     sown_ref[...] = jnp.zeros_like(sown_ref)
     sown_ref[0:1, :width] = qvb_ref[0:1, :]
@@ -691,6 +691,8 @@
     for copy in small:
         copy.start()
     width = praw_ref.shape[0]
+    for i in (3, 6, 9):
+        keeps[i].wait()
     tall = jnp.concatenate([praw_ref[...], jnp.zeros((LANES - width, D), F32)])
     wproj_ref[pl.ds(pl.multiple_of(head * LANES, LANES), LANES), :] = tall.astype(BF16)
     shard = pl.ds(pl.multiple_of(head * D, LANES), D)
@@ -733,13 +735,16 @@
     others[0][3]()
     others[1][3]()
     load_og.wait()
+    for i in range(24):
+        if i % 3 or i >= 12:
+            keeps[i].start()
     lax.fori_loop(0, span(4) // 2, widen, 0)
     others[2][2]()
     lax.fori_loop(span(4) // 2, clips // 2, widen, 0)
     others[2][3]()
     one = reduce_stages(buf_1, core_1, cell_1, up_1, head_1, one_ref, rsems.at[0])
     two = reduce_stages(buf_2, core_2, cell_2, up_2, head_2, two_ref, rsems.at[1])
-    late = reduce_stages(lbuf, core_l, cell_l, up_l, head_l, late_ref, rsems.at[2])
+    late = reduce_stages(lbuf, core_2, cell_2, up_2, head_l, late_ref, rsems.at[2])
     early_small = small_stages(esbuf, core_es, cell_es, up_es, head_es, esmall_ref, rsems.at[3])
     late_small = small_stages(lsbuf, core_ls, cell_ls, up_ls, head_ls, lsmall_ref, rsems.at[4])
     wide_grads(buf_2, og_ref, hid_ref)
@@ -812,15 +817,10 @@
     for copy in sends:
         copy.wait()
     total = (nslots[0] + nslots[1]) + (nslots[2] + nslots[3])
+    for i in range(24):
+        if i % 3 or i >= 12:
+            keeps[i].wait()
     norm_ref[...] = jnp.sqrt(total + jnp.sum(common, keepdims=True))
-
-    def finish(c, carry):
-        rows = clip_rows(c, PAIR)
-        send_out(c).wait()
-        pltpu.make_async_copy(dmid_ref.at[rows, :], din_hbm.at[rows, :], osems.at[1, c]).wait()
-        return carry
-
-    lax.fori_loop(0, clips // 2, finish, 0)
 
 
 def fold_table(tacc_ref, lsbuf):
@@ -849,7 +849,7 @@
                 ]
 
 
-def block(frames, tok, og, qraw, praw, araw, braw, qvb, table, fc1b, rowp):
+def block(frames, tok, og, held, qvb, table, fc1b, rowp):
     rows = tok.shape[0]
     clips = rows // CLIP
     upper = max(lax.axis_size("win") // 8, 1).bit_length() - 1
@@ -860,26 +860,26 @@
     inside = lambda: spec(memory_space=vmem)
     outside = lambda: spec(memory_space=pl.ANY)
     half, part = D // 2, D // 8
+    praw = held[3]
     return pl.pallas_call(
         partial(block_kernel, clips),
-        in_specs=[spec(memory_space=pltpu.SMEM), outside(), outside()] + [inside()] * 8,
-        out_specs=[outside(), outside()] + [inside()] * 6,
+        in_specs=[spec(memory_space=pltpu.SMEM)] + [outside()] * 26 + [inside()] * 4,
+        out_specs=[inside()] * 32,
         out_shape=[
-            shape((rows, D), F32),
-            shape((rows, D), F32),
-            shape((D, D), BF16),
-            shape((D, D), BF16),
-            shape((D, D), BF16),
-            shape((8, D), F32),
-            shape((8, D), F32),
-            shape((8, LANES), F32),
-        ],
+            vmem((rows, D), F32),
+            vmem((rows, D), F32),
+            vmem((D, D), BF16),
+            vmem((D, D), BF16),
+            vmem((D, D), BF16),
+            vmem((8, D), F32),
+            vmem((8, D), F32),
+            vmem((8, LANES), F32),
+        ]
+        + [vmem(a.shape, F32) for a in held],
         scratch_shapes=[
             vmem((8, D), F32),
             vmem((rows, D), BF16),
             vmem((rows, D), BF16),
-            vmem((rows, D), F32),
-            vmem((rows, D), F32),
             vmem((D + 16, rows), BF16),
             vmem((rows, D), BF16),
             vmem((rows, 1536), BF16),
@@ -901,20 +901,17 @@
             vmem((GROUPS, SPOT, PER * SPOT), F32),
             vmem((D, 1536), BF16),
             vmem((D, 1536), BF16),
-            vmem((D, 1536), BF16),
+            vmem((praw.shape[0], 1536), BF16),
             vmem((8, 1536), F32),
             vmem((8, 1536), F32),
-            vmem((half, 1536), BF16),
             vmem((half, 1536), BF16),
             vmem((half, 1536), BF16),
             vmem((8, 1536), F32),
             vmem((8, 1536), F32),
             vmem((3, part, 1536), BF16),
             vmem((3, part, 1536), BF16),
-            vmem((3, part, 1536), BF16),
             vmem((4, 8, 1536), F32),
             vmem((4, 8, 1536), F32),
-            vmem((upper + 1, part, 1536), BF16),
             vmem((upper + 1, part, 1536), BF16),
             vmem((upper + 1, part, 1536), BF16),
             vmem((upper + 1, 8, 1536), F32),
@@ -929,12 +926,12 @@
             sems((3, 3)),
             sems((5, 2, 14 + upper)),
             sems((2, 3)),
-            sems((3, max(clips, 2))),
+            sems((1, 26)),
         ],
         compiler_params=pltpu.CompilerParams(
             vmem_limit_bytes=VMEM_LIMIT, collective_id=0, has_side_effects=True
         ),
-    )(frames, tok, og, qraw, praw, araw, braw, qvb, table, fc1b, rowp)
+    )(frames, tok, og, *held, qvb, table, fc1b, rowp)
 
 
 def adam_step(weight, gradient, moment, second, factor, rate):
@@ -950,50 +947,50 @@
 
 
 def step_kernel(cuts, *refs):
-    norm_ref, e1_ref, e2_ref, ep_ref, late_ref, es_ref, ls_ref, one_hbm, two_hbm = refs[:9]
-    weights, firsts, seconds = refs[9:17], refs[17:25], refs[25:33]
-    gn_ref, one_out, two_out, outs, sems = refs[33], refs[34], refs[35], refs[36:68], refs[68]
-    bounce = refs[69:71]
-    pulls = [
-        pltpu.make_async_copy(one_hbm, bounce[0], sems.at[0]),
-        pltpu.make_async_copy(two_hbm, bounce[1], sems.at[1]),
+    norm_ref, g1_ref, g2_ref, late_ref, es_ref, ls_ref, one_ref, two_ref = refs[:8]
+    large, little = refs[8:20], refs[20:32]
+    gn_ref, one_out, two_out, outs, sems = refs[32], refs[33], refs[34], refs[35:67], refs[67]
+    step = pl.program_id(0)
+    pushes = [
+        pltpu.make_async_copy(one_ref, one_out, sems.at[0]),
+        pltpu.make_async_copy(two_ref, two_out, sems.at[1]),
     ]
-    pushes = [
-        pltpu.make_async_copy(bounce[0], one_out, sems.at[2]),
-        pltpu.make_async_copy(bounce[1], two_out, sems.at[3]),
-    ]
-
-    @pl.when(pl.program_id(0) == 0)
+
+    @pl.when(step == 0)
     def _():
-        for pull in pulls:
-            pull.start()
-
-    @pl.when(pl.program_id(0) == 1)
-    def _():
-        for pull, push in zip(pulls, pushes):
-            pull.wait()
+        for push in pushes:
             push.start()
 
     norm = norm_ref[0:1, 0:1]
     factor = jnp.minimum(1.0, CLIP_LIMIT / (norm + 1e-06))
 
-    def put(i, gradient, rate, at=(slice(None), slice(None))):
-        given = [ref[i][at].reshape(gradient.shape) for ref in (weights, firsts, seconds)]
+    def put(i, gradient, rate, given):
+        given = [value.reshape(gradient.shape) for value in given]
         values = adam_step(given[0], gradient, given[1], given[2], factor, rate)
         for k in range(4):
-            outs[4 * i + k][at] = values[k].reshape(outs[4 * i + k][at].shape)
-
-    width = weights[0].shape[1]
-    put(0, late_ref[...].astype(F32), LEARN_RATE, (0, slice(None), slice(None)))
-    put(3, ep_ref[...].astype(F32), LEARN_RATE)
-    put(4, e1_ref[...].astype(F32), LEARN_RATE)
-    put(6, e2_ref[...].astype(F32).T, LEARN_RATE)
-
-    @pl.when(pl.program_id(0) == 0)
+            out = outs[4 * i + k]
+            out[...] = values[k].reshape(out.shape)
+
+    def some(k, count):
+        rows = pl.ds(pl.multiple_of(step * count, count), count)
+        return [large[3 * k + n][rows, :] for n in range(3)]
+
+    width = large[0].shape[1]
+    rows, tall = D // cuts, width // cuts
+    late = late_ref[pl.ds(pl.multiple_of(step * width, width), width), :].astype(F32)
+    put(0, late, LEARN_RATE, [large[n][step] for n in range(3)])
+    late = late_ref[pl.ds(pl.multiple_of(cuts * width + step * tall, tall), tall), :].astype(F32)
+    put(3, late, LEARN_RATE, some(1, tall))
+    own = pl.ds(pl.multiple_of(step * rows, rows), rows)
+    put(4, g1_ref[own, :].astype(F32), LEARN_RATE, some(2, rows))
+    put(6, g2_ref[:, own].astype(F32).T, LEARN_RATE, some(3, rows))
+
+    @pl.when(step == 0)
     def _():
         gn_ref[...] = norm
+        whole = lambda k: [little[3 * k + n][...] for n in range(3)]
         both = jnp.concatenate([ls_ref[0:1, :width], ls_ref[0:1, 2 * LANES : 2 * LANES + width]])
-        put(1, both, LEARN_RATE)
+        put(1, both, LEARN_RATE, whole(0))
         lines = []
         for h in range(PER):
             pieces = []
@@ -1002,63 +999,49 @@
                 pieces.append(ls_ref[1 + at // D : 2 + at // D, at % D : at % D + LANES])
             lines.append(jnp.concatenate(pieces, axis=1))
         lines = jnp.concatenate(lines + [jnp.zeros((8 - PER, 256), F32)])
-        offsets = weights[2].shape[1]
+        offsets = little[3].shape[1]
         flip = iota((256, 256), 0) + iota((256, 256), 1) == offsets - 1
         flip = jnp.where(flip, 1.0, 0.0).astype(F32).astype(BF16)
         table = None
         for part in split_three(lines):
             term = nn(part, flip)
             table = term if table is None else table + term
-        put(2, table[:PER, :offsets], ROW_RATE)
-        put(5, es_ref[0:1, :], LEARN_RATE, (slice(None),))
-        put(7, jnp.concatenate([ls_ref[4:6, :], es_ref[1:5, :]]), ROW_RATE)
-
-    @pl.when(pl.program_id(0) == cuts - 1)
+        put(2, table[:PER, :offsets], ROW_RATE, whole(1))
+        put(5, es_ref[0:1, :], LEARN_RATE, whole(2))
+        put(7, jnp.concatenate([ls_ref[4:6, :], es_ref[1:5, :]]), ROW_RATE, whole(3))
+
+    @pl.when(step == cuts - 1)
     def _():
         for push in pushes:
             push.wait()
 
 
-def take_step(norm, g1, g2, late, esmall, lsmall, one, two, weights, firsts, seconds):
+def take_step(held, results):
+    little = held[12:]
     cuts = 3
     spec = pl.BlockSpec
+    near = spec(memory_space=pltpu.VMEM)
     full = lambda a: spec(a.shape, lambda i: (0,) * a.ndim)
     third = lambda a: spec(
         (a.shape[0] // cuts,) + a.shape[1:], lambda i: (i,) + (0,) * (a.ndim - 1)
     )
-    each = [
-        third(a) if k in (0, 3, 4, 6) else full(a) for k, a in enumerate(weights)
-    ]
-    rows = D // cuts
-    tall = weights[3].shape[0] // cuts
+    order = [(third, held[0]), (full, little[0]), (full, little[3]), (third, held[3])]
+    order += [(third, held[6]), (full, little[6]), (third, held[9]), (full, little[9])]
+    one, two = results[6:]
     shape = jax.ShapeDtypeStruct
+    close = [pltpu.with_memory_space_constraint(v, pltpu.VMEM) for v in (*results, *held)]
     outs = pl.pallas_call(
         partial(step_kernel, cuts),
         grid=(cuts,),
-        in_specs=[
-            full(norm),
-            spec((rows, D), lambda i: (i, 0)),
-            spec((D, rows), lambda i: (0, i)),
-            spec((tall, D), lambda i: (cuts * (cuts * tall) // tall + i, 0)),
-            spec((cuts * tall, D), lambda i: (i, 0)),
-            full(esmall),
-            full(lsmall),
-            spec(memory_space=pl.ANY),
-            spec(memory_space=pl.ANY),
-        ]
-        + each * 3,
+        in_specs=[near] * 32,
         out_specs=[spec((1, 1), lambda i: (0, 0))]
         + [spec(memory_space=pl.ANY)] * 2
-        + [e for e in each for _ in range(4)],
+        + [kind(a) for kind, a in order for _ in range(4)],
         out_shape=[shape((1, 1), F32), shape(one.shape, F32), shape(two.shape, F32)]
-        + [shape(a.shape, F32) for a in weights for _ in range(4)],
-        scratch_shapes=[
-            pltpu.SemaphoreType.DMA((4,)),
-            pltpu.VMEM(one.shape, F32),
-            pltpu.VMEM(two.shape, F32),
-        ],
-        compiler_params=pltpu.CompilerParams(vmem_limit_bytes=VMEM_LIMIT),
-    )(norm, g1, g2, late, late, esmall, lsmall, one, two, *weights, *firsts, *seconds)
+        + [shape(a.shape, F32) for _, a in order for _ in range(4)],
+        scratch_shapes=[pltpu.SemaphoreType.DMA((2,))],
+        compiler_params=pltpu.CompilerParams(vmem_limit_bytes=TAIL_LIMIT),
+    )(*close)
     return outs[0], outs[1], outs[2], outs[3:]
 
 
@@ -1092,52 +1075,16 @@
     rows_second,
 ):
     parts = lambda v: v.transpose(1, 2, 0)
-    weights = (
-        parts(qkv_weight),
-        qv_bias,
-        rel_table.T,
-        proj_weight,
-        fc1_weight,
-        fc1_bias,
-        fc2_weight,
-        row_params,
+    large = [parts(qkv_weight), parts(qkv_first), parts(qkv_second)]
+    large += [proj_weight, proj_first, proj_second, fc1_weight, fc1_first, fc1_second]
+    large += [fc2_weight, fc2_first, fc2_second]
+    little = [qv_bias, qvb_first, qvb_second, rel_table.T, table_first.T, table_second.T]
+    little += [fc1_bias, fc1b_first, fc1b_second, row_params, rows_first, rows_second]
+    output, input_grad, g1, g2, late, esmall, lsmall, norm, *kept = block(
+        clip_frames, tokens, out_grad, large + little, qv_bias, little[3], fc1_bias, row_params
     )
-    firsts = (
-        parts(qkv_first),
-        qvb_first,
-        table_first.T,
-        proj_first,
-        fc1_first,
-        fc1b_first,
-        fc2_first,
-        rows_first,
-    )
-    seconds = (
-        parts(qkv_second),
-        qvb_second,
-        table_second.T,
-        proj_second,
-        fc1_second,
-        fc1b_second,
-        fc2_second,
-        rows_second,
-    )
-    output, input_grad, g1, g2, late, esmall, lsmall, norm = block(
-        clip_frames,
-        tokens,
-        out_grad,
-        weights[0],
-        proj_weight,
-        fc1_weight,
-        fc2_weight,
-        qv_bias,
-        weights[2],
-        fc1_bias,
-        row_params,
-    )
-    grad_norm, output, input_grad, updated = take_step(
-        norm, g1, g2, late, esmall, lsmall, output, input_grad, weights, firsts, seconds
-    )
+    results = (norm, g1, g2, late, esmall, lsmall, output, input_grad)
+    grad_norm, output, input_grad, updated = take_step(kept, results)
     updated = [
         v.transpose(2, 0, 1) if k < 4 else v.T if 8 <= k < 12 else v for k, v in enumerate(updated)
     ]

time: 116 us -> 111 us (0.957)
  Pallas kernels: 115 us -> 110 us
    pallas_call x1, Pallas kernels: 10.2 us -> 6.02 us  [take_step(): pl.pallas_call(partial(step_kernel, cuts), grid=(cuts,), in_specs=[near]...]
    pallas_call x1, Pallas kernels: 105 us -> 104 us  [block(): pl.pallas_call(partial(block_kernel, clips), in_specs=[spec(memory_space=...]
where the time goes in v7:
time: 111 us
  Pallas kernels  110 us (99%)
    pallas_call x1, Pallas kernels, block(): pl.pallas_call(partial(block_kernel, clips), in_specs=[spec(memory_space=...  104 us
    pallas_call x1, Pallas kernels, take_step(): pl.pallas_call(partial(step_kernel, cuts), grid=(cuts,), in_specs=[near]...  6.02 us

profile of v7, /device:TPU:0, one launch (start us, length us, event | category | flops | bytes accessed | tf_op | source)
XLA Modules:
  0.0 110.5 jit_solution(3555052055748455900)
XLA Ops:
  0.7 103.6 %shard_map.530 = (f32[2048,384]{1,0:T(8,128)S(1)}, f32[2048,384]{1,0:T(8,128)S(1)}, bf16[384,384]{1,0:T(8,128)(2,1)S(1)}, bf16[384,384]{1,0:T(8,128)(2,1)S(1)}, ...) custom-call(s32[32]{0:T(128)} %refs_0_.1, ...), custom_call_target="tpu_custom_call" | custom-call | tf_op jit(solution)/shard_map/pallas_call | solution.py:864
  104.3 6.0 %shard_map.531 = (f32[1,1]{1,0:T(1,128)}, f32[2048,384]{1,0:T(8,128)}, f32[2048,384]{1,0:T(8,128)}, f32[3,96,384]{2,1,0:T(8,128)}, f32[3,96,384]{2,1,0:T(8,128)}...) custom-call(f32[8,128]{1,0:T(8,128)S(1)} %get-tuple-element.102.refs, ...), custom_call_target="tpu_custom_call" | custom-call | tf_op jit(solution)/shard_map/pallas_call | solution.py:1033
